TPU v7x, 32 devices: a whole 2x2x4 slice. The times are simulated.
32 devices in a mesh: seq: 8 (over y, x, core), head: 4 (over z).
Axes of the slice: x: 2, y: 2, z: 4, core: 2. Of those that a mesh axis runs over, the one named last changes fastest.
Arguments:
- inputs: bfloat16 [4096, 4096], P('seq', 'head'), may hold values from -6 to 6
- grad_out: bfloat16 [4096, 4096], P('seq', 'head'), may hold values from -6 to 6
- write_proj: bfloat16 [4096, 128], P('seq'), may hold values from -0.1875 to 0.1875
- read_proj: bfloat16 [4096, 128], P('seq'), may hold values from -0.1875 to 0.1875
- log_decay: float32 [64, 4096], P('head', 'seq'), may hold values from -0.6 to 0
Outputs:
- grad_inputs: bfloat16 [4096, 4096], P('seq', 'head')
- grad_write: float32 [4096, 128], P('seq')
- grad_read: float32 [4096, 128], P('seq')
- grad_decay: float32 [64, 4096], P('head', 'seq')
All inputs are finite; a program needn't handle non-finite values.
Results may differ from a plain program's by a relative error of at most 0.03.
Values sent between devices are 32-bit elements; how exact they have to be, the bound alone decides.
No kernel may reach another device: no remote copies, remote signals or barrier semaphores. Data moves between devices by JAX's collectives and lax.ppermute only.
A program may use at most 192 MiB of HBM per device.

v0:
```python
import jax
import jax.numpy as jnp
from jax import lax
from jax.sharding import PartitionSpec as P

Q = 256


def carried_in(part, axis, combine, identity, reverse):
    count = lax.axis_size(axis)
    place = lax.axis_index(axis)
    ahead = count - 1 - place if reverse else place
    gathered = jax.tree.map(lambda a: lax.all_gather(a, axis), part)
    state = jax.tree.map(lambda a, e: jnp.zeros_like(a) + jnp.asarray(e, a.dtype), part, identity)

    def one(hop, state):
        source = count - 1 - hop if reverse else hop
        return combine(
            state, jax.tree.map(lambda a: lax.dynamic_index_in_dim(a, source, 0, False), gathered)
        )

    return lax.fori_loop(0, ahead, one, state)


def split_dot(form, data, state):
    high = state.astype(jnp.bfloat16)
    low = (state - high.astype(jnp.float32)).astype(jnp.bfloat16)
    first = jnp.einsum(form, data, high, preferred_element_type=jnp.float32)
    return first + jnp.einsum(form, data, low, preferred_element_type=jnp.float32)


def span_local(blocks):
    inputs_blk, grads_blk, write_blk, read_blk, decay_blk = blocks
    running = jnp.cumsum(decay_blk, axis=1)
    totals = running[:, -1]
    length = decay_blk.shape[1]
    causal = jnp.tril(jnp.ones((length, length), jnp.bool_))
    gap_matrix = jnp.where(causal[None], running[:, :, None] - running[:, None, :], -jnp.inf)
    decay_mat = jnp.exp(gap_matrix)
    scores = jnp.dot(read_blk, write_blk.T, preferred_element_type=jnp.float32)
    weights = (scores[None] * decay_mat).astype(jnp.bfloat16)
    out_intra = jnp.einsum("hts,shp->thp", weights, inputs_blk, preferred_element_type=jnp.float32)
    grad_intra = jnp.einsum("hts,thp->shp", weights, grads_blk, preferred_element_type=jnp.float32)
    grad_pairs = jnp.einsum(
        "thp,shp->hts", grads_blk, inputs_blk, preferred_element_type=jnp.float32
    )
    grad_scores = jnp.sum(decay_mat * grad_pairs, axis=0)
    decay_in = jnp.exp(running).T[:, :, None]
    decay_out = jnp.exp(totals[:, None] - running).T[:, :, None]
    input_weighted = (inputs_blk.astype(jnp.float32) * decay_out).astype(jnp.bfloat16)
    grad_weighted = (grads_blk.astype(jnp.float32) * decay_in).astype(jnp.bfloat16)
    state_part = jnp.einsum(
        "qhp,qn->hpn", input_weighted, write_blk, preferred_element_type=jnp.float32
    )
    grad_part = jnp.einsum(
        "qhp,qn->hpn", grad_weighted, read_blk, preferred_element_type=jnp.float32
    )
    write_intra = split_dot("tn,ts->sn", read_blk, grad_scores)
    read_intra = split_dot("sn,ts->tn", write_blk, grad_scores)
    return (
        totals,
        decay_in,
        decay_out,
        out_intra,
        grad_intra,
        input_weighted,
        grad_weighted,
        state_part,
        grad_part,
        write_intra,
        read_intra,
    )


def combine(earlier, later):
    return (earlier[0] * later[0], later[1] + later[0][:, None, None] * earlier[1])


def add_pair(earlier, later):
    return earlier + later


def local(inputs, grad_out, write_proj, read_proj, log_decay):
    head_count = log_decay.shape[0]
    row_count = log_decay.shape[1]
    head_size = inputs.shape[1] // head_count
    state_width = write_proj.shape[1]
    span_count = row_count // Q
    inputs_c = inputs.reshape(span_count, Q, head_count, head_size)
    grads_c = grad_out.reshape(span_count, Q, head_count, head_size)
    write_c = write_proj.reshape(span_count, Q, state_width)
    read_c = read_proj.reshape(span_count, Q, state_width)
    decay_c = log_decay.reshape(head_count, span_count, Q).transpose(1, 0, 2)
    (
        totals,
        decay_in,
        decay_out,
        out_intra,
        grad_intra,
        input_weighted,
        grad_weighted,
        state_part,
        grad_part,
        write_intra,
        read_intra,
    ) = lax.map(span_local, (inputs_c, grads_c, write_c, read_c, decay_c))
    write_local = write_intra.reshape(row_count, state_width)
    read_local = read_intra.reshape(row_count, state_width)
    summed = jnp.cumsum(totals, axis=0)
    device_total = summed[-1]
    before_span = jnp.exp(summed - totals)
    after_span = jnp.exp(device_total[None] - summed)

    def forward_step(state_now, blocks):
        span_total, part_now = blocks
        return (jnp.exp(span_total)[:, None, None] * state_now + part_now, state_now)

    def backward_step(grad_now, blocks):
        span_total, part_now = blocks
        return (part_now + jnp.exp(span_total)[:, None, None] * grad_now, grad_now)

    zero_state = jnp.zeros((head_count, head_size, state_width), jnp.float32)
    state_end, state_local = lax.scan(forward_step, zero_state, (totals, state_part))
    grad_start, grad_local = lax.scan(backward_step, zero_state, (totals, grad_part), reverse=True)
    decay_scale = (head_size * row_count * lax.axis_size("seq")) ** (-0.5)
    groups = 1
    group_size = head_count // groups
    device_decay = jnp.exp(device_total)
    identity = (jnp.ones_like(device_decay), jnp.zeros_like(state_end))
    carried = carried_in((device_decay, state_end), "seq", combine, identity, False)[1]
    grad_right = carried_in((device_decay, grad_start), "seq", combine, identity, True)[1]
    state_in = state_local + before_span[:, 0:group_size, None, None] * carried[None]
    grad_end = grad_local + after_span[:, 0:group_size, None, None] * grad_right[None]
    out_inter = split_dot("ktn,khpn->kthp", read_c, state_in) * decay_in
    out_full = out_intra + out_inter
    output_dot = jnp.sum(grads_c.astype(jnp.float32) * out_full, axis=3)
    read_inter = split_dot("kthp,khpn->ktn", grad_weighted, state_in)
    grad_inter = split_dot("ksn,khpn->kshp", write_c, grad_end) * decay_out
    grad_full = grad_intra + grad_inter
    input_dot = jnp.sum(inputs_c.astype(jnp.float32) * grad_full, axis=3)
    write_inter = split_dot("kshp,khpn->ksn", input_weighted, grad_end)
    change = (output_dot - input_dot).reshape(row_count, group_size)
    suffix = jnp.cumsum(change[::-1], axis=0)[::-1]
    offset = carried_in(
        jnp.sum(change, axis=0), "seq", add_pair, jnp.zeros((group_size,), jnp.float32), True
    )
    decay_pieces = ((suffix + offset[None]) * decay_scale).T
    grad_inputs = grad_full.reshape(row_count, head_count * head_size).astype(jnp.bfloat16)
    write_late = write_inter.reshape(row_count, state_width)
    read_late = read_inter.reshape(row_count, state_width)
    grad_write, grad_read = lax.psum((write_local + write_late, read_local + read_late), "head")
    return (grad_inputs, grad_write, grad_read, decay_pieces)


def solution(mesh):
    in_specs = (
        P("seq", "head"),
        P("seq", "head"),
        P("seq", None),
        P("seq", None),
        P("head", "seq"),
    )
    out_specs = (P("seq", "head"), P("seq", None), P("seq", None), P("head", "seq"))
    return jax.shard_map(local, mesh=mesh, in_specs=in_specs, out_specs=out_specs, check_vma=False)
```

profile of v0, /device:TPU:0, one launch (start us, length us, event | category | flops | bytes accessed | tf_op | source)
XLA Modules:
  0.0 215.8 jit_solution(10515103041631133143)
XLA Ops:
  7.3 4.0 %reshape.164 = bf16[2,256,16,64]{3,2,1,0:T(8,128)(2,1)} reshape(bf16[512,1024]{1,0:T(8,128)(2,1)} %param.17) | data formatting | bytes 2097152 | tf_op jit(solution)/shard_map/reshape | solution.py:89
  11.3 2.9 %copy.59 = bf16[2,256,16,64]{1,3,2,0:T(8,128)(2,1)S(1)} copy(bf16[2,256,16,64]{3,2,1,0:T(8,128)(2,1)} %reshape.164) | data formatting | bytes 2097152 | tf_op jit(solution)/shard_map/while | solution.py:106
  14.2 2.3 %reshape.165 = bf16[2,256,16,64]{3,2,1,0:T(8,128)(2,1)} reshape(bf16[512,1024]{1,0:T(8,128)(2,1)S(1)} %copy-done.20) | data formatting | bytes 2097152 | tf_op jit(solution)/shard_map/reshape | solution.py:90
  16.6 2.8 %copy.60 = bf16[2,256,16,64]{1,3,2,0:T(8,128)(2,1)S(1)} copy(bf16[2,256,16,64]{3,2,1,0:T(8,128)(2,1)} %reshape.165) | data formatting | bytes 2097152 | tf_op jit(solution)/shard_map/while | solution.py:106
  21.7 21.4 %while.98 = (s32[]{:T(128)}, f32[2,16]{1,0:T(2,128)S(1)}, f32[2,256,16,1]{1,2,3,0:T(8,128)S(1)}, f32[2,256,16,1]{1,2,3,0:T(8,128)S(1)}, f32[2,256,16,64]{1,3,2,0...) while((s32[]{:T(128)}, f32[2,16]{1,0:T(2,128)S(1)}, ...), condition=%wide.region_4.5_spmd, body=%wide.region_0.4_spmd.sunk | while | flops 637747264 | bytes 54407928 | solution.py:106
  22.8 1.3 fusion.150
  29.9 1.5 multiply_reduce_fusion.3
  33.6 1.3 fusion.150
  40.5 1.5 multiply_reduce_fusion.3
  44.2 4.0 %while.102 = (s32[]{:T(128)}, f32[16,64,128]{2,1,0:T(8,128)S(1)}, f32[2,16,64,128]{3,2,1,0:T(8,128)}, f32[2,16,64,128]{3,2,1,0:T(8,128)}, f32[2,16]{1,0:T(2,128)S(1)}, /*index=5*/s32[]{:T(128)}, s32[]{:T(128)}) while((s32[]{:T(128)}, f32[16,64,128]{2,1,0:T(8,128)S(1)}, f32[2,16,64,128]{3,2,1,0:T(8,128)}, ...), condition=%wide.region_6.7_spmd.clone, body=%wide.region_5.6_spmd.clone.sunk | while | flops 524292 | bytes 2621744 | solution.py:124
  50.2 4.0 %while.103 = (s32[]{:T(128)}, f32[16,64,128]{2,1,0:T(8,128)S(1)}, f32[2,16,64,128]{3,2,1,0:T(8,128)}, f32[2,16]{1,0:T(2,128)S(1)}, f32[2,16,64,128]{3,2,1,0:T(8,128)}, /*index=5*/s32[]{:T(128)}, s32[]{:T(128)}) while((s32[]{:T(128)}, f32[16,64,128]{2,1,0:T(8,128)S(1)}, f32[2,16,64,128]{3,2,1,0:T(8,128)}, ...), condition=%wide.region_12.13_spmd.clone, body=%wide.region_11.12_spmd.clone.sunk | while | flops 524291 | bytes 2622240 | solution.py:123
  56.5 10.2 %all-gather.3 = f32[8,1,16]{2,1,0:T(1,128)S(1)} all-gather(f32[1,1,16]{2,1,0:T(1,128)S(1)} %get-tuple-element.652), channel_id=1, replica_groups=mesh['seq'=8,'head'=4] {'seq'}, dimensions={0}, use_global_device_ids=true | all-gather | bytes 576 | tf_op jit(solution)/shard_map/all_gather | solution.py:13
  66.7 22.0 %all-gather.7.cloned.1.call-done = f32[128,64,128]{2,1,0:T(8,128)} async-done(((f32[16,64,128]{2,1,0:T(8,128)}), f32[128,64,128]{2,1,0:T(8,128)}) %all-gather.7.cloned.1.call-update) | async-done | bytes 4194320 | tf_op jit(solution)/shard_map/all_gather | solution.py:13
  88.7 8.7 %while.99 = (s32[]{:T(128)}, f32[16,64,128]{2,1,0:T(8,128)S(1)}, s32[]{:T(128)}, f32[8,16,64,128]{3,2,1,0:T(8,128)}, f32[8,16]{1,0:T(8,128)S(1)}, /*index=5*/s32[]{:T(128)}, s32[]{:T(128)}, s32[]{:T(128)}, s32[]{:T(128)}) while((s32[]{:T(128)}, f32[16,64,128]{2,1,0:T(8,128)S(1)}, s32[]{:T(128)}, f32[8,16,64,128]{3,2,1,0:T(8,128)}, ...), condition=%wide.region_9.10_spmd, body=%wide.region_8.9_spmd.sunk | while | flops 262150 | bytes 1573203 | solution.py:22
  88.8 1.2 bitcast_add_fusion.10
  90.0 1.2 bitcast_add_fusion.10
  93.7 1.2 bitcast_add_fusion.10
  96.2 1.2 bitcast_add_fusion.10
  97.4 29.9 %all-gather.9.cloned.1.call-done = f32[128,64,128]{2,1,0:T(8,128)} async-done(((f32[16,64,128]{2,1,0:T(8,128)}), f32[128,64,128]{2,1,0:T(8,128)}) %all-gather.9.cloned.1.call-update) | async-done | bytes 4194320 | tf_op jit(solution)/shard_map/all_gather | solution.py:13
  127.4 1.8 fusion.84
  130.2 1.5 copy-done.12
  133.2 1.7 multiply_reduce_fusion.1
  135.6 21.9 %all-reduce = f32[128]{0:T(128)S(1)} all-reduce(f32[128]{0:T(128)S(1)} %dynamic-update-slice), channel_id=4, replica_groups=mesh['seq'=8,'head'=4] {'seq'}, use_global_device_ids=true, to_apply=%add | all-reduce | flops 128 | bytes 1024
  158.0 2.5 %convolution_bitcast_fusion.2 = f32[2,256,128]{2,1,0:T(8,128)} fusion(bf16[2,256,16,64]{1,3,2,0:T(8,128)(2,1)} %get-tuple-element.427, bf16[2,16,64,128]{3,2,1,0:T(8,128)(2,1)S(1)} %copy-done.17), kind=kOutput, calls=%fused_computation.112 | convolution fusion | flops 134217728 | bytes 1835008 | tf_op jit(solution)/shard_map/kthp,khpn->ktn/dot_general | solution.py:29
  160.5 2.5 %convolution_bitcast_fusion.4 = f32[2,256,128]{2,1,0:T(8,128)} fusion(bf16[2,256,16,64]{1,3,2,0:T(8,128)(2,1)} %get-tuple-element.425, bf16[2,16,64,128]{3,2,1,0:T(8,128)(2,1)S(1)} %copy-done.19), kind=kOutput, calls=%fused_computation.114 | convolution fusion | flops 134217728 | bytes 1835008 | tf_op jit(solution)/shard_map/kshp,khpn->ksn/dot_general | solution.py:29
  164.1 2.8 %fusion.81 = f32[2,256,128]{2,1,0:T(8,128)} fusion(f32[2,256,128]{2,1,0:T(8,128)} %copy-done.22, f32[2,256,128]{2,1,0:T(8,128)} %convolution_bitcast_fusion.2, bf16[2,256,16,64]{1,3,2,0:T(8,128)(2,1)} %get-tuple-element.427, f32[2,16,64,128]{3,2,1,0:T(8,128)S(1)} %copy-done.7, f32[16,64,128]{2,1,0:T(8,128)S(1)} %get-tuple-element.431, ...), kind=kOutput, calls=%fused_computation.119 | convolution fusion | flops 135135232 | bytes 3408000 | tf_op jit(solution)/shard_map/kthp,khpn->ktn/dot_general | solution.py:28
  166.9 1.3 fusion.79
  168.8 3.0 %copy.74 = bf16[2,256,16,64]{3,2,1,0:T(8,128)(2,1)S(1)} copy(bf16[2,256,16,64]{1,3,2,0:T(8,128)(2,1)} %get-tuple-element.646) | data formatting | bytes 2097152
  171.8 2.3 %reshape.163 = bf16[512,1024]{1,0:T(8,128)(2,1)} reshape(bf16[2,256,16,64]{3,2,1,0:T(8,128)(2,1)S(1)} %copy.74) | data formatting | bytes 2097152
  174.8 31.2 %all-reduce.4.cloned.1.call-done = (f32[512,128]{1,0:T(8,128)}, f32[512,128]{1,0:T(8,128)}) async-done(((f32[512,128]{1,0:T(8,128)}, f32[512,128]{1,0:T(8,128)}), (f32[512,128]{1,0:T(8,128)}, f32[512,128]{1,0:T(8,128)})) %all-reduce.4.cloned.1.call-update) | async-done | bytes 524304 | tf_op jit(solution)/shard_map/psum | solution.py:151
  205.9 1.7 copy.196
  207.6 1.7 copy.197
  (186 shorter events, 40.4 us)
Async XLA Ops:
  7.2 81.5 %all-gather.7.cloned.1.call-start = ((), (), s32[]{:S(2)}) async-start(), calls=%async_computation | async-start | bytes 4718592 | tf_op jit(solution)/shard_map/all_gather | solution.py:13
  11.3 2.9 %copy-start.20 = (bf16[512,1024]{1,0:T(8,128)(2,1)S(1)}, bf16[512,1024]{1,0:T(8,128)(2,1)}, u32[]{:S(2)}) copy-start(bf16[512,1024]{1,0:T(8,128)(2,1)} %param.18) | copy-start | bytes 3145732
  16.6 2.8 %copy-start.26 = (f32[16,512]{1,0:T(8,128)S(1)}, f32[16,512]{1,0:T(8,128)}, u32[]{:S(2)}) copy-start(f32[16,512]{1,0:T(8,128)} %param.21) | copy-start | bytes 98308
  16.6 5.1 %copy-start.2 = (bf16[512,128]{1,0:T(8,128)(2,1)S(1)}, bf16[512,128]{1,0:T(8,128)(2,1)}, u32[]{:S(2)}) copy-start(bf16[512,128]{1,0:T(8,128)(2,1)} %param.20) | copy-start | bytes 393220
  16.6 5.1 %copy-start.3 = (bf16[512,128]{1,0:T(8,128)(2,1)S(1)}, bf16[512,128]{1,0:T(8,128)(2,1)}, u32[]{:S(2)}) copy-start(bf16[512,128]{1,0:T(8,128)(2,1)} %param.19) | copy-start | bytes 393220
  22.5 1.9 copy-start.10
  24.3 1.6 copy-start.13
  25.5 1.6 copy-start.11
  25.9 1.5 copy-start.8
  27.0 5.3 %copy-start.14 = (f32[2,256,16,64]{1,3,2,0:T(8,128)}, f32[2,256,16,64]{1,3,2,0:T(8,128)S(1)}, u32[]{:S(2)}) copy-start(f32[2,256,16,64]{1,3,2,0:T(8,128)S(1)} %fusion.149) | copy-start | bytes 6291460 | tf_op jit(solution)/shard_map/while
  33.2 1.9 copy-start.10
  35.1 1.6 copy-start.13
  36.2 1.6 copy-start.11
  36.6 1.5 copy-start.8
  37.7 5.2 %copy-start.14 = (f32[2,256,16,64]{1,3,2,0:T(8,128)}, f32[2,256,16,64]{1,3,2,0:T(8,128)S(1)}, u32[]{:S(2)}) copy-start(f32[2,256,16,64]{1,3,2,0:T(8,128)S(1)} %fusion.149) | copy-start | bytes 6291460 | tf_op jit(solution)/shard_map/while
  43.0 1.1 copy-start.22
  49.1 78.2 %all-gather.9.cloned.1.call-start = ((), (), s32[]{:S(2)}) async-start(), calls=%async_computation.1 | async-start | bytes 4718592 | tf_op jit(solution)/shard_map/all_gather | solution.py:13
  50.2 5.0 %copy-start.27 = (u32[32]{0:T(128)S(1)}, u32[32]{0:T(128)}, u32[]{:S(2)}) copy-start(u32[32]{0:T(128)} %constant.186) | copy-start | bytes 388
  55.1 150.8 %all-reduce.4.cloned.1.call-start = ((), (), s32[]{:S(2)}) async-start(), calls=%async_computation.2 | async-start | bytes 1048576 | tf_op jit(solution)/shard_map/psum | solution.py:151
  127.4 1.9 copy-start.4
  127.4 1.9 copy-start.6
  129.7 2.7 %copy-start.16 = (bf16[2,16,64,128]{3,2,1,0:T(8,128)(2,1)}, bf16[2,16,64,128]{3,2,1,0:T(8,128)(2,1)S(1)}, u32[]{:S(2)}) copy-start(bf16[2,16,64,128]{3,2,1,0:T(8,128)(2,1)S(1)} %get-tuple-element.654) | copy-start | bytes 1572868
  129.7 2.7 %copy-start.18 = (bf16[2,16,64,128]{3,2,1,0:T(8,128)(2,1)}, bf16[2,16,64,128]{3,2,1,0:T(8,128)(2,1)S(1)}, u32[]{:S(2)}) copy-start(bf16[2,16,64,128]{3,2,1,0:T(8,128)(2,1)S(1)} %get-tuple-element.655) | copy-start | bytes 1572868
  129.7 2.0 copy-start.12
  131.6 1.6 copy-start.15
  133.2 24.8 %copy-start.17 = (bf16[2,16,64,128]{3,2,1,0:T(8,128)(2,1)S(1)}, bf16[2,16,64,128]{3,2,1,0:T(8,128)(2,1)}, u32[]{:S(2)}) copy-start(bf16[2,16,64,128]{3,2,1,0:T(8,128)(2,1)} %copy-done.16) | copy-start | bytes 1572868
  135.0 25.5 %copy-start.19 = (bf16[2,16,64,128]{3,2,1,0:T(8,128)(2,1)S(1)}, bf16[2,16,64,128]{3,2,1,0:T(8,128)(2,1)}, u32[]{:S(2)}) copy-start(bf16[2,16,64,128]{3,2,1,0:T(8,128)(2,1)} %copy-done.18) | copy-start | bytes 1572868
  135.4 28.7 %copy-start.7 = (f32[2,16,64,128]{3,2,1,0:T(8,128)S(1)}, f32[2,16,64,128]{3,2,1,0:T(8,128)}, u32[]{:S(2)}) copy-start(f32[2,16,64,128]{3,2,1,0:T(8,128)} %get-tuple-element.429) | copy-start | bytes 3145732
  162.9 3.9 %copy-start.5 = (f32[2,16,64,128]{3,2,1,0:T(8,128)S(1)}, f32[2,16,64,128]{3,2,1,0:T(8,128)}, u32[]{:S(2)}) copy-start(f32[2,16,64,128]{3,2,1,0:T(8,128)} %get-tuple-element.420) | copy-start | bytes 3145732
  164.1 2.8 %copy-start.21 = (bf16[2,256,16,64]{1,3,2,0:T(8,128)(2,1)S(1)}, bf16[2,256,16,64]{1,3,2,0:T(8,128)(2,1)}, u32[]{:S(2)}) copy-start(bf16[2,256,16,64]{1,3,2,0:T(8,128)(2,1)} %get-tuple-element.425) | copy-start | bytes 3145732
  164.1 2.8 %copy-start.24 = (f32[2,256,128]{2,1,0:T(8,128)S(1)}, f32[2,256,128]{2,1,0:T(8,128)}, u32[]{:S(2)}) copy-start(f32[2,256,128]{2,1,0:T(8,128)} %copy-done.23) | copy-start | bytes 786436
  164.1 2.8 %copy-start.25 = (f32[2,256,128]{2,1,0:T(8,128)S(1)}, f32[2,256,128]{2,1,0:T(8,128)}, u32[]{:S(2)}) copy-start(f32[2,256,128]{2,1,0:T(8,128)} %convolution_bitcast_fusion.4) | copy-start | bytes 786436
  (5 other events, 4.7 us)
Sparse Core Ops, SparseCore 0:
  49.2 39.4 all-gather.6
  90.6 36.7 all-gather.8
  168.3 37.5 all-reduce.3
where the time goes:
time: 217 us; the launch traced here: 216 us
  waiting for transfers between devices  83.1 us (38%)
  local copies, waits for them, and re-layouts  35.5 us (16%)
  blocking collectives  32.1 us (15%)
  matrix products  26 us (12%)
  other arithmetic  23.3 us (11%)
  between operations  14.8 us (7%)
    all_gather x2, waiting for transfers between devices, carried_in(): gathered = jax.tree.map(lambda a: lax.all_gather(a, axis), part)  51.9 us
    psum x1, waiting for transfers between devices, local(): lax.psum((write_local + write_late, read_local + read_late), 'head')  31.2 us
    unnamed x1, blocking collectives  21.9 us
    unnamed x51, local copies, waits for them, and re-layouts  13.5 us
    all_gather x1, blocking collectives, carried_in(): gathered = jax.tree.map(lambda a: lax.all_gather(a, axis), part)  10.2 us
    add x7, other arithmetic, combine(): later[1] + later[0][:, None, None] * earlier[1]  8.34 us
    dot_general x8, matrix products, split_dot(): jnp.einsum(form, data, low, preferred_element_type=jnp.float32)  8.17 us
    dot_general x8, matrix products, split_dot(): first = jnp.einsum(form, data, high, preferred_element_type=jnp.float32)  7.22 us
  transfers between devices with their start and end apart: 3, of which 3 were waited for; matrix products, arithmetic and copies ran while one was open for 10% of the time, Pallas kernels for 0%

commit v1 on v0

v1 whole, which is shorter than its diff:
```python
import jax
import jax.numpy as jnp
from jax import lax
from jax.experimental import pallas as pl
from jax.experimental.pallas import tpu as pltpu
from jax.sharding import PartitionSpec as P

Q = 256
GROUP = 8
F32 = jnp.float32
BF16 = jnp.bfloat16
VMEM_LIMIT = 48 * 1024 * 1024


def dot(a, b):
    return jnp.dot(a, b, preferred_element_type=F32)


def dot_t(a, b):
    return lax.dot_general(a, b, (((1,), (1,)), ((), ())), preferred_element_type=F32)


def iota(shape, dim):
    return lax.broadcasted_iota(jnp.int32, shape, dim)


def split_two(values):
    high = values.astype(BF16).astype(F32)
    return high, values - high


def split_three(values):
    high, rest = split_two(values)
    mid, low = split_two(rest)
    return high, mid, low


def times_ones(values, ones):
    high, mid, low = split_three(values)
    stacked = jnp.concatenate([high, mid, low, jnp.zeros_like(low)], axis=0).astype(BF16)
    out = dot(stacked, ones)
    return out[0:GROUP] + out[GROUP : 2 * GROUP] + out[2 * GROUP : 3 * GROUP]


def running_of(decay_blk):
    upto = (iota((Q, Q), 0) <= iota((Q, Q), 1)).astype(BF16)
    return times_ones(decay_blk, upto)


def spread_decays(running, head_size):
    lanes = GROUP * head_size
    total = running[:, Q - 1 : Q]
    parts = split_two(jnp.exp(running)) + split_two(jnp.exp(total - running))
    stacked = jnp.concatenate(parts, axis=0).T.astype(BF16)
    row = iota((4 * GROUP, lanes), 0)
    owner = row % GROUP == iota((4 * GROUP, lanes), 1) // head_size
    first = (owner & (row < 2 * GROUP)).astype(F32).astype(BF16)
    second = (owner & (row >= 2 * GROUP)).astype(F32).astype(BF16)
    return dot(stacked, first), dot(stacked, second)


def state_kernel(sel, x_ref, g_ref, w_ref, r_ref, ld_ref, pay_ref, iw_ref, gw_ref, part_ref, tot_ref):
    lanes = x_ref.shape[1]
    width = w_ref.shape[1]
    f_parts, g_parts, ends = [], [], []
    for b in range(2):
        rows = slice(b * Q, (b + 1) * Q)
        running = running_of(ld_ref[:, rows])
        decay_in, decay_out = spread_decays(running, lanes // GROUP)
        iw = (x_ref[rows, :].astype(F32) * decay_out).astype(BF16)
        gw = (g_ref[rows, :].astype(F32) * decay_in).astype(BF16)
        iw_ref[rows, :] = iw
        gw_ref[rows, :] = gw
        f_parts.append(dot(w_ref[rows, :].astype(F32).T.astype(BF16), iw))
        g_parts.append(dot(r_ref[rows, :].astype(F32).T.astype(BF16), gw))
        ends.append(decay_in[Q - 1 : Q, :])
    pay_ref[0:width, :] = ends[1] * f_parts[0] + f_parts[1]
    pay_ref[width : 2 * width, :] = ends[0] * g_parts[1] + g_parts[0]
    pay_ref[2 * width : 2 * width + 8, :] = jnp.broadcast_to(ends[0] * ends[1], (8, lanes))
    part_ref[0:width, :] = f_parts[0]
    part_ref[width : 2 * width, :] = g_parts[1]
    tot_ref[0:8, :] = jnp.broadcast_to(ends[0], (8, lanes))
    tot_ref[8:16, :] = jnp.broadcast_to(ends[1], (8, lanes))


def params():
    return pltpu.CompilerParams(vmem_limit_bytes=VMEM_LIMIT)


def states(which, inputs, grad_out, write_proj, read_proj, log_decay, head_size):
    rows, width = write_proj.shape
    lanes = GROUP * head_size
    wide = pl.BlockSpec((rows, lanes), lambda i, s: (0, s[0]))
    whole = lambda shape: pl.BlockSpec(shape, lambda i, s: (0, 0))
    outs = [
        ((2 * width + 8, lanes), F32),
        ((rows, lanes), BF16),
        ((rows, lanes), BF16),
        ((2 * width, lanes), F32),
        ((16, lanes), F32),
    ]
    return pl.pallas_call(
        state_kernel,
        grid_spec=pltpu.PrefetchScalarGridSpec(
            num_scalar_prefetch=1,
            grid=(1,),
            in_specs=[
                wide,
                wide,
                whole((rows, width)),
                whole((rows, width)),
                pl.BlockSpec((GROUP, rows), lambda i, s: (s[0], 0)),
            ],
            out_specs=[whole(s) for s, _ in outs],
        ),
        out_shape=[jax.ShapeDtypeStruct(s, t) for s, t in outs],
        compiler_params=params(),
        cost_estimate=pl.CostEstimate(flops=4 * rows * lanes * width, bytes_accessed=4 * rows * lanes * 2, transcendentals=0),
        name="states",
    )(which, inputs, grad_out, write_proj, read_proj, log_decay)


def chip_kernel(sel, mine_ref, got_ref, px_ref, py_ref):
    width = (mine_ref.shape[0] - 8) // 2
    lead = sel[0] == 0
    f_rows, b_rows, d_rows = slice(0, width), slice(width, 2 * width), slice(2 * width, 2 * width + 8)
    dec_mine, dec_got = mine_ref[d_rows, :], got_ref[d_rows, :]
    dec_first = jnp.where(lead, dec_mine, dec_got)[0:1]
    dec_second = jnp.where(lead, dec_got, dec_mine)[0:1]
    f_mine, f_got = mine_ref[f_rows, :], got_ref[f_rows, :]
    b_mine, b_got = mine_ref[b_rows, :], got_ref[b_rows, :]
    forward = dec_second * jnp.where(lead, f_mine, f_got) + jnp.where(lead, f_got, f_mine)
    backward = jnp.where(lead, b_mine, b_got) + dec_first * jnp.where(lead, b_got, b_mine)
    both = dec_mine * dec_got
    px_ref[f_rows, :] = jnp.where(sel[1] == 0, forward, backward)
    py_ref[f_rows, :] = jnp.where(sel[2] == 0, forward, backward)
    px_ref[width : width + 8, :] = both
    py_ref[width : width + 8, :] = both


def full(ref_or_shape):
    shape = ref_or_shape.shape
    return pl.BlockSpec(shape, lambda i, s: (0,) * len(shape))


def whole_call(kernel, name, sel, args, outs, flops=0):
    out_shape = [jax.ShapeDtypeStruct(s, t) for s, t in outs]
    moved = sum(a.size * a.dtype.itemsize for a in list(args) + out_shape)
    return pl.pallas_call(
        kernel,
        grid_spec=pltpu.PrefetchScalarGridSpec(
            num_scalar_prefetch=1,
            grid=(1,),
            in_specs=[full(a) for a in args],
            out_specs=[full(o) for o in out_shape],
        ),
        out_shape=out_shape,
        compiler_params=params(),
        cost_estimate=pl.CostEstimate(flops=flops, bytes_accessed=moved, transcendentals=0),
        name=name,
    )(sel, *args)


def carry_kernel(sel, rx_ref, ry_ref, rd_ref, mine_ref, got_ref, own_ref, other_ref):
    width = rx_ref.shape[0] - 8
    head, tail = slice(0, width), slice(width, width + 1)
    lead = sel[0] == 0
    low_x, low_y = sel[1] == 0, sel[2] == 0
    rx, ry, rd = rx_ref[head, :], ry_ref[head, :], rd_ref[head, :]
    dx, dy, dd = rx_ref[tail, :], ry_ref[tail, :], rd_ref[tail, :]
    far = jnp.where(low_x == low_y, rx + dx * (ry + dy * rd), rd + dd * ry)
    near = jnp.where(low_x == low_y, jnp.zeros_like(rx), rx)
    f_in = jnp.where(low_y, near, far)
    b_in = jnp.where(low_y, far, near)
    b_rows = slice(width, 2 * width)
    d_row = slice(2 * width, 2 * width + 1)
    f_next_mine = mine_ref[d_row, :] * f_in + mine_ref[head, :]
    b_next_mine = mine_ref[d_row, :] * b_in + mine_ref[b_rows, :]
    f_next_got = got_ref[d_row, :] * f_in + got_ref[head, :]
    b_next_got = got_ref[d_row, :] * b_in + got_ref[b_rows, :]
    own_ref[head, :] = jnp.where(lead, f_in, f_next_got)
    own_ref[b_rows, :] = jnp.where(lead, b_next_got, b_in)
    other_ref[head, :] = jnp.where(lead, f_next_mine, f_in)
    other_ref[b_rows, :] = jnp.where(lead, b_in, b_next_mine)


def block_states(car_ref, part_ref, tot_ref):
    width = car_ref.shape[0] // 2
    f_car, b_car = car_ref[0:width, :], car_ref[width : 2 * width, :]
    f_next = tot_ref[0:1, :] * f_car + part_ref[0:width, :]
    b_next = tot_ref[8:9, :] * b_car + part_ref[width : 2 * width, :]
    return (f_car, f_next), (b_next, b_car)


def late_kernel(sel, iw_ref, gw_ref, car_ref, part_ref, tot_ref, acc_ref, out_ref):
    rows = iw_ref.shape[0]
    state_in, grad_end = block_states(car_ref, part_ref, tot_ref)
    for b in range(2):
        at, late = slice(b * Q, (b + 1) * Q), slice(rows + b * Q, rows + (b + 1) * Q)
        out_ref[at, :] = acc_ref[at, :] + dot_t(gw_ref[at, :], state_in[b].astype(BF16))
        out_ref[late, :] = acc_ref[late, :] + dot_t(iw_ref[at, :], grad_end[b].astype(BF16))


def cut_kernel(sel, iw_ref, gw_ref, car_ref, part_ref, tot_ref, acc_ref, *rest):
    outs, total = rest[:-1], rest[-1]
    late_kernel(sel, iw_ref, gw_ref, car_ref, part_ref, tot_ref, acc_ref, total)
    rows = iw_ref.shape[0]
    step = rows // len(outs)
    for k, out in enumerate(outs):
        at = pl.multiple_of(jnp.bitwise_xor(sel[3], k) * step, step)
        out[0:step, :] = total[pl.ds(at, step), :]
        out[step : 2 * step, :] = total[pl.ds(rows + at, step), :]


def intra_kernel(x_ref, g_ref, w_ref, r_ref, ld_ref, gint_ref, dot_ref, acc_ref, gs_ref):
    group = pl.program_id(1)
    size = x_ref.shape[1] // GROUP
    half = Q // 2
    running = running_of(ld_ref[...])
    columns = jnp.concatenate([running] * (128 // GROUP), axis=0).T
    scores = dot_t(w_ref[...], r_ref[...])
    keep_top = iota((half, Q), 0) <= iota((half, Q), 1)
    keep_low = iota((half, half), 0) <= iota((half, half), 1)
    lane = iota((Q, 2 * size), 1)

    @pl.when(group == 0)
    def _():
        gs_ref[...] = jnp.zeros_like(gs_ref)

    sums_top, sums_low = [], []
    gs_top = jnp.zeros((half, Q), F32)
    gs_low = jnp.zeros((half, half), F32)
    for pair in range(GROUP // 2):
        at = slice(pair * 2 * size, (pair + 1) * 2 * size)
        x_pair, g_pair = x_ref[:, at], g_ref[:, at]
        top, low = None, None
        for k in range(2):
            h = 2 * pair + k
            mine = (lane < size) if k == 0 else (lane >= size)
            g_own = jnp.where(mine, g_pair, jnp.zeros_like(g_pair))
            row = running[h : h + 1, :]
            col = columns[:, h : h + 1]
            decay_top = jnp.exp(jnp.where(keep_top, row - col[0:half], -jnp.inf))
            decay_low = jnp.exp(jnp.where(keep_low, row[:, half:] - col[half:], -jnp.inf))
            pairs_top = dot_t(x_pair[0:half], g_own)
            pairs_low = dot_t(x_pair[half:], g_own[half:])
            weights_top = scores[0:half] * decay_top
            weights_low = scores[half:, half:] * decay_low
            sums_top.append(jnp.sum(weights_top * pairs_top, axis=0, keepdims=True))
            sums_low.append(jnp.sum(weights_low * pairs_low, axis=0, keepdims=True))
            gs_top = gs_top + decay_top * pairs_top
            gs_low = gs_low + decay_low * pairs_low
            part_top = dot(weights_top.astype(BF16), g_own)
            part_low = dot(weights_low.astype(BF16), g_own[half:])
            top = part_top if top is None else top + part_top
            low = part_low if low is None else low + part_low
        gint_ref[0:half, at] = top
        gint_ref[half:, at] = low
    gs_ref[0:half, :] += gs_top
    gs_ref[half:, half:] += gs_low
    dot_ref[...] = jnp.concatenate(sums_top, axis=0)
    dot_ref[:, half:] += jnp.concatenate(sums_low, axis=0)

    @pl.when(group == pl.num_programs(1) - 1)
    def _():
        grad_scores = gs_ref[...]
        acc_ref[0] = dot(grad_scores.T.astype(BF16), w_ref[...])
        acc_ref[1] = dot(grad_scores.astype(BF16), r_ref[...])


def intra(inputs, grad_out, write_proj, read_proj, log_decay, head_size):
    rows, width = write_proj.shape
    heads = log_decay.shape[0]
    lanes = GROUP * head_size
    spans, groups = rows // Q, heads // GROUP
    wide = pl.BlockSpec((Q, lanes), lambda b, j: (b, j))
    narrow = pl.BlockSpec((Q, width), lambda b, j: (b, 0))
    decays = pl.BlockSpec((GROUP, Q), lambda b, j: (j, b))
    return pl.pallas_call(
        intra_kernel,
        grid=(spans, groups),
        in_specs=[wide, wide, narrow, narrow, decays],
        out_specs=[wide, decays, pl.BlockSpec((2, Q, width), lambda b, j: (0, b, 0))],
        out_shape=[
            jax.ShapeDtypeStruct((rows, heads * head_size), F32),
            jax.ShapeDtypeStruct((heads, rows), F32),
            jax.ShapeDtypeStruct((2, rows, width), F32),
        ],
        scratch_shapes=[pltpu.VMEM((Q, Q), F32)],
        compiler_params=params(),
        cost_estimate=pl.CostEstimate(
            flops=16 * rows * Q * heads * head_size, bytes_accessed=8 * rows * heads * head_size, transcendentals=rows * Q * heads
        ),
        name="intra",
    )(inputs, grad_out, write_proj, read_proj, log_decay)


def grads_kernel(scale, count, sel, x_ref, g_ref, w_ref, r_ref, ld_ref, gint_ref, dot_ref, *rest):
    refs, (gi_ref, gd_ref) = rest[: 4 * count], rest[4 * count :]
    j = pl.program_id(0)
    lanes = x_ref.shape[1]
    width = w_ref.shape[1]
    size = lanes // GROUP

    def body(car_ref, part_ref, tot_ref, pay_ref):
        state_in, grad_end = block_states(car_ref, part_ref, tot_ref)
        last = pay_ref[2 * width : 2 * width + 1, :] * car_ref[0:width, :] + pay_ref[0:width, :]
        after = (state_in[1], last)
        owner = (iota((16, lanes), 0) == iota((16, lanes), 1) // size).astype(F32).astype(BF16)
        onward = (iota((Q, Q), 0) >= iota((Q, Q), 1)).astype(F32).astype(BF16)
        for b in range(2):
            at = slice(b * Q, (b + 1) * Q)
            running = running_of(ld_ref[:, at])
            decay_in, decay_out = spread_decays(running, size)
            g, x = g_ref[at, :].astype(F32), x_ref[at, :].astype(F32)
            out_inter = dot(r_ref[at, :], state_in[b].astype(BF16)) * decay_in
            grad_full = gint_ref[at, :] + dot(w_ref[at, :], grad_end[b].astype(BF16)) * decay_out
            gi_ref[at, :] = grad_full.astype(BF16)
            high, low = split_two(g * out_inter - x * grad_full)
            change = dot_t(owner, high.astype(BF16)) + dot_t(owner, low.astype(BF16))
            change = change[0:GROUP] + dot_ref[:, at]
            cross = jnp.sum(after[b] * grad_end[b], axis=0, keepdims=True)
            cross = jnp.broadcast_to(cross, (Q, lanes))
            c1, c2, c3 = split_three(cross)
            crossing = dot_t(owner, c1.astype(BF16)) + dot_t(owner, c2.astype(BF16)) + dot_t(owner, c3.astype(BF16))
            gd_ref[:, at] = (times_ones(change, onward) + crossing[0:GROUP]) * scale

    if count == 1:
        body(*refs)
    else:
        for k in range(count):
            pl.when(j == sel[4 + k])(lambda k=k: body(*refs[4 * k : 4 * k + 4]))


def grads(sel, inputs, grad_out, write_proj, read_proj, log_decay, gint, dots, per_group, scale, head_size):
    rows, width = write_proj.shape
    heads = log_decay.shape[0]
    lanes = GROUP * head_size
    wide = pl.BlockSpec((rows, lanes), lambda j, s: (0, j))
    decays = pl.BlockSpec((GROUP, rows), lambda j, s: (j, 0))
    flat = [a for group in per_group for a in group]

    def kernel(*refs):
        grads_kernel(scale, len(per_group), *refs)

    return pl.pallas_call(
        kernel,
        grid_spec=pltpu.PrefetchScalarGridSpec(
            num_scalar_prefetch=1,
            grid=(heads // GROUP,),
            in_specs=[wide, wide, full(write_proj), full(read_proj), decays, wide, decays] + [full(a) for a in flat],
            out_specs=[wide, decays],
        ),
        out_shape=[jax.ShapeDtypeStruct((rows, heads * head_size), BF16), jax.ShapeDtypeStruct((heads, rows), F32)],
        compiler_params=params(),
        cost_estimate=pl.CostEstimate(
            flops=8 * rows * width * heads * head_size, bytes_accessed=12 * rows * heads * head_size, transcendentals=0
        ),
        name="grads",
    )(sel, inputs, grad_out, write_proj, read_proj, log_decay, gint, dots, *flat)


def join_kernel(sel, *refs):
    parts, (read_ref, write_ref) = refs[:-2], refs[-2:]
    step = parts[0].shape[0] // 2
    for k, part in enumerate(parts):
        at = pl.multiple_of(jnp.bitwise_xor(sel[3], k) * step, step)
        read_ref[pl.ds(at, step), :] = part[0:step, :]
        write_ref[pl.ds(at, step), :] = part[step : 2 * step, :]


def swap(values, axis, mask):
    count = lax.axis_size(axis)
    return lax.ppermute(values, axis, [(i, i ^ mask) for i in range(count)])


def scan_over(pay, width, reverse):
    count = lax.axis_size("seq")
    place = lax.axis_index("seq")
    ahead = count - 1 - place if reverse else place
    part = pay[width : 2 * width] if reverse else pay[0:width]
    dec = pay[2 * width : 2 * width + 1]

    def shifted(values, hop):
        route = [(i, i - hop) if reverse else (i, i + hop) for i in range(count)]
        return lax.ppermute(values, "seq", [(a, b) for a, b in route if 0 <= b < count])

    hop = 1
    while hop < count:
        got_part, got_dec = shifted(part, hop), shifted(dec, hop)
        use = ahead >= hop
        part = jnp.where(use, part + dec * got_part, part)
        dec = jnp.where(use, dec * got_dec, dec)
        hop *= 2
    return shifted(part, 1)


def local(inputs, grad_out, write_proj, read_proj, log_decay):
    head_count, rows = log_decay.shape
    head_size = inputs.shape[1] // head_count
    width = write_proj.shape[1]
    lanes = GROUP * head_size
    groups = head_count // GROUP
    seq_count, head_parts = lax.axis_size("seq"), lax.axis_size("head")
    scale = (head_size * rows * seq_count) ** (-0.5)
    place = lax.axis_index("seq").astype(jnp.int32)
    mine = place % 2
    fast = seq_count == 8 and groups == 2
    order = [mine, 1 - mine] if fast else [jnp.int32(k) for k in range(groups)]
    sel = jnp.stack(
        [mine, (place // 2) % 2, (place // 4) % 2, lax.axis_index("head").astype(jnp.int32)] + order
    )
    data = (inputs, grad_out, write_proj, read_proj, log_decay)
    if fast:
        other_state = states(order[1][None], *data, head_size)
        got = swap(other_state[0], "seq", 1)
        mine_state = states(order[0][None], *data, head_size)
        per_state = [mine_state, other_state]
        px, py = whole_call(
            chip_kernel, "chip", sel, (mine_state[0], got), [((width + 8, lanes), F32)] * 2
        )
        rx, ry, rd = swap(px, "seq", 2), swap(py, "seq", 4), swap(py, "seq", 6)
    else:
        per_state = [states(k[None], *data, head_size) for k in order]
    gint, dots, early = intra(*data, head_size)
    if fast:
        own, send = whole_call(
            carry_kernel, "carry", sel, (rx, ry, rd, mine_state[0], got), [((2 * width, lanes), F32)] * 2
        )
        carried = [own, swap(send, "seq", 1)]
    else:
        carried = [
            jnp.concatenate([scan_over(s[0], width, False), scan_over(s[0], width, True)]) for s in per_state
        ]
    acc = early.reshape(2 * rows, width)
    late_flops = 8 * rows * lanes * width
    for k in range(groups):
        pay, iw, gw, part, tot = per_state[k]
        args = (iw, gw, carried[k], part, tot, acc)
        if k < groups - 1 or head_parts != 4:
            (acc,) = whole_call(late_kernel, "late", sel, args, [((2 * rows, width), F32)], late_flops)
        else:
            cut = rows // head_parts
            outs = [jax.ShapeDtypeStruct((2 * cut, width), F32)] * head_parts
            pieces = pl.pallas_call(
                cut_kernel,
                grid_spec=pltpu.PrefetchScalarGridSpec(
                    num_scalar_prefetch=1,
                    grid=(1,),
                    in_specs=[full(a) for a in args],
                    out_specs=[full(o) for o in outs],
                    scratch_shapes=[pltpu.VMEM((2 * rows, width), F32)],
                ),
                out_shape=outs,
                compiler_params=params(),
                cost_estimate=pl.CostEstimate(flops=late_flops, bytes_accessed=4 * rows * lanes * 2, transcendentals=0),
                name="late_cut",
            )(sel, *args)
    per_group = [(carried[k], per_state[k][3], per_state[k][4], per_state[k][0]) for k in range(groups)]
    if head_parts == 4:
        got = [swap(pieces[k], "head", k) for k in (1, 2, 3)]
        grad_inputs, grad_decay = grads(sel, *data, gint, dots, per_group, scale, head_size)
        total = pieces[0] + got[0] + got[1] + got[2]
        got = [swap(total, "head", k) for k in (1, 2, 3)]
        grad_read, grad_write = whole_call(
            join_kernel, "join", sel, (total, *got), [((rows, width), F32)] * 2
        )
    else:
        grad_inputs, grad_decay = grads(sel, *data, gint, dots, per_group, scale, head_size)
        summed = lax.psum(acc, "head")
        grad_read, grad_write = summed[:rows], summed[rows:]
    return grad_inputs, grad_write, grad_read, grad_decay


def solution(mesh):
    in_specs = (
        P("seq", "head"),
        P("seq", "head"),
        P("seq", None),
        P("seq", None),
        P("head", "seq"),
    )
    out_specs = (P("seq", "head"), P("seq", None), P("seq", None), P("head", "seq"))
    return jax.shard_map(local, mesh=mesh, in_specs=in_specs, out_specs=out_specs, check_vma=False)
```

time: 217 us -> 71.3 us (0.33)
  waiting for transfers between devices: 83.1 us -> 26.9 us
  blocking collectives: 32.1 us -> 0 us
  local copies, waits for them, and re-layouts: 35.5 us -> 8.24 us
  matrix products: 26 us -> 0 us
  other arithmetic: 23.3 us -> 0.03 us
  Pallas kernels: 0 us -> 21.2 us
  between operations: 14.8 us -> 0.78 us
  starting transfers between devices: 0.12 us -> 13.9 us
    all_gather x2 -> x0, waiting for transfers between devices: 51.9 us -> none  [carried_in(): gathered = jax.tree.map(lambda a: lax.all_gather(a, axis), part)]
    psum x1 -> x0, waiting for transfers between devices: 31.2 us -> none  [local(): lax.psum((write_local + write_late, read_local + read_late), 'head')]
    ppermute x0 -> x11, waiting for transfers between devices: none -> 26.9 us  [swap(): return lax.ppermute(values, axis, [(i, i ^ mask) for i in range(count)])]
    dot_general x28 -> x0, matrix products: 26 us -> none  [the longest x8 8.17 us: split_dot(): jnp.einsum(form, data, low, preferred_element_type=jnp.float32)]
    unnamed x1 -> x0, blocking collectives: 21.9 us -> none
    pallas_call x0 -> x9, Pallas kernels: none -> 21.2 us  [the longest x1 7.65 us: grads(): pl.pallas_call(kernel, grid_spec=pltpu.PrefetchScalarGridSpec(num_scalar_...]
    ppermute x0 -> x11, starting transfers between devices: none -> 13.9 us  [swap(): return lax.ppermute(values, axis, [(i, i ^ mask) for i in range(count)])]
    add x18 -> x1, other arithmetic: 13.1 us -> 0.03 us  [local(): total = pieces[0] + got[0] + got[1] + got[2]]
  transfers between devices with their start and end apart: 3 -> 11, of which waited for: 3 -> 7; matrix products, arithmetic and copies ran while one was open for 10% -> 0% of each run, Pallas kernels for 0% -> 21%
where the time goes in v1:
time: 71.3 us; the launch traced here: 71 us
  waiting for transfers between devices  26.9 us (38%)
  Pallas kernels  21.2 us (30%)
  starting transfers between devices  13.9 us (19%)
  local copies, waits for them, and re-layouts  8.24 us (12%)
  between operations  0.78 us (1%)
    ppermute x11, waiting for transfers between devices, swap(): return lax.ppermute(values, axis, [(i, i ^ mask) for i in range(count)])  26.9 us
    ppermute x11, starting transfers between devices, swap(): return lax.ppermute(values, axis, [(i, i ^ mask) for i in range(count)])  13.9 us
    unnamed x30, local copies, waits for them, and re-layouts  8.16 us
    pallas_call x1, Pallas kernels, grads(): pl.pallas_call(kernel, grid_spec=pltpu.PrefetchScalarGridSpec(num_scalar_...  7.65 us
    pallas_call x1, Pallas kernels, intra(): pl.pallas_call(intra_kernel, grid=(spans, groups), in_specs=[wide, wide,...  5.3 us
    pallas_call x4, Pallas kernels, whole_call(): pl.pallas_call(kernel, grid_spec=pltpu.PrefetchScalarGridSpec(num_scalar_...  3.79 us
    pallas_call x2, Pallas kernels, states(): pl.pallas_call(state_kernel, grid_spec=pltpu.PrefetchScalarGridSpec(num_s...  3.41 us
  transfers between devices with their start and end apart: 11, of which 7 were waited for; matrix products, arithmetic and copies ran while one was open for 0% of the time, Pallas kernels for 21%

profile of v1, /device:TPU:0, one launch (start us, length us, event | category | flops | bytes accessed | tf_op | source)
XLA Modules:
  0.0 71.0 jit_solution(9813701530999351215)
XLA Ops:
  0.7 1.2 %copy-done = bf16[512,1024]{1,0:T(8,128)(2,1)S(1)} copy-done((bf16[512,1024]{1,0:T(8,128)(2,1)S(1)}, bf16[512,1024]{1,0:T(8,128)(2,1)}, u32[]{:S(2)}) %copy-start) | copy-done | bytes 1048600
  1.9 1.2 %copy-done.2 = bf16[512,1024]{1,0:T(8,128)(2,1)S(1)} copy-done((bf16[512,1024]{1,0:T(8,128)(2,1)S(1)}, bf16[512,1024]{1,0:T(8,128)(2,1)}, u32[]{:S(2)}) %copy-start.2) | copy-done | bytes 1048600
  3.1 0.9 %copy-done.5 = bf16[512,128]{1,0:T(8,128)(2,1)S(1)} copy-done((bf16[512,128]{1,0:T(8,128)(2,1)S(1)}, bf16[512,128]{1,0:T(8,128)(2,1)}, u32[]{:S(2)}) %copy-start.5) | copy-done | bytes 131096
  4.0 0.9 %copy-done.7 = bf16[512,128]{1,0:T(8,128)(2,1)S(1)} copy-done((bf16[512,128]{1,0:T(8,128)(2,1)S(1)}, bf16[512,128]{1,0:T(8,128)(2,1)}, u32[]{:S(2)}) %copy-start.7) | copy-done | bytes 131096
  4.9 0.8 %copy-done.13 = f32[16,512]{1,0:T(8,128)S(1)} copy-done((f32[16,512]{1,0:T(8,128)S(1)}, f32[16,512]{1,0:T(8,128)}, u32[]{:S(2)}) %copy-start.13) | copy-done | bytes 32792
  5.7 2.1 %states.3 = (f32[264,512]{1,0:T(8,128)}, bf16[512,512]{1,0:T(8,128)(2,1)S(1)}, bf16[512,512]{1,0:T(8,128)(2,1)S(1)}, f32[256,512]{1,0:T(8,128)S(1)}, f32[16,512]{1,0:T(8,128)S(1)}) custom-call(s32[1]{0:T(128)} %bitcast.4.sel, bf16[512,1024]{1,0:T(8,128)(2,1)S(1)} %copy-done, bf16[512,1024]{1,0:T(8,128)(2,1)S(1)} %copy-done.2, ...), custom_call_target="tpu_custom_call" | custom-call | flops 134217728 | bytes 2097152 | tf_op jit(solution)/shard_map/states/pallas_call | solution.py:102
  7.8 0.8 %copy-done.9 = bf16[512,512]{1,0:T(8,128)(2,1)} copy-done((bf16[512,512]{1,0:T(8,128)(2,1)}, bf16[512,512]{1,0:T(8,128)(2,1)S(1)}, u32[]{:S(2)}) %copy-start.9) | copy-done | bytes 524312
  8.6 0.8 %copy-done.11 = bf16[512,512]{1,0:T(8,128)(2,1)} copy-done((bf16[512,512]{1,0:T(8,128)(2,1)}, bf16[512,512]{1,0:T(8,128)(2,1)S(1)}, u32[]{:S(2)}) %copy-start.11) | copy-done | bytes 524312
  9.4 0.5 collective-permute-start
  10.0 1.3 %states.2 = (f32[264,512]{1,0:T(8,128)S(1)}, bf16[512,512]{1,0:T(8,128)(2,1)S(1)}, bf16[512,512]{1,0:T(8,128)(2,1)S(1)}, f32[256,512]{1,0:T(8,128)S(1)}, f32[16,512]{1,0:T(8,128)S(1)}) custom-call(s32[1]{0:T(128)} %bitcast.sel, bf16[512,1024]{1,0:T(8,128)(2,1)S(1)} %copy-done.1, bf16[512,1024]{1,0:T(8,128)(2,1)S(1)} %copy-done.3, ...), custom_call_target="tpu_custom_call" | custom-call | flops 134217728 | bytes 2097152 | tf_op jit(solution)/shard_map/states/pallas_call | solution.py:102
  11.3 0.3 collective-permute-done.got_ref
  11.6 0.7 chip.1
  12.3 2.9 %collective-permute-start.1 = (f32[136,512]{1,0:T(8,128)S(1)}, f32[136,512]{1,0:T(8,128)S(1)}, u32[]{:S(2)}, u32[]{:S(2)}) collective-permute-start(f32[136,512]{1,0:T(8,128)S(1)} %get-tuple-element.33), channel_id=1, source_target_pairs={{0,8},{4,12},{8,0},{12,4},{16,24},{20,28},{24,16},{28,20},{1,9},{5... | collective-permute-start | bytes 835592 | tf_op jit(solution)/shard_map/ppermute | solution.py:374
  15.2 1.5 %collective-permute-start.3 = (f32[136,512]{1,0:T(8,128)S(1)}, f32[136,512]{1,0:T(8,128)S(1)}, u32[]{:S(2)}, u32[]{:S(2)}) collective-permute-start(f32[136,512]{1,0:T(8,128)S(1)} %get-tuple-element.34), channel_id=1, source_target_pairs={{0,24},{4,28},{8,16},{12,20},{16,8},{20,12},{24,0},{28,4},{1,25},{... | collective-permute-start | bytes 835592 | tf_op jit(solution)/shard_map/ppermute | solution.py:374
  16.7 5.9 %collective-permute-done.1.rx_ref = f32[136,512]{1,0:T(8,128)S(1)} collective-permute-done((f32[136,512]{1,0:T(8,128)S(1)}, f32[136,512]{1,0:T(8,128)S(1)}, u32[]{:S(2)}, u32[]{:S(2)}) %collective-permute-start.1) | collective-permute-done | bytes 278560 | tf_op jit(solution)/shard_map/ppermute | solution.py:374
  22.6 6.8 %collective-permute-done.3.rd_ref = f32[136,512]{1,0:T(8,128)S(1)} collective-permute-done((f32[136,512]{1,0:T(8,128)S(1)}, f32[136,512]{1,0:T(8,128)S(1)}, u32[]{:S(2)}, u32[]{:S(2)}) %collective-permute-start.3) | collective-permute-done | bytes 278560 | tf_op jit(solution)/shard_map/ppermute | solution.py:374
  29.4 1.4 %collective-permute-done.2.ry_ref = f32[136,512]{1,0:T(8,128)S(1)} collective-permute-done((f32[136,512]{1,0:T(8,128)S(1)}, f32[136,512]{1,0:T(8,128)S(1)}, u32[]{:S(2)}, u32[]{:S(2)}) %collective-permute-start.2) | collective-permute-done | bytes 278560 | tf_op jit(solution)/shard_map/ppermute | solution.py:374
  30.8 0.8 %carry.1 = (f32[256,512]{1,0:T(8,128)S(1)}, f32[256,512]{1,0:T(8,128)S(1)}) custom-call(s32[6]{0:T(128)S(1)} %stack.24.sel.refs_0_, f32[136,512]{1,0:T(8,128)S(1)} %collective-permute-done.1.rx_ref, f32[136,512]{1,0:T(8,128)S(1)} %collective-permute-done.2.ry_ref, f32[136,512]{1,0:T(8,128)S(1)} %collective-permute-done.3.rd_ref, ...), custom_call_target="tpu_custom_call" | custom-call | bytes 2965504 | tf_op jit(solution)/shard_map/carry/pallas_call | solution.py:149
  31.7 5.3 %intra.1 = (f32[512,1024]{1,0:T(8,128)S(1)}, f32[16,512]{1,0:T(8,128)S(1)}, f32[2,512,128]{2,1,0:T(8,128)S(1)}) custom-call(bf16[512,1024]{1,0:T(8,128)(2,1)S(1)} %copy-done.1, bf16[512,1024]{1,0:T(8,128)(2,1)S(1)} %copy-done.3, bf16[512,128]{1,0:T(8,128)(2,1)S(1)} %copy-done.6, bf16[512,128]{1,0:T(8,128)(2,1)S(1)} %copy-done.8, f32[16,512]{1,0:T(8,128)S(1)} %copy-done.14), custom_call_target="tpu_custom_call" | custom-call | flops 2147483648 | bytes 4194304 | tf_op jit(solution)/shard_map/intra/pallas_call | solution.py:279
  37.0 1.3 %copy-done.4 = f32[512,1024]{1,0:T(8,128)} copy-done((f32[512,1024]{1,0:T(8,128)}, f32[512,1024]{1,0:T(8,128)S(1)}, u32[]{:S(2)}) %copy-start.4) | copy-done | bytes 2097176
  38.3 1.0 %late.1.acc_ref = f32[1024,128]{1,0:T(8,128)S(1)} custom-call(s32[6]{0:T(128)S(1)} %stack.24.sel.refs_0_, bf16[512,512]{1,0:T(8,128)(2,1)S(1)} %get-tuple-element.44.iw_ref, bf16[512,512]{1,0:T(8,128)(2,1)S(1)} %get-tuple-element.45.gw_ref, f32[256,512]{1,0:T(8,128)S(1)} %get-tuple-element.35.refs_8_.car_ref, ...), custom_call_target="tpu_custom_call" | custom-call | flops 268435456 | bytes 3178496 | tf_op jit(solution)/shard_map/late/pallas_call | solution.py:149
  39.5 1.0 %late_cut.1 = (f32[256,128]{1,0:T(8,128)S(1)}, f32[256,128]{1,0:T(8,128)S(1)}, f32[256,128]{1,0:T(8,128)S(1)}, f32[256,128]{1,0:T(8,128)S(1)}) custom-call(s32[6]{0:T(128)S(1)} %stack.24.sel.refs_0_, bf16[512,512]{1,0:T(8,128)(2,1)S(1)} %copy-done.10, bf16[512,512]{1,0:T(8,128)(2,1)S(1)} %copy-done.12, ...), custom_call_target="tpu_custom_call" | custom-call | flops 268435456 | bytes 2097152 | tf_op jit(solution)/shard_map/late_cut/pallas_call | solution.py:445
  40.6 1.6 %collective-permute-start.5 = (f32[256,128]{1,0:T(8,128)S(1)}, f32[256,128]{1,0:T(8,128)S(1)}, u32[]{:S(2)}, u32[]{:S(2)}) collective-permute-start(f32[256,128]{1,0:T(8,128)S(1)} %get-tuple-element.48), channel_id=1, source_target_pairs={{0,1},{1,0},{2,3},{3,2},{4,5},{5,4},{6,7},{7,6},{8,9},{9,8},{10,11... | collective-permute-start | bytes 393224 | tf_op jit(solution)/shard_map/ppermute | solution.py:374
  42.2 2.6 %collective-permute-start.6 = (f32[256,128]{1,0:T(8,128)S(1)}, f32[256,128]{1,0:T(8,128)S(1)}, u32[]{:S(2)}, u32[]{:S(2)}) collective-permute-start(f32[256,128]{1,0:T(8,128)S(1)} %get-tuple-element.49), channel_id=1, source_target_pairs={{0,2},{1,3},{2,0},{3,1},{4,6},{5,7},{6,4},{7,5},{8,10},{9,11},{10,... | collective-permute-start | bytes 393224 | tf_op jit(solution)/shard_map/ppermute | solution.py:374
  45.0 3.8 %collective-permute-done.5 = f32[256,128]{1,0:T(8,128)S(1)} collective-permute-done((f32[256,128]{1,0:T(8,128)S(1)}, f32[256,128]{1,0:T(8,128)S(1)}, u32[]{:S(2)}, u32[]{:S(2)}) %collective-permute-start.5) | collective-permute-done | bytes 131104 | tf_op jit(solution)/shard_map/ppermute | solution.py:374
  48.8 6.3 %collective-permute-done.6 = f32[256,128]{1,0:T(8,128)S(1)} collective-permute-done((f32[256,128]{1,0:T(8,128)S(1)}, f32[256,128]{1,0:T(8,128)S(1)}, u32[]{:S(2)}, u32[]{:S(2)}) %collective-permute-start.6) | collective-permute-done | bytes 131104 | tf_op jit(solution)/shard_map/ppermute | solution.py:374
  55.1 2.5 %collective-permute-start.10 = (f32[256,128]{1,0:T(8,128)S(1)}, f32[256,128]{1,0:T(8,128)S(1)}, u32[]{:S(2)}, u32[]{:S(2)}) collective-permute-start(f32[256,128]{1,0:T(8,128)S(1)} %add_add_fusion.refs_0_), channel_id=1, source_target_pairs={{0,3},{1,2},{2,1},{3,0},{4,7},{5,6},{6,5},{7,4},{8,11},{9,10},{10,... | collective-permute-start | bytes 393224 | tf_op jit(solution)/shard_map/ppermute | solution.py:374
  57.7 1.6 %collective-permute-start.9 = (f32[256,128]{1,0:T(8,128)S(1)}, f32[256,128]{1,0:T(8,128)S(1)}, u32[]{:S(2)}, u32[]{:S(2)}) collective-permute-start(f32[256,128]{1,0:T(8,128)S(1)} %add_add_fusion.refs_0_), channel_id=1, source_target_pairs={{0,2},{1,3},{2,0},{3,1},{4,6},{5,7},{6,4},{7,5},{8,10},{9,11},{10,... | collective-permute-start | bytes 393224 | tf_op jit(solution)/shard_map/ppermute | solution.py:374
  59.3 0.3 collective-permute-start.8
  59.6 7.7 %grads.1 = (bf16[512,1024]{1,0:T(8,128)(2,1)}, f32[16,512]{1,0:T(8,128)}) custom-call(s32[6]{0:T(128)S(1)} %stack.24.sel.refs_0_, bf16[512,1024]{1,0:T(8,128)(2,1)S(1)} %copy-done.1, bf16[512,1024]{1,0:T(8,128)(2,1)S(1)} %copy-done.3, bf16[512,128]{1,0:T(8,128)(2,1)S(1)} %copy-done.6, bf16[512,128]{1,0:T(8,128)(2,1)S(1)} %copy-done.8, ...), custom_call_target="tpu_custom_call" | custom-call | flops 536870912 | bytes 6291456 | tf_op jit(solution)/shard_map/grads/pallas_call | solution.py:346
  67.3 2.4 %collective-permute-done.9.refs_2_ = f32[256,128]{1,0:T(8,128)S(1)} collective-permute-done((f32[256,128]{1,0:T(8,128)S(1)}, f32[256,128]{1,0:T(8,128)S(1)}, u32[]{:S(2)}, u32[]{:S(2)}) %collective-permute-start.9) | collective-permute-done | bytes 131104 | tf_op jit(solution)/shard_map/ppermute | solution.py:374
  69.6 1.4 %join.1 = (f32[512,128]{1,0:T(8,128)}, f32[512,128]{1,0:T(8,128)}) custom-call(s32[6]{0:T(128)S(1)} %stack.24.sel.refs_0_, f32[256,128]{1,0:T(8,128)S(1)} %add_add_fusion.refs_0_, f32[256,128]{1,0:T(8,128)S(1)} %collective-permute-done.8.refs_1_, f32[256,128]{1,0:T(8,128)S(1)} %collective-permute-done.9.refs_2_, f32[256,128]{1,0:T(8,128)S(1)} %collective-permute-done.10.refs_3_), custom_call_target="tpu_custom_call" | custom-call | bytes 1048576 | tf_op jit(solution)/shard_map/join/pallas_call | solution.py:149
  (31 shorter events, 0.7 us)
Async XLA Ops:
  0.6 9.3 %copy-start.14 = (f32[16,512]{1,0:T(8,128)S(1)}, f32[16,512]{1,0:T(8,128)}, u32[]{:S(2)}) copy-start(f32[16,512]{1,0:T(8,128)} %refs_5_.1) | copy-start | bytes 98308
  0.7 1.2 %copy-start = (bf16[512,1024]{1,0:T(8,128)(2,1)S(1)}, bf16[512,1024]{1,0:T(8,128)(2,1)}, u32[]{:S(2)}) copy-start(bf16[512,1024]{1,0:T(8,128)(2,1)} %refs_1_.1) | copy-start | bytes 3145732
  1.9 1.2 %copy-start.2 = (bf16[512,1024]{1,0:T(8,128)(2,1)S(1)}, bf16[512,1024]{1,0:T(8,128)(2,1)}, u32[]{:S(2)}) copy-start(bf16[512,1024]{1,0:T(8,128)(2,1)} %refs_2_.1) | copy-start | bytes 3145732
  3.1 0.9 %copy-start.5 = (bf16[512,128]{1,0:T(8,128)(2,1)S(1)}, bf16[512,128]{1,0:T(8,128)(2,1)}, u32[]{:S(2)}) copy-start(bf16[512,128]{1,0:T(8,128)(2,1)} %refs_3_.1) | copy-start | bytes 393220
  4.0 0.9 %copy-start.7 = (bf16[512,128]{1,0:T(8,128)(2,1)S(1)}, bf16[512,128]{1,0:T(8,128)(2,1)}, u32[]{:S(2)}) copy-start(bf16[512,128]{1,0:T(8,128)(2,1)} %refs_4_.1) | copy-start | bytes 393220
  4.9 0.8 %copy-start.13 = (f32[16,512]{1,0:T(8,128)S(1)}, f32[16,512]{1,0:T(8,128)}, u32[]{:S(2)}) copy-start(f32[16,512]{1,0:T(8,128)} %refs_5_.1) | copy-start | bytes 98308
  5.7 4.2 %copy-start.1 = (bf16[512,1024]{1,0:T(8,128)(2,1)S(1)}, bf16[512,1024]{1,0:T(8,128)(2,1)}, u32[]{:S(2)}) copy-start(bf16[512,1024]{1,0:T(8,128)(2,1)} %refs_1_.1) | copy-start | bytes 3145732
  5.7 4.2 %copy-start.3 = (bf16[512,1024]{1,0:T(8,128)(2,1)S(1)}, bf16[512,1024]{1,0:T(8,128)(2,1)}, u32[]{:S(2)}) copy-start(bf16[512,1024]{1,0:T(8,128)(2,1)} %refs_2_.1) | copy-start | bytes 3145732
  5.7 4.3 %copy-start.6 = (bf16[512,128]{1,0:T(8,128)(2,1)S(1)}, bf16[512,128]{1,0:T(8,128)(2,1)}, u32[]{:S(2)}) copy-start(bf16[512,128]{1,0:T(8,128)(2,1)} %refs_3_.1) | copy-start | bytes 393220
  5.7 4.3 %copy-start.8 = (bf16[512,128]{1,0:T(8,128)(2,1)S(1)}, bf16[512,128]{1,0:T(8,128)(2,1)}, u32[]{:S(2)}) copy-start(bf16[512,128]{1,0:T(8,128)(2,1)} %refs_4_.1) | copy-start | bytes 393220
  7.8 0.8 %copy-start.9 = (bf16[512,512]{1,0:T(8,128)(2,1)}, bf16[512,512]{1,0:T(8,128)(2,1)S(1)}, u32[]{:S(2)}) copy-start(bf16[512,512]{1,0:T(8,128)(2,1)S(1)} %get-tuple-element.42.iw_ref) | copy-start | bytes 1572868
  8.6 0.8 %copy-start.11 = (bf16[512,512]{1,0:T(8,128)(2,1)}, bf16[512,512]{1,0:T(8,128)(2,1)S(1)}, u32[]{:S(2)}) copy-start(bf16[512,512]{1,0:T(8,128)(2,1)S(1)} %get-tuple-element.43.gw_ref) | copy-start | bytes 1572868
  9.4 2.2 %collective-permute-start = (f32[264,512]{1,0:T(8,128)}, f32[264,512]{1,0:T(8,128)S(1)}, u32[]{:S(2)}, u32[]{:S(2)}) collective-permute-start(f32[264,512]{1,0:T(8,128)} %get-tuple-element.32.refs_15_), channel_id=1, source_target_pairs={{0,4},{4,0},{8,12},{12,8},{16,20},{20,16},{24,28},{28,24},{1,5},{5... | collective-permute-start | bytes 1622024 | tf_op jit(solution)/shard_map/ppermute | solution.py:374
  12.3 10.4 %collective-permute-start.1 = (f32[136,512]{1,0:T(8,128)S(1)}, f32[136,512]{1,0:T(8,128)S(1)}, u32[]{:S(2)}, u32[]{:S(2)}) collective-permute-start(f32[136,512]{1,0:T(8,128)S(1)} %get-tuple-element.33), channel_id=1, source_target_pairs={{0,8},{4,12},{8,0},{12,4},{16,24},{20,28},{24,16},{28,20},{1,9},{5... | collective-permute-start | bytes 835592 | tf_op jit(solution)/shard_map/ppermute | solution.py:374
  15.2 14.2 %collective-permute-start.3 = (f32[136,512]{1,0:T(8,128)S(1)}, f32[136,512]{1,0:T(8,128)S(1)}, u32[]{:S(2)}, u32[]{:S(2)}) collective-permute-start(f32[136,512]{1,0:T(8,128)S(1)} %get-tuple-element.34), channel_id=1, source_target_pairs={{0,24},{4,28},{8,16},{12,20},{16,8},{20,12},{24,0},{28,4},{1,25},{... | collective-permute-start | bytes 835592 | tf_op jit(solution)/shard_map/ppermute | solution.py:374
  16.7 14.1 %collective-permute-start.2 = (f32[136,512]{1,0:T(8,128)S(1)}, f32[136,512]{1,0:T(8,128)S(1)}, u32[]{:S(2)}, u32[]{:S(2)}) collective-permute-start(f32[136,512]{1,0:T(8,128)S(1)} %get-tuple-element.34), channel_id=1, source_target_pairs={{0,16},{4,20},{8,24},{12,28},{16,0},{20,4},{24,8},{28,12},{1,17},{... | collective-permute-start | bytes 835592 | tf_op jit(solution)/shard_map/ppermute | solution.py:374
  31.6 7.7 %collective-permute-start.4 = (f32[256,512]{1,0:T(8,128)S(1)}, f32[256,512]{1,0:T(8,128)S(1)}, u32[]{:S(2)}, u32[]{:S(2)}) collective-permute-start(f32[256,512]{1,0:T(8,128)S(1)} %get-tuple-element.38), channel_id=1, source_target_pairs={{0,4},{4,0},{8,12},{12,8},{16,20},{20,16},{24,28},{28,24},{1,5},{5... | collective-permute-start | bytes 1572872 | tf_op jit(solution)/shard_map/ppermute | solution.py:374
  37.0 1.4 %copy-start.4 = (f32[512,1024]{1,0:T(8,128)}, f32[512,1024]{1,0:T(8,128)S(1)}, u32[]{:S(2)}) copy-start(f32[512,1024]{1,0:T(8,128)S(1)} %get-tuple-element.29.refs_6_) | copy-start | bytes 6291460
  38.3 1.0 %copy-start.10 = (bf16[512,512]{1,0:T(8,128)(2,1)S(1)}, bf16[512,512]{1,0:T(8,128)(2,1)}, u32[]{:S(2)}) copy-start(bf16[512,512]{1,0:T(8,128)(2,1)} %copy-done.9) | copy-start | bytes 1572868
  38.3 1.2 %copy-start.12 = (bf16[512,512]{1,0:T(8,128)(2,1)S(1)}, bf16[512,512]{1,0:T(8,128)(2,1)}, u32[]{:S(2)}) copy-start(bf16[512,512]{1,0:T(8,128)(2,1)} %copy-done.11) | copy-start | bytes 1572868
  40.6 8.2 %collective-permute-start.5 = (f32[256,128]{1,0:T(8,128)S(1)}, f32[256,128]{1,0:T(8,128)S(1)}, u32[]{:S(2)}, u32[]{:S(2)}) collective-permute-start(f32[256,128]{1,0:T(8,128)S(1)} %get-tuple-element.48), channel_id=1, source_target_pairs={{0,1},{1,0},{2,3},{3,2},{4,5},{5,4},{6,7},{7,6},{8,9},{9,8},{10,11... | collective-permute-start | bytes 393224 | tf_op jit(solution)/shard_map/ppermute | solution.py:374
  42.2 12.9 %collective-permute-start.6 = (f32[256,128]{1,0:T(8,128)S(1)}, f32[256,128]{1,0:T(8,128)S(1)}, u32[]{:S(2)}, u32[]{:S(2)}) collective-permute-start(f32[256,128]{1,0:T(8,128)S(1)} %get-tuple-element.49), channel_id=1, source_target_pairs={{0,2},{1,3},{2,0},{3,1},{4,6},{5,7},{6,4},{7,5},{8,10},{9,11},{10,... | collective-permute-start | bytes 393224 | tf_op jit(solution)/shard_map/ppermute | solution.py:374
  44.8 10.3 %collective-permute-start.7 = (f32[256,128]{1,0:T(8,128)S(1)}, f32[256,128]{1,0:T(8,128)S(1)}, u32[]{:S(2)}, u32[]{:S(2)}) collective-permute-start(f32[256,128]{1,0:T(8,128)S(1)} %get-tuple-element.50), channel_id=1, source_target_pairs={{0,3},{1,2},{2,1},{3,0},{4,7},{5,6},{6,5},{7,4},{8,11},{9,10},{10,... | collective-permute-start | bytes 393224 | tf_op jit(solution)/shard_map/ppermute | solution.py:374
  55.1 12.1 %collective-permute-start.10 = (f32[256,128]{1,0:T(8,128)S(1)}, f32[256,128]{1,0:T(8,128)S(1)}, u32[]{:S(2)}, u32[]{:S(2)}) collective-permute-start(f32[256,128]{1,0:T(8,128)S(1)} %add_add_fusion.refs_0_), channel_id=1, source_target_pairs={{0,3},{1,2},{2,1},{3,0},{4,7},{5,6},{6,5},{7,4},{8,11},{9,10},{10,... | collective-permute-start | bytes 393224 | tf_op jit(solution)/shard_map/ppermute | solution.py:374
  57.7 11.9 %collective-permute-start.9 = (f32[256,128]{1,0:T(8,128)S(1)}, f32[256,128]{1,0:T(8,128)S(1)}, u32[]{:S(2)}, u32[]{:S(2)}) collective-permute-start(f32[256,128]{1,0:T(8,128)S(1)} %add_add_fusion.refs_0_), channel_id=1, source_target_pairs={{0,2},{1,3},{2,0},{3,1},{4,6},{5,7},{6,4},{7,5},{8,10},{9,11},{10,... | collective-permute-start | bytes 393224 | tf_op jit(solution)/shard_map/ppermute | solution.py:374
  59.3 10.3 %collective-permute-start.8 = (f32[256,128]{1,0:T(8,128)S(1)}, f32[256,128]{1,0:T(8,128)S(1)}, u32[]{:S(2)}, u32[]{:S(2)}) collective-permute-start(f32[256,128]{1,0:T(8,128)S(1)} %add_add_fusion.refs_0_), channel_id=1, source_target_pairs={{0,1},{1,0},{2,3},{3,2},{4,5},{5,4},{6,7},{7,6},{8,9},{9,8},{10,11... | collective-permute-start | bytes 393224 | tf_op jit(solution)/shard_map/ppermute | solution.py:374

commit v2 on v1

v2 whole, which is shorter than its diff:
```python
import functools

import jax
import jax.numpy as jnp
from jax import lax
from jax.experimental import pallas as pl
from jax.experimental.pallas import tpu as pltpu
from jax.sharding import PartitionSpec as P

Q = 256
GROUP = 8
F32 = jnp.float32
BF16 = jnp.bfloat16
FREE = pl.CostEstimate(flops=1000, bytes_accessed=1000, transcendentals=0)


def dot(a, b):
    return jnp.dot(a, b, preferred_element_type=F32)


def dot_t(a, b):
    return lax.dot_general(a, b, (((1,), (1,)), ((), ())), preferred_element_type=F32)


def iota(shape, dim):
    return lax.broadcasted_iota(jnp.int32, shape, dim)


def split_two(values):
    high = values.astype(BF16).astype(F32)
    return high, values - high


def split_three(values):
    high, rest = split_two(values)
    mid, low = split_two(rest)
    return high, mid, low


def times_ones(values, ones):
    high, mid, low = split_three(values)
    stacked = jnp.concatenate([high, mid, low, jnp.zeros_like(low)], axis=0).astype(BF16)
    out = dot(stacked, ones)
    return out[0:GROUP] + out[GROUP : 2 * GROUP] + out[2 * GROUP : 3 * GROUP]


def running_of(decay_blk):
    upto = (iota((Q, Q), 0) <= iota((Q, Q), 1)).astype(BF16)
    return times_ones(decay_blk, upto)


def spread_decays(running, head_size):
    lanes = GROUP * head_size
    total = running[:, Q - 1 : Q]
    parts = split_two(jnp.exp(running)) + split_two(jnp.exp(total - running))
    stacked = jnp.concatenate(parts, axis=0).T.astype(BF16)
    row = iota((4 * GROUP, lanes), 0)
    owner = row % GROUP == iota((4 * GROUP, lanes), 1) // head_size
    first = (owner & (row < 2 * GROUP)).astype(F32).astype(BF16)
    second = (owner & (row >= 2 * GROUP)).astype(F32).astype(BF16)
    return dot(stacked, first), dot(stacked, second)


def state_kernel(sel, x_hbm, g_hbm, w_hbm, r_hbm, ld_hbm, pay_ref, x_ref, g_ref, w_ref, r_ref, ld_ref, sems):
    rows, lanes = x_ref.shape
    width = w_ref.shape[1]
    here = pl.ds(pl.multiple_of(sel[0] * lanes, lanes), lanes)
    group = pl.ds(pl.multiple_of(sel[0] * GROUP, GROUP), GROUP)
    small = [
        pltpu.make_async_copy(src, dst, sems.at[k])
        for k, (src, dst) in enumerate(((ld_hbm.at[group, :], ld_ref), (w_hbm, w_ref), (r_hbm, r_ref)))
    ]
    large = []
    for b in range(2):
        at = pl.ds(b * Q, Q)
        large.append(pltpu.make_async_copy(x_hbm.at[at, here], x_ref.at[at, :], sems.at[3 + 2 * b]))
        large.append(pltpu.make_async_copy(g_hbm.at[at, here], g_ref.at[at, :], sems.at[4 + 2 * b]))
    for move in small + large:
        move.start()
    small[0].wait()
    decays = [spread_decays(running_of(ld_ref[:, b * Q : (b + 1) * Q]), lanes // GROUP) for b in range(2)]
    small[1].wait()
    small[2].wait()
    f_parts, g_parts, ends = [], [], []
    for b in range(2):
        at = slice(b * Q, (b + 1) * Q)
        decay_in, decay_out = decays[b]
        large[2 * b].wait()
        iw = (x_ref[at, :].astype(F32) * decay_out).astype(BF16)
        f_parts.append(dot(w_ref[at, :].astype(F32).T.astype(BF16), iw))
        large[2 * b + 1].wait()
        gw = (g_ref[at, :].astype(F32) * decay_in).astype(BF16)
        g_parts.append(dot(r_ref[at, :].astype(F32).T.astype(BF16), gw))
        ends.append(decay_in[Q - 1 : Q, :])
    pay_ref[0:width, :] = ends[1] * f_parts[0] + f_parts[1]
    pay_ref[width : 2 * width, :] = ends[0] * g_parts[1] + g_parts[0]
    pay_ref[2 * width : 2 * width + 8, :] = jnp.broadcast_to(ends[0] * ends[1], (8, lanes))


def params(limit=32):
    return pltpu.CompilerParams(vmem_limit_bytes=limit * 1024 * 1024)


def shape_of(shape, dtype=F32):
    return jax.ShapeDtypeStruct(shape, dtype)


def stored(shape, dtype=F32):
    return pltpu.HBM(shape, dtype)


def far_off(values):
    return pltpu.with_memory_space_constraint(values, pltpu.HBM)


def states(which, inputs, grad_out, write_proj, read_proj, log_decay, head_size):
    rows, width = write_proj.shape
    lanes = GROUP * head_size
    outs = [shape_of((2 * width + 8, lanes))]
    return pl.pallas_call(
        state_kernel,
        grid_spec=pltpu.PrefetchScalarGridSpec(
            num_scalar_prefetch=1,
            grid=(1,),
            in_specs=[pl.BlockSpec(memory_space=pltpu.HBM)] * 5,
            out_specs=[full(o) for o in outs],
            scratch_shapes=[
                pltpu.VMEM((rows, lanes), BF16),
                pltpu.VMEM((rows, lanes), BF16),
                pltpu.VMEM((rows, width), BF16),
                pltpu.VMEM((rows, width), BF16),
                pltpu.VMEM((GROUP, rows), F32),
                pltpu.SemaphoreType.DMA((7,)),
            ],
        ),
        out_shape=outs,
        compiler_params=params(),
        cost_estimate=FREE,
        name="states",
    )(which, *map(far_off, (inputs, grad_out, write_proj, read_proj, log_decay)))[0]


def chip_kernel(sel, mine_ref, got_ref, px_ref, py_ref):
    width = (mine_ref.shape[0] - 8) // 2
    lead = sel[2] == 0
    f_rows, b_rows, d_rows = slice(0, width), slice(width, 2 * width), slice(2 * width, 2 * width + 8)
    dec_mine, dec_got = mine_ref[d_rows, :], got_ref[d_rows, :]
    dec_first = jnp.where(lead, dec_mine, dec_got)[0:1]
    dec_second = jnp.where(lead, dec_got, dec_mine)[0:1]
    f_mine, f_got = mine_ref[f_rows, :], got_ref[f_rows, :]
    b_mine, b_got = mine_ref[b_rows, :], got_ref[b_rows, :]
    forward = dec_second * jnp.where(lead, f_mine, f_got) + jnp.where(lead, f_got, f_mine)
    backward = jnp.where(lead, b_mine, b_got) + dec_first * jnp.where(lead, b_got, b_mine)
    both = dec_mine * dec_got
    px_ref[f_rows, :] = jnp.where(sel[3] == 0, forward, backward)
    py_ref[f_rows, :] = jnp.where(sel[4] == 0, forward, backward)
    px_ref[width : width + 8, :] = both
    py_ref[width : width + 8, :] = both


def full(ref_or_shape):
    shape = ref_or_shape.shape
    return pl.BlockSpec(shape, lambda i, s: (0,) * len(shape))


ANYWHERE = pl.BlockSpec(memory_space=pl.ANY)


def call(kernel, name, sel, args, outs, in_specs=None, scratch=(), out_specs=None, after=()):
    skip, count = len(args), len(after)

    def body(s, *refs):
        kernel(s, *refs[:skip], *refs[skip + count :])

    return pl.pallas_call(
        body,
        grid_spec=pltpu.PrefetchScalarGridSpec(
            num_scalar_prefetch=1,
            grid=(1,),
            in_specs=(in_specs or [full(a) for a in args]) + [ANYWHERE] * count,
            out_specs=out_specs or [full(o) for o in outs],
            scratch_shapes=list(scratch),
        ),
        out_shape=list(outs),
        compiler_params=params(),
        cost_estimate=FREE,
        name=name,
    )(sel, *args, *after)


def carry_kernel(way, sel, *refs):
    *got_refs, mine_ref, got_ref, mine_dec, got_dec, own_ref, send_ref = refs
    width = mine_ref.shape[0]
    head, tail = slice(0, width), slice(width, width + 1)
    same = sel[3] == sel[4]
    rx = got_refs[0][head, :]
    if len(got_refs) == 1:
        entering = jnp.where(same, jnp.zeros_like(rx), rx)
    else:
        ry, rd = got_refs[1][head, :], got_refs[2][head, :]
        dx, dy, dd = (ref[tail, :] for ref in got_refs)
        entering = jnp.where(same, rx + dx * (ry + dy * rd), rd + dd * ry)
    first = sel[way] == sel[2]
    own_ref[...] = jnp.where(first, entering, got_dec[0:1, :] * entering + got_ref[...])
    send_ref[...] = jnp.where(first, mine_dec[0:1, :] * entering + mine_ref[...], entering)


def carry(way, sel, arrived, mine, got, name, after=()):
    width, lanes = arrived[0].shape[0] - 8, arrived[0].shape[1]
    part = pl.BlockSpec((width, lanes), lambda i, s: (s[way], 0))
    dec = pl.BlockSpec((8, lanes), lambda i, s: (2 * width // 8, 0))
    return call(
        functools.partial(carry_kernel, way),
        name,
        sel,
        [*arrived, mine, got, mine, got],
        [shape_of((width, lanes))] * 2,
        in_specs=[full(a) for a in arrived] + [part, part, dec, dec],
        after=after,
    )


def late_kernel(way, sel, wg_ref, car_ref, part_ref, tot_ref, acc_ref, out_ref):
    car = car_ref[...]
    onward = tot_ref[0:1, :] * car + part_ref[...]
    forward = sel[way] == 0
    for b in range(2):
        at = slice(b * Q, (b + 1) * Q)
        held = jnp.where(forward, onward if b else car, car if b else onward).astype(BF16)
        out_ref[at, :] = acc_ref[0, at, :] + dot_t(wg_ref[0, at, :], held)


def cut_kernel(way, sel, wg_ref, car_ref, part_ref, tot_ref, acc_ref, keep_ref, send_ref, total):
    late_kernel(way, sel, wg_ref, car_ref, part_ref, tot_ref, acc_ref, total)
    step = keep_ref.shape[0]
    odd = sel[5] % 2
    keep_ref[...] = total[pl.ds(pl.multiple_of(odd * step, step), step), :]
    send_ref[...] = total[pl.ds(pl.multiple_of((1 - odd) * step, step), step), :]


def late(way, sel, k, local_parts, carried, acc, cut, name):
    wg, part, tot = local_parts
    rows = wg.shape[1]
    width, lanes = carried.shape
    both = acc.shape[0] == 2
    outs = [shape_of((rows // 2, width))] * 2 if cut else [shape_of((rows, width))]
    return call(
        functools.partial(cut_kernel if cut else late_kernel, way),
        name,
        sel,
        [wg, carried, part, tot, acc],
        outs,
        in_specs=[
            pl.BlockSpec((1, rows, lanes), lambda i, s: (s[way], 0, s[6 + k])),
            full(carried),
            pl.BlockSpec((width, lanes), lambda i, s: (s[way], s[6 + k])),
            pl.BlockSpec((8, lanes), lambda i, s: (s[way], s[6 + k])),
            pl.BlockSpec((1, rows, width), lambda i, s: (s[way] if both else 0, 0, 0)),
        ],
        scratch=[pltpu.VMEM((rows, width), F32)] if cut else [],
    )


def decay_blocks(running):
    half = Q // 2
    columns = jnp.concatenate([running] * (128 // GROUP), axis=0).T
    keep_top = iota((half, Q), 0) <= iota((half, Q), 1)
    keep_low = iota((half, half), 0) <= iota((half, half), 1)

    def of(h):
        row, col = running[h : h + 1, :], columns[:, h : h + 1]
        top = jnp.exp(jnp.where(keep_top, row - col[0:half], -jnp.inf))
        low = jnp.exp(jnp.where(keep_low, row[:, half:] - col[half:], -jnp.inf))
        return top, low

    return of


def pair_products(x_pair, g_pair):
    half = Q // 2
    lane = iota(x_pair.shape, 1)
    none = jnp.zeros_like(x_pair)
    left = lane < x_pair.shape[1] // 2
    first, second = jnp.where(left, x_pair, none), jnp.where(left, none, x_pair)
    top = dot_t(jnp.concatenate([first[0:half], second[0:half]], axis=0), g_pair)
    low = dot_t(jnp.concatenate([first[half:], second[half:]], axis=0), g_pair[half:])
    return (top[0:half], low[0:half]), (top[half:], low[half:])


def scores_kernel(x_ref, g_ref, w_ref, r_ref, ld_ref, *rest):
    acc_ref, wg_ref, part_ref, tot_ref, gs_ref = rest[-5:]
    group = pl.program_id(1)
    size = x_ref.shape[1] // GROUP
    half = Q // 2
    running = running_of(ld_ref[...])
    decay_in, decay_out = spread_decays(running, size)
    iw = (x_ref[...].astype(F32) * decay_out).astype(BF16)
    gw = (g_ref[...].astype(F32) * decay_in).astype(BF16)
    wg_ref[0] = gw
    wg_ref[1] = iw
    tot_ref[...] = jnp.broadcast_to(decay_in[Q - 1 : Q, :], tot_ref.shape)

    @pl.when(pl.program_id(0) == 0)
    def _():
        part_ref[...] = dot(w_ref[...].astype(F32).T.astype(BF16), iw)

    @pl.when(pl.program_id(0) == 1)
    def _():
        part_ref[...] = dot(r_ref[...].astype(F32).T.astype(BF16), gw)

    decays = decay_blocks(running)
    gs_top = jnp.zeros((half, Q), F32)
    gs_low = jnp.zeros((half, half), F32)
    for pair in range(GROUP // 2):
        at = slice(pair * 2 * size, (pair + 1) * 2 * size)
        for k, (pairs_top, pairs_low) in enumerate(pair_products(x_ref[:, at], g_ref[:, at])):
            decay_top, decay_low = decays(2 * pair + k)
            gs_top = gs_top + decay_top * pairs_top
            gs_low = gs_low + decay_low * pairs_low

    @pl.when(group == 0)
    def _():
        gs_ref[0:half, :] = gs_top
        gs_ref[half:, 0:half] = jnp.zeros_like(gs_low)
        gs_ref[half:, half:] = gs_low

    @pl.when(group > 0)
    def _():
        gs_ref[0:half, :] += gs_top
        gs_ref[half:, half:] += gs_low

    @pl.when(group == pl.num_programs(1) - 1)
    def _():
        grad_scores = gs_ref[...]
        acc_ref[0] = dot(grad_scores.T.astype(BF16), w_ref[...])
        acc_ref[1] = dot(grad_scores.astype(BF16), r_ref[...])


def scores(inputs, grad_out, write_proj, read_proj, log_decay, head_size, after):
    rows, width = write_proj.shape
    heads = log_decay.shape[0]
    lanes = GROUP * head_size
    wide = pl.BlockSpec((Q, lanes), lambda b, j: (b, j))
    narrow = pl.BlockSpec((Q, width), lambda b, j: (b, 0))
    return pl.pallas_call(
        scores_kernel,
        grid=(rows // Q, heads // GROUP),
        in_specs=[wide, wide, narrow, narrow, pl.BlockSpec((GROUP, Q), lambda b, j: (j, b))] + [ANYWHERE] * len(after),
        out_specs=[
            pl.BlockSpec((2, Q, width), lambda b, j: (0, b, 0)),
            pl.BlockSpec((2, Q, lanes), lambda b, j: (0, b, j)),
            pl.BlockSpec((width, lanes), lambda b, j: (b, j)),
            pl.BlockSpec((8, lanes), lambda b, j: (b, j)),
        ],
        out_shape=[
            shape_of((2, rows, width)),
            stored((2, rows, heads * head_size), BF16),
            stored((2 * width, heads * head_size)),
            stored((16, heads * head_size)),
        ],
        scratch_shapes=[pltpu.VMEM((Q, Q), F32)],
        compiler_params=params(),
        cost_estimate=FREE,
        name="scores",
    )(inputs, grad_out, write_proj, read_proj, log_decay, *after)


def grads_kernel(scale, sel, x_ref, g_ref, gw_ref, w_ref, r_ref, ld_ref, part_ref, tot_ref, near_ref, far_ref, pay_ref, *rest):
    gi_ref, gd_ref = rest[-2:]
    lanes = x_ref.shape[1]
    width = w_ref.shape[1]
    size = lanes // GROUP
    half = Q // 2
    near_forward = sel[0] == 0
    f_car = jnp.where(near_forward, near_ref[...], far_ref[...])
    b_car = jnp.where(near_forward, far_ref[...], near_ref[...])
    f_next = tot_ref[0:1, :] * f_car + part_ref[0:width, :]
    b_next = tot_ref[8:9, :] * b_car + part_ref[width : 2 * width, :]
    state_in, grad_end = (f_car, f_next), (b_next, b_car)
    last = pay_ref[2 * width : 2 * width + 1, :] * f_car + pay_ref[0:width, :]
    after = (f_next, last)
    owner = iota((16, lanes), 0) == iota((16, lanes), 1) // size
    ones = owner.astype(F32).astype(BF16)
    onward = (iota((Q, Q), 0) >= iota((Q, Q), 1)).astype(F32).astype(BF16)
    left = iota((Q, 2 * size), 1) < size
    for b in range(2):
        at = slice(b * Q, (b + 1) * Q)
        running = running_of(ld_ref[:, at])
        decays = decay_blocks(running)
        decay_out = spread_decays(running, size)[1]
        products = dot_t(w_ref[at, :], r_ref[at, :])
        sums_top, sums_low, changes = [], [], None
        for pair in range(GROUP // 2):
            here = slice(pair * 2 * size, (pair + 1) * 2 * size)
            x_pair, g_pair = x_ref[at, here], g_ref[at, here]
            none = jnp.zeros_like(g_pair)
            top = low = None
            for k, (pairs_top, pairs_low) in enumerate(pair_products(x_pair, g_pair)):
                decay_top, decay_low = decays(2 * pair + k)
                weights_top = products[0:half] * decay_top
                weights_low = products[half:, half:] * decay_low
                sums_top.append(jnp.sum(weights_top * pairs_top, axis=0, keepdims=True))
                sums_low.append(jnp.sum(weights_low * pairs_low, axis=0, keepdims=True))
                g_own = jnp.where(left, g_pair, none) if k == 0 else jnp.where(left, none, g_pair)
                part_top = dot(weights_top.astype(BF16), g_own)
                part_low = dot(weights_low.astype(BF16), g_own[half:])
                top = part_top if top is None else top + part_top
                low = part_low if low is None else low + part_low
            out_inter = dot(r_ref[at, :], state_in[b][:, here].astype(BF16))
            grad_inter = dot(w_ref[at, :], grad_end[b][:, here].astype(BF16)) * decay_out[:, here]
            grad_full = jnp.concatenate([top, low], axis=0) + grad_inter
            gi_ref[at, here] = grad_full.astype(BF16)
            high, low = split_two(gw_ref[0, at, here].astype(F32) * out_inter - x_pair.astype(F32) * grad_full)
            change = dot_t(ones[:, here], high.astype(BF16)) + dot_t(ones[:, here], low.astype(BF16))
            changes = change if changes is None else changes + change
        early, late_half = jnp.concatenate(sums_top, axis=0), jnp.concatenate(sums_low, axis=0)
        within = changes[0:GROUP] + early + jnp.concatenate([jnp.zeros_like(late_half), late_half], axis=1)
        cross = jnp.sum(after[b] * grad_end[b], axis=0, keepdims=True)
        crossing = jnp.sum(jnp.where(owner[0:GROUP], cross, 0.0), axis=1, keepdims=True)
        gd_ref[:, at] = (times_ones(within, onward) + crossing) * scale


def grads(sel, k, data, local_parts, carried, scale, head_size, held=(), after=()):
    inputs, grad_out, write_proj, read_proj, log_decay = data
    wg, part, tot = local_parts
    rows, width = write_proj.shape
    heads = log_decay.shape[0]
    lanes = GROUP * head_size
    wide = pl.BlockSpec((rows, lanes), lambda i, s: (0, s[6 + k]))
    decays = pl.BlockSpec((GROUP, rows), lambda i, s: (s[6 + k], 0))
    args = [inputs, grad_out, wg, write_proj, read_proj, log_decay, part, tot, *carried]
    return pl.pallas_call(
        functools.partial(grads_kernel, scale),
        grid_spec=pltpu.PrefetchScalarGridSpec(
            num_scalar_prefetch=1,
            grid=(1,),
            in_specs=[
                wide,
                wide,
                pl.BlockSpec((1, rows, lanes), lambda i, s: (0, 0, s[6 + k])),
                full(write_proj),
                full(read_proj),
                decays,
                pl.BlockSpec((2 * width, lanes), lambda i, s: (0, s[6 + k])),
                pl.BlockSpec((16, lanes), lambda i, s: (0, s[6 + k])),
            ]
            + [full(a) for a in carried]
            + [ANYWHERE] * (len(held) + len(after)),
            out_specs=[wide, decays],
        ),
        out_shape=[stored((rows, heads * head_size), BF16), stored((heads, rows))],
        input_output_aliases={1 + len(args): 0, 2 + len(args): 1} if held else {},
        compiler_params=params(),
        cost_estimate=FREE,
        name="grads",
    )(sel, *args, *held, *after)


def join_kernel(sel, near_own, near_other, far_own, far_other, read_ref, write_ref, sems):
    step = near_own.shape[0]
    odd = sel[5] % 2

    def copies(near_ref, far_ref):
        moves = []
        for k, (part, out) in enumerate(
            ((near_own, near_ref), (near_other, near_ref), (far_own, far_ref), (far_other, far_ref))
        ):
            at = pl.multiple_of((odd if k % 2 == 0 else 1 - odd) * step, step)
            moves.append(pltpu.make_async_copy(part, out.at[pl.ds(at, step), :], sems.at[k]))
        for move in moves:
            move.start()
        for move in moves:
            move.wait()

    pl.when(sel[0] == 0)(lambda: copies(read_ref, write_ref))
    pl.when(sel[0] != 0)(lambda: copies(write_ref, read_ref))


def swap(values, axis, mask):
    count = lax.axis_size(axis)
    return lax.ppermute(values, axis, [(i, i ^ mask) for i in range(count)])


def scan_over(pay, width, reverse):
    count = lax.axis_size("seq")
    place = lax.axis_index("seq")
    ahead = count - 1 - place if reverse else place
    part = pay[width : 2 * width] if reverse else pay[0:width]
    dec = pay[2 * width : 2 * width + 1]

    def shifted(values, hop):
        route = [(i, i - hop) if reverse else (i, i + hop) for i in range(count)]
        return lax.ppermute(values, "seq", [(a, b) for a, b in route if 0 <= b < count])

    hop = 1
    while hop < count:
        got_part, got_dec = shifted(part, hop), shifted(dec, hop)
        use = ahead >= hop
        part = jnp.where(use, part + dec * got_part, part)
        dec = jnp.where(use, dec * got_dec, dec)
        hop *= 2
    return shifted(part, 1)


def tied(value, *others):
    return lax.optimization_barrier((value, *others))[0]


def local(inputs, grad_out, write_proj, read_proj, log_decay):
    head_count, rows = log_decay.shape
    head_size = inputs.shape[1] // head_count
    width = write_proj.shape[1]
    lanes = GROUP * head_size
    groups = head_count // GROUP
    seq_count, head_parts = lax.axis_size("seq"), lax.axis_size("head")
    scale = (head_size * rows * seq_count) ** (-0.5)
    place = lax.axis_index("seq").astype(jnp.int32)
    core, x, y = place % 2, (place // 2) % 2, (place // 4) % 2
    fast = seq_count == 8 and groups == 2 and head_parts == 4
    order = [core, 1 - core] if fast else [jnp.int32(k) for k in range(groups)]
    ways = [y, 1 - y] if fast else [jnp.int32(0), jnp.int32(1)]
    sel = jnp.stack([*ways, core, x, y, lax.axis_index("head").astype(jnp.int32), *order])
    data = (inputs, grad_out, write_proj, read_proj, log_decay)

    if fast:
        other = states(order[1][None], *data, head_size)
        got = swap(other, "seq", 1)
        mine = states(order[0][None], *data, head_size)
        px, py = call(chip_kernel, "chip", sel, (mine, got), [shape_of((width + 8, lanes))] * 2)
        rx, ry, rd = swap(px, "seq", 2), swap(py, "seq", 4), swap(py, "seq", 6)
        early, *parts = scores(*data, head_size, (px, py))
        near_own, send = carry(0, sel, [rx], mine, got, "carry_near", (parts[2],))
        near_got = swap(send, "seq", 1)
        (acc,) = late(0, sel, 0, parts, near_own, early, False, "late_near_mine")
        near_parts = late(0, sel, 1, parts, near_got, acc[None], True, "late_near_other")
        near_half = near_parts[0] + swap(near_parts[1], "head", 1)
        near_cross = swap(near_half, "head", 2)
        far_own, send = carry(1, sel, [rx, ry, rd], mine, got, "carry_far", (near_half,))
        far_got = swap(send, "seq", 1)
        (acc,) = late(1, sel, 0, parts, far_own, early, False, "late_far_mine")
        far_parts = late(1, sel, 1, parts, far_got, acc[None], True, "late_far_other")
        far_arrived = swap(far_parts[1], "head", 1)
        near_sum = near_half + near_cross
        near_rest = swap(near_sum, "head", 1)
        held = grads(sel, 0, data, parts, (near_own, far_own, mine), scale, head_size, (), (far_parts[1],))
        far_half = far_parts[0] + tied(far_arrived, *held)
        far_cross = swap(far_half, "head", 2)
        grad_inputs, grad_decay = grads(
            sel, 1, data, parts, (near_got, far_got, other), scale, head_size, held, (far_half,)
        )
        far_sum = far_half + tied(far_cross, grad_decay)
        far_rest = swap(far_sum, "head", 1)
        grad_read, grad_write = call(
            join_kernel,
            "join",
            sel,
            (near_sum, near_rest, far_sum, far_rest),
            [shape_of((rows, width))] * 2,
            in_specs=[ANYWHERE] * 4,
            out_specs=[ANYWHERE] * 2,
            scratch=[pltpu.SemaphoreType.DMA((4,))],
        )
        return grad_inputs, grad_write, grad_read, grad_decay

    pays = [states(k[None], *data, head_size) for k in order]
    early, *parts = scores(*data, head_size, ())
    carried = [[scan_over(pay, width, bool(way)) for pay in pays] for way in (0, 1)]
    totals = []
    for way in (0, 1):
        acc = early
        for k in range(groups):
            acc = late(way, sel, k, parts, carried[way][k], acc, False, "late")[0][None]
        totals.append(acc[0])
    held = ()
    for k in range(groups):
        held = grads(sel, k, data, parts, (carried[0][k], carried[1][k], pays[k]), scale, head_size, tuple(held))
    grad_inputs, grad_decay = held
    grad_read, grad_write = lax.psum(tuple(totals), "head")
    return grad_inputs, grad_write, grad_read, grad_decay


def solution(mesh):
    in_specs = (
        P("seq", "head"),
        P("seq", "head"),
        P("seq", None),
        P("seq", None),
        P("head", "seq"),
    )
    out_specs = (P("seq", "head"), P("seq", None), P("seq", None), P("head", "seq"))
    return jax.shard_map(local, mesh=mesh, in_specs=in_specs, out_specs=out_specs, check_vma=False)
```

time: 71.3 us -> 64.6 us (0.906)
  waiting for transfers between devices: 26.9 us -> 14.4 us
  Pallas kernels: 21.2 us -> 31.9 us
  local copies, waits for them, and re-layouts: 8.24 us -> 2.32 us
  starting transfers between devices: 13.9 us -> 14.8 us
    ppermute x11 -> x12, waiting for transfers between devices: 26.9 us -> 14.4 us  [swap(): return lax.ppermute(values, axis, [(i, i ^ mask) for i in range(count)])]
    pallas_call x7 -> x11, Pallas kernels: 17.8 us -> 25.4 us  [the longest x2 11.6 us: grads(): pl.pallas_call(functools.partial(grads_kernel, scale), grid_spec=pltpu.Pr...]
    unnamed x30 -> x18, local copies, waits for them, and re-layouts: 8.16 us -> 2.23 us
    pallas_call x2, Pallas kernels: 3.41 us -> 6.44 us  [states(): pl.pallas_call(state_kernel, grid_spec=pltpu.PrefetchScalarGridSpec(num_s...]
    ppermute x11 -> x12, starting transfers between devices: 13.9 us -> 14.8 us  [swap(): return lax.ppermute(values, axis, [(i, i ^ mask) for i in range(count)])]
  transfers between devices with their start and end apart: 11 -> 12, of which waited for: 7 -> 7; matrix products, arithmetic and copies ran while one was open for 0% -> 0% of each run, Pallas kernels for 21% -> 38%
where the time goes in v2:
time: 64.6 us; the launch traced here: 64.3 us
  Pallas kernels  31.9 us (49%)
  starting transfers between devices  14.8 us (23%)
  waiting for transfers between devices  14.4 us (22%)
  local copies, waits for them, and re-layouts  2.32 us (4%)
  between operations  0.85 us (1%)
    ppermute x12, starting transfers between devices, swap(): return lax.ppermute(values, axis, [(i, i ^ mask) for i in range(count)])  14.8 us
    ppermute x12, waiting for transfers between devices, swap(): return lax.ppermute(values, axis, [(i, i ^ mask) for i in range(count)])  14.4 us
    pallas_call x2, Pallas kernels, grads(): pl.pallas_call(functools.partial(grads_kernel, scale), grid_spec=pltpu.Pr...  11.6 us
    pallas_call x1, Pallas kernels, scores(): pl.pallas_call(scores_kernel, grid=(rows // Q, heads // GROUP), in_specs=...  7.05 us
    pallas_call x8, Pallas kernels, call(): pl.pallas_call(body, grid_spec=pltpu.PrefetchScalarGridSpec(num_scalar_pr...  6.81 us
    pallas_call x2, Pallas kernels, states(): pl.pallas_call(state_kernel, grid_spec=pltpu.PrefetchScalarGridSpec(num_s...  6.44 us
    unnamed x18, local copies, waits for them, and re-layouts  2.23 us
  transfers between devices with their start and end apart: 12, of which 7 were waited for; matrix products, arithmetic and copies ran while one was open for 0% of the time, Pallas kernels for 38%

profile of v2, /device:TPU:0, one launch (start us, length us, event | category | flops | bytes accessed | tf_op | source)
XLA Modules:
  0.0 64.3 jit_solution(18070132148754429274)
XLA Ops:
  0.6 3.5 %states.3.pay_ref = f32[264,512]{1,0:T(8,128)} custom-call(s32[1]{0:T(128)} %bitcast.5.sel, bf16[512,1024]{1,0:T(8,128)(2,1)} %x_ref.5, bf16[512,1024]{1,0:T(8,128)(2,1)} %g_ref.5, bf16[512,128]{1,0:T(8,128)(2,1)} %w_ref.5, bf16[512,128]{1,0:T(8,128)(2,1)} %r_ref.5, f32[16,512]{1,0:T(8,128)} %ld_ref.5), custom_call_target="tpu_custom_call" | custom-call | flops 1000 | bytes 1000 | tf_op jit(solution)/shard_map/states/pallas_call | solution.py:120
  4.3 0.5 collective-permute-start
  4.8 2.9 %states.2.refs_0_.refs_1_.refs_3_.refs_5_.pay_ref = f32[264,512]{1,0:T(8,128)S(1)} custom-call(s32[1]{0:T(128)} %bitcast.2.sel, bf16[512,1024]{1,0:T(8,128)(2,1)} %x_ref.5, bf16[512,1024]{1,0:T(8,128)(2,1)} %g_ref.5, bf16[512,128]{1,0:T(8,128)(2,1)} %w_ref.5, bf16[512,128]{1,0:T(8,128)(2,1)} %r_ref.5, f32[16,512]{1,0:T(8,128)} %ld_ref.5), custom_call_target="tpu_custom_call" | custom-call | flops 1000 | bytes 1000 | tf_op jit(solution)/shard_map/states/pallas_call | solution.py:120
  7.8 0.7 %chip.1 = (f32[136,512]{1,0:T(8,128)S(1)}, f32[136,512]{1,0:T(8,128)S(1)}) custom-call(s32[8]{0:T(128)S(1)} %stack.29.s.sel, f32[264,512]{1,0:T(8,128)S(1)} %states.2.refs_0_.refs_1_.refs_3_.refs_5_.pay_ref, f32[264,512]{1,0:T(8,128)S(1)} %collective-permute-done.refs_1_.refs_2_.refs_4_.refs_6_), custom_call_target="tpu_custom_call" | custom-call | flops 1000 | bytes 1000 | tf_op jit(solution)/shard_map/chip/pallas_call | solution.py:175
  8.5 2.6 %collective-permute-start.1 = (f32[136,512]{1,0:T(8,128)S(1)}, f32[136,512]{1,0:T(8,128)S(1)}, u32[]{:S(2)}, u32[]{:S(2)}) collective-permute-start(f32[136,512]{1,0:T(8,128)S(1)} %get-tuple-element.26.rest_0_), channel_id=1, source_target_pairs={{0,8},{4,12},{8,0},{12,4},{16,24},{20,28},{24,16},{28,20},{1,9},{5... | collective-permute-start | bytes 835592 | tf_op jit(solution)/shard_map/ppermute | solution.py:481
  11.1 7.0 %scores.1 = (f32[2,512,128]{2,1,0:T(8,128)S(1)}, bf16[2,512,1024]{2,1,0:T(8,128)(2,1)}, f32[256,1024]{1,0:T(8,128)}, f32[16,1024]{1,0:T(8,128)}) custom-call(bf16[512,1024]{1,0:T(8,128)(2,1)S(1)} %copy-done.2, bf16[512,1024]{1,0:T(8,128)(2,1)S(1)} %copy-done.3, bf16[512,128]{1,0:T(8,128)(2,1)S(1)} %copy-done.4, bf16[512,128]{1,0:T(8,128)(2,1)S(1)} %copy-done.5, ...), custom_call_target="tpu_custom_call" | custom-call | flops 1000 | bytes 1000 | tf_op jit(solution)/shard_map/scores/pallas_call | solution.py:345
  18.2 1.0 %copy-done.6 = f32[16,1024]{1,0:T(8,128)S(1)} copy-done((f32[16,1024]{1,0:T(8,128)S(1)}, f32[16,1024]{1,0:T(8,128)}, u32[]{:S(2)}) %copy-start.6) | copy-done | bytes 65560
  19.2 0.6 carry_near.1
  19.9 2.6 %collective-permute-start.4 = (f32[136,512]{1,0:T(8,128)S(1)}, f32[136,512]{1,0:T(8,128)S(1)}, u32[]{:S(2)}, u32[]{:S(2)}) collective-permute-start(f32[136,512]{1,0:T(8,128)S(1)} %get-tuple-element.27.rest_1_), channel_id=1, source_target_pairs={{0,24},{4,28},{8,16},{12,20},{16,8},{20,12},{24,0},{28,4},{1,25},{... | collective-permute-start | bytes 835592 | tf_op jit(solution)/shard_map/ppermute | solution.py:481
  22.5 0.5 collective-permute-start.3
  23.1 1.2 %copy-done.1 = f32[256,1024]{1,0:T(8,128)S(1)} copy-done((f32[256,1024]{1,0:T(8,128)S(1)}, f32[256,1024]{1,0:T(8,128)}, u32[]{:S(2)}) %copy-start.1) | copy-done | bytes 1048600
  24.3 0.9 %late_near_mine.1 = f32[512,128]{1,0:T(8,128)S(1)} custom-call(s32[8]{0:T(128)S(1)} %stack.29.s.sel, bf16[2,512,1024]{2,1,0:T(8,128)(2,1)S(1)} %copy-done, f32[128,512]{1,0:T(8,128)S(1)} %get-tuple-element.32.refs_1_.near_ref, f32[256,1024]{1,0:T(8,128)S(1)} %copy-done.1, f32[16,1024]{1,0:T(8,128)S(1)} %copy-done.7, f32[2,512,128]{2,1,0:T(8,128)S(1)} %get-tuple-element.33.refs_4_), custom_call_target="tpu_custom_call" | custom-call | flops 1000 | bytes 1000 | tf_op jit(solution)/shard_map/late_near_mine/pallas_call | solution.py:175
  25.2 0.9 %late_near_other.1 = (f32[256,128]{1,0:T(8,128)S(1)}, f32[256,128]{1,0:T(8,128)S(1)}) custom-call(s32[8]{0:T(128)S(1)} %stack.29.s.sel, bf16[2,512,1024]{2,1,0:T(8,128)(2,1)S(1)} %copy-done, f32[128,512]{1,0:T(8,128)S(1)} %collective-permute-done.2.refs_1_.near_ref, f32[256,1024]{1,0:T(8,128)S(1)} %copy-done.1, f32[16,1024]{1,0:T(8,128)S(1)} %copy-done.7, ...), custom_call_target="tpu_custom_call" | custom-call | flops 1000 | bytes 1000 | tf_op jit(solution)/shard_map/late_near_other/pallas_call | solution.py:175
  26.1 1.6 %collective-permute-start.5 = (f32[256,128]{1,0:T(8,128)S(1)}, f32[256,128]{1,0:T(8,128)S(1)}, u32[]{:S(2)}, u32[]{:S(2)}) collective-permute-start(f32[256,128]{1,0:T(8,128)S(1)} %get-tuple-element.35), channel_id=1, source_target_pairs={{0,1},{1,0},{2,3},{3,2},{4,5},{5,4},{6,7},{7,6},{8,9},{9,8},{10,11... | collective-permute-start | bytes 393224 | tf_op jit(solution)/shard_map/ppermute | solution.py:481
  27.7 3.7 %collective-permute-done.5 = f32[256,128]{1,0:T(8,128)S(1)} collective-permute-done((f32[256,128]{1,0:T(8,128)S(1)}, f32[256,128]{1,0:T(8,128)S(1)}, u32[]{:S(2)}, u32[]{:S(2)}) %collective-permute-start.5) | collective-permute-done | bytes 131104 | tf_op jit(solution)/shard_map/ppermute | solution.py:481
  31.4 4.4 %collective-permute-done.3.refs_1_ = f32[136,512]{1,0:T(8,128)S(1)} collective-permute-done((f32[136,512]{1,0:T(8,128)S(1)}, f32[136,512]{1,0:T(8,128)S(1)}, u32[]{:S(2)}, u32[]{:S(2)}) %collective-permute-start.3) | collective-permute-done | bytes 278560 | tf_op jit(solution)/shard_map/ppermute | solution.py:481
  35.9 0.7 %carry_far.1 = (f32[128,512]{1,0:T(8,128)S(1)}, f32[128,512]{1,0:T(8,128)S(1)}) custom-call(s32[8]{0:T(128)S(1)} %stack.29.s.sel, f32[136,512]{1,0:T(8,128)S(1)} %collective-permute-done.1.refs_0_, f32[136,512]{1,0:T(8,128)S(1)} %collective-permute-done.3.refs_1_, f32[136,512]{1,0:T(8,128)S(1)} %collective-permute-done.4.refs_2_, ...), custom_call_target="tpu_custom_call" | custom-call | flops 1000 | bytes 1000 | tf_op jit(solution)/shard_map/carry_far/pallas_call | solution.py:175
  36.5 0.1 collective-permute-start.6
  36.6 0.9 %late_far_mine.1 = f32[512,128]{1,0:T(8,128)S(1)} custom-call(s32[8]{0:T(128)S(1)} %stack.29.s.sel, bf16[2,512,1024]{2,1,0:T(8,128)(2,1)S(1)} %copy-done, f32[128,512]{1,0:T(8,128)S(1)} %get-tuple-element.37.refs_1_.far_ref, f32[256,1024]{1,0:T(8,128)S(1)} %copy-done.1, f32[16,1024]{1,0:T(8,128)S(1)} %copy-done.7, f32[2,512,128]{2,1,0:T(8,128)S(1)} %get-tuple-element.33.refs_4_), custom_call_target="tpu_custom_call" | custom-call | flops 1000 | bytes 1000 | tf_op jit(solution)/shard_map/late_far_mine/pallas_call | solution.py:175
  37.5 0.6 collective-permute-done.6.refs_1_.far_ref
  38.1 0.9 %late_far_other.1 = (f32[256,128]{1,0:T(8,128)S(1)}, f32[256,128]{1,0:T(8,128)S(1)}) custom-call(s32[8]{0:T(128)S(1)} %stack.29.s.sel, bf16[2,512,1024]{2,1,0:T(8,128)(2,1)S(1)} %copy-done, f32[128,512]{1,0:T(8,128)S(1)} %collective-permute-done.6.refs_1_.far_ref, f32[256,1024]{1,0:T(8,128)S(1)} %copy-done.1, f32[16,1024]{1,0:T(8,128)S(1)} %copy-done.7, ...), custom_call_target="tpu_custom_call" | custom-call | flops 1000 | bytes 1000 | tf_op jit(solution)/shard_map/late_far_other/pallas_call | solution.py:175
  39.0 1.9 %collective-permute-start.7 = (f32[256,128]{1,0:T(8,128)S(1)}, f32[256,128]{1,0:T(8,128)S(1)}, u32[]{:S(2)}, u32[]{:S(2)}) collective-permute-start(f32[256,128]{1,0:T(8,128)S(1)} %get-tuple-element.38.rest_0_), channel_id=1, source_target_pairs={{0,1},{1,0},{2,3},{3,2},{4,5},{5,4},{6,7},{7,6},{8,9},{9,8},{10,11... | collective-permute-start | bytes 393224 | tf_op jit(solution)/shard_map/ppermute | solution.py:481
  41.0 2.6 %collective-permute-start.8 = (f32[256,128]{1,0:T(8,128)S(1)}, f32[256,128]{1,0:T(8,128)S(1)}, u32[]{:S(2)}, u32[]{:S(2)}) collective-permute-start(f32[256,128]{1,0:T(8,128)S(1)} %add.27.refs_7_), channel_id=1, source_target_pairs={{0,2},{1,3},{2,0},{3,1},{4,6},{5,7},{6,4},{7,5},{8,10},{9,11},{10,... | collective-permute-start | bytes 393224 | tf_op jit(solution)/shard_map/ppermute | solution.py:481
  43.6 5.2 %grads.2 = (bf16[512,1024]{1,0:T(8,128)(2,1)}, f32[16,512]{1,0:T(8,128)}) custom-call(s32[8]{0:T(128)S(1)} %stack.29.s.sel, bf16[512,1024]{1,0:T(8,128)(2,1)S(1)} %copy-done.2, bf16[512,1024]{1,0:T(8,128)(2,1)S(1)} %copy-done.3, bf16[2,512,1024]{2,1,0:T(8,128)(2,1)S(1)} %copy-done, bf16[512,128]{1,0:T(8,128)(2,1)S(1)} %copy-done.4, ...), custom_call_target="tpu_custom_call" | custom-call | flops 1000 | bytes 1000 | tf_op jit(solution)/shard_map/grads/pallas_call | solution.py:432
  48.8 0.4 collective-permute-start.10
  49.2 0.8 %collective-permute-done.8 = f32[256,128]{1,0:T(8,128)S(1)} collective-permute-done((f32[256,128]{1,0:T(8,128)S(1)}, f32[256,128]{1,0:T(8,128)S(1)}, u32[]{:S(2)}, u32[]{:S(2)}) %collective-permute-start.8) | collective-permute-done | bytes 131104 | tf_op jit(solution)/shard_map/ppermute | solution.py:481
  50.0 0.8 %collective-permute-start.9 = (f32[256,128]{1,0:T(8,128)S(1)}, f32[256,128]{1,0:T(8,128)S(1)}, u32[]{:S(2)}, u32[]{:S(2)}) collective-permute-start(f32[256,128]{1,0:T(8,128)S(1)} %add.29.refs_0_), channel_id=1, source_target_pairs={{0,1},{1,0},{2,3},{3,2},{4,5},{5,4},{6,7},{7,6},{8,9},{9,8},{10,11... | collective-permute-start | bytes 393224 | tf_op jit(solution)/shard_map/ppermute | solution.py:481
  50.8 6.4 %grads.3 = (bf16[512,1024]{1,0:T(8,128)(2,1)}, f32[16,512]{1,0:T(8,128)}) custom-call(s32[8]{0:T(128)S(1)} %stack.29.s.sel, bf16[512,1024]{1,0:T(8,128)(2,1)S(1)} %copy-done.2, bf16[512,1024]{1,0:T(8,128)(2,1)S(1)} %copy-done.3, bf16[2,512,1024]{2,1,0:T(8,128)(2,1)S(1)} %copy-done, ...), custom_call_target="tpu_custom_call", output_to_operand_aliasing={{0}: (12, {}), {1}: (13, {})} | custom-call | flops 1000 | bytes 1000 | tf_op jit(solution)/shard_map/grads/pallas_call | solution.py:432
  57.2 0.3 collective-permute-done.10
  57.6 1.0 %collective-permute-start.11 = (f32[256,128]{1,0:T(8,128)S(1)}, f32[256,128]{1,0:T(8,128)S(1)}, u32[]{:S(2)}, u32[]{:S(2)}) collective-permute-start(f32[256,128]{1,0:T(8,128)S(1)} %add.30.refs_2_), channel_id=1, source_target_pairs={{0,1},{1,0},{2,3},{3,2},{4,5},{5,4},{6,7},{7,6},{8,9},{9,8},{10,11... | collective-permute-start | bytes 393224 | tf_op jit(solution)/shard_map/ppermute | solution.py:481
  58.5 4.4 %collective-permute-done.11.refs_3_ = f32[256,128]{1,0:T(8,128)S(1)} collective-permute-done((f32[256,128]{1,0:T(8,128)S(1)}, f32[256,128]{1,0:T(8,128)S(1)}, u32[]{:S(2)}, u32[]{:S(2)}) %collective-permute-start.11) | collective-permute-done | bytes 131104 | tf_op jit(solution)/shard_map/ppermute | solution.py:481
  63.0 1.4 %join.1 = (f32[512,128]{1,0:T(8,128)}, f32[512,128]{1,0:T(8,128)}) custom-call(s32[8]{0:T(128)S(1)} %stack.29.s.sel, f32[256,128]{1,0:T(8,128)S(1)} %add.29.refs_0_, f32[256,128]{1,0:T(8,128)S(1)} %collective-permute-done.9.refs_1_, f32[256,128]{1,0:T(8,128)S(1)} %add.30.refs_2_, f32[256,128]{1,0:T(8,128)S(1)} %collective-permute-done.11.refs_3_), custom_call_target="tpu_custom_call" | custom-call | flops 1000 | bytes 1000 | tf_op jit(solution)/shard_map/join/pallas_call | solution.py:175
  (28 shorter events, 0.4 us)
Async XLA Ops:
  4.2 6.9 %copy-start.2 = (bf16[512,1024]{1,0:T(8,128)(2,1)S(1)}, bf16[512,1024]{1,0:T(8,128)(2,1)}, u32[]{:S(2)}) copy-start(bf16[512,1024]{1,0:T(8,128)(2,1)} %x_ref.5) | copy-start | bytes 3145732
  4.2 6.8 %copy-start.3 = (bf16[512,1024]{1,0:T(8,128)(2,1)S(1)}, bf16[512,1024]{1,0:T(8,128)(2,1)}, u32[]{:S(2)}) copy-start(bf16[512,1024]{1,0:T(8,128)(2,1)} %g_ref.5) | copy-start | bytes 3145732
  4.2 6.8 %copy-start.4 = (bf16[512,128]{1,0:T(8,128)(2,1)S(1)}, bf16[512,128]{1,0:T(8,128)(2,1)}, u32[]{:S(2)}) copy-start(bf16[512,128]{1,0:T(8,128)(2,1)} %w_ref.5) | copy-start | bytes 393220
  4.2 6.8 %copy-start.5 = (bf16[512,128]{1,0:T(8,128)(2,1)S(1)}, bf16[512,128]{1,0:T(8,128)(2,1)}, u32[]{:S(2)}) copy-start(bf16[512,128]{1,0:T(8,128)(2,1)} %r_ref.5) | copy-start | bytes 393220
  4.2 6.8 %copy-start.8 = (f32[16,512]{1,0:T(8,128)S(1)}, f32[16,512]{1,0:T(8,128)}, u32[]{:S(2)}) copy-start(f32[16,512]{1,0:T(8,128)} %ld_ref.5) | copy-start | bytes 98308
  4.3 3.6 %collective-permute-start = (f32[264,512]{1,0:T(8,128)}, f32[264,512]{1,0:T(8,128)S(1)}, u32[]{:S(2)}, u32[]{:S(2)}) collective-permute-start(f32[264,512]{1,0:T(8,128)} %states.3.pay_ref), channel_id=1, source_target_pairs={{0,4},{4,0},{8,12},{12,8},{16,20},{20,16},{24,28},{28,24},{1,5},{5... | collective-permute-start | bytes 1622024 | tf_op jit(solution)/shard_map/ppermute | solution.py:481
  8.5 9.7 %collective-permute-start.1 = (f32[136,512]{1,0:T(8,128)S(1)}, f32[136,512]{1,0:T(8,128)S(1)}, u32[]{:S(2)}, u32[]{:S(2)}) collective-permute-start(f32[136,512]{1,0:T(8,128)S(1)} %get-tuple-element.26.rest_0_), channel_id=1, source_target_pairs={{0,8},{4,12},{8,0},{12,4},{16,24},{20,28},{24,16},{28,20},{1,9},{5... | collective-permute-start | bytes 835592 | tf_op jit(solution)/shard_map/ppermute | solution.py:481
  18.1 4.9 %copy-start = (bf16[2,512,1024]{2,1,0:T(8,128)(2,1)S(1)}, bf16[2,512,1024]{2,1,0:T(8,128)(2,1)}, u32[]{:S(2)}) copy-start(bf16[2,512,1024]{2,1,0:T(8,128)(2,1)} %get-tuple-element.28.refs_0_.gw_ref) | copy-start | bytes 6291460
  18.2 1.0 %copy-start.6 = (f32[16,1024]{1,0:T(8,128)S(1)}, f32[16,1024]{1,0:T(8,128)}, u32[]{:S(2)}) copy-start(f32[16,1024]{1,0:T(8,128)} %get-tuple-element.30.refs_5_.refs_3_.tot_ref) | copy-start | bytes 196612
  19.2 3.9 %copy-start.7 = (f32[16,1024]{1,0:T(8,128)S(1)}, f32[16,1024]{1,0:T(8,128)}, u32[]{:S(2)}) copy-start(f32[16,1024]{1,0:T(8,128)} %get-tuple-element.30.refs_5_.refs_3_.tot_ref) | copy-start | bytes 196612
  19.8 5.3 %collective-permute-start.2 = (f32[128,512]{1,0:T(8,128)S(1)}, f32[128,512]{1,0:T(8,128)S(1)}, u32[]{:S(2)}, u32[]{:S(2)}) collective-permute-start(f32[128,512]{1,0:T(8,128)S(1)} %get-tuple-element.31), channel_id=1, source_target_pairs={{0,4},{4,0},{8,12},{12,8},{16,20},{20,16},{24,28},{28,24},{1,5},{5... | collective-permute-start | bytes 786440 | tf_op jit(solution)/shard_map/ppermute | solution.py:481
  19.9 11.5 %collective-permute-start.4 = (f32[136,512]{1,0:T(8,128)S(1)}, f32[136,512]{1,0:T(8,128)S(1)}, u32[]{:S(2)}, u32[]{:S(2)}) collective-permute-start(f32[136,512]{1,0:T(8,128)S(1)} %get-tuple-element.27.rest_1_), channel_id=1, source_target_pairs={{0,24},{4,28},{8,16},{12,20},{16,8},{20,12},{24,0},{28,4},{1,25},{... | collective-permute-start | bytes 835592 | tf_op jit(solution)/shard_map/ppermute | solution.py:481
  22.5 13.3 %collective-permute-start.3 = (f32[136,512]{1,0:T(8,128)S(1)}, f32[136,512]{1,0:T(8,128)S(1)}, u32[]{:S(2)}, u32[]{:S(2)}) collective-permute-start(f32[136,512]{1,0:T(8,128)S(1)} %get-tuple-element.27.rest_1_), channel_id=1, source_target_pairs={{0,16},{4,20},{8,24},{12,28},{16,0},{20,4},{24,8},{28,12},{1,17},{... | collective-permute-start | bytes 835592 | tf_op jit(solution)/shard_map/ppermute | solution.py:481
  23.1 1.2 %copy-start.1 = (f32[256,1024]{1,0:T(8,128)S(1)}, f32[256,1024]{1,0:T(8,128)}, u32[]{:S(2)}) copy-start(f32[256,1024]{1,0:T(8,128)} %get-tuple-element.29.refs_2_.part_ref) | copy-start | bytes 3145732
  26.1 5.4 %collective-permute-start.5 = (f32[256,128]{1,0:T(8,128)S(1)}, f32[256,128]{1,0:T(8,128)S(1)}, u32[]{:S(2)}, u32[]{:S(2)}) collective-permute-start(f32[256,128]{1,0:T(8,128)S(1)} %get-tuple-element.35), channel_id=1, source_target_pairs={{0,1},{1,0},{2,3},{3,2},{4,5},{5,4},{6,7},{7,6},{8,9},{9,8},{10,11... | collective-permute-start | bytes 393224 | tf_op jit(solution)/shard_map/ppermute | solution.py:481
  36.5 1.6 %collective-permute-start.6 = (f32[128,512]{1,0:T(8,128)S(1)}, f32[128,512]{1,0:T(8,128)S(1)}, u32[]{:S(2)}, u32[]{:S(2)}) collective-permute-start(f32[128,512]{1,0:T(8,128)S(1)} %get-tuple-element.36), channel_id=1, source_target_pairs={{0,4},{4,0},{8,12},{12,8},{16,20},{20,16},{24,28},{28,24},{1,5},{5... | collective-permute-start | bytes 786440 | tf_op jit(solution)/shard_map/ppermute | solution.py:481
  39.0 9.7 %collective-permute-start.7 = (f32[256,128]{1,0:T(8,128)S(1)}, f32[256,128]{1,0:T(8,128)S(1)}, u32[]{:S(2)}, u32[]{:S(2)}) collective-permute-start(f32[256,128]{1,0:T(8,128)S(1)} %get-tuple-element.38.rest_0_), channel_id=1, source_target_pairs={{0,1},{1,0},{2,3},{3,2},{4,5},{5,4},{6,7},{7,6},{8,9},{9,8},{10,11... | collective-permute-start | bytes 393224 | tf_op jit(solution)/shard_map/ppermute | solution.py:481
  41.0 9.0 %collective-permute-start.8 = (f32[256,128]{1,0:T(8,128)S(1)}, f32[256,128]{1,0:T(8,128)S(1)}, u32[]{:S(2)}, u32[]{:S(2)}) collective-permute-start(f32[256,128]{1,0:T(8,128)S(1)} %add.27.refs_7_), channel_id=1, source_target_pairs={{0,2},{1,3},{2,0},{3,1},{4,6},{5,7},{6,4},{7,5},{8,10},{9,11},{10,... | collective-permute-start | bytes 393224 | tf_op jit(solution)/shard_map/ppermute | solution.py:481
  48.8 8.8 %collective-permute-start.10 = (f32[256,128]{1,0:T(8,128)S(1)}, f32[256,128]{1,0:T(8,128)S(1)}, u32[]{:S(2)}, u32[]{:S(2)}) collective-permute-start(f32[256,128]{1,0:T(8,128)S(1)} %add.28.rest_2_), channel_id=1, source_target_pairs={{0,2},{1,3},{2,0},{3,1},{4,6},{5,7},{6,4},{7,5},{8,10},{9,11},{10,... | collective-permute-start | bytes 393224 | tf_op jit(solution)/shard_map/ppermute | solution.py:481
  50.0 8.6 %collective-permute-start.9 = (f32[256,128]{1,0:T(8,128)S(1)}, f32[256,128]{1,0:T(8,128)S(1)}, u32[]{:S(2)}, u32[]{:S(2)}) collective-permute-start(f32[256,128]{1,0:T(8,128)S(1)} %add.29.refs_0_), channel_id=1, source_target_pairs={{0,1},{1,0},{2,3},{3,2},{4,5},{5,4},{6,7},{7,6},{8,9},{9,8},{10,11... | collective-permute-start | bytes 393224 | tf_op jit(solution)/shard_map/ppermute | solution.py:481
  57.6 5.4 %collective-permute-start.11 = (f32[256,128]{1,0:T(8,128)S(1)}, f32[256,128]{1,0:T(8,128)S(1)}, u32[]{:S(2)}, u32[]{:S(2)}) collective-permute-start(f32[256,128]{1,0:T(8,128)S(1)} %add.30.refs_2_), channel_id=1, source_target_pairs={{0,1},{1,0},{2,3},{3,2},{4,5},{5,4},{6,7},{7,6},{8,9},{9,8},{10,11... | collective-permute-start | bytes 393224 | tf_op jit(solution)/shard_map/ppermute | solution.py:481

commit v3 on v2

--- a/solution.py
+++ b/solution.py
@@ -11,6 +11,7 @@
 GROUP = 8
 F32 = jnp.float32
 BF16 = jnp.bfloat16
+ANYWHERE = pl.BlockSpec(memory_space=pl.ANY)
 FREE = pl.CostEstimate(flops=1000, bytes_accessed=1000, transcendentals=0)
 
 
@@ -61,7 +62,8 @@
     return dot(stacked, first), dot(stacked, second)
 
 
-def state_kernel(sel, x_hbm, g_hbm, w_hbm, r_hbm, ld_hbm, pay_ref, x_ref, g_ref, w_ref, r_ref, ld_ref, sems):
+def state_kernel(sel, x_hbm, g_hbm, w_hbm, r_hbm, ld_hbm, *rest):
+    outs, (x_ref, g_ref, w_ref, r_ref, ld_ref, pay_ref, wg_ref, part_ref, tot_ref, sems) = rest[:4], rest[4:]
     rows, lanes = x_ref.shape
     width = w_ref.shape[1]
     here = pl.ds(pl.multiple_of(sel[0] * lanes, lanes), lanes)
@@ -77,24 +79,44 @@
         large.append(pltpu.make_async_copy(g_hbm.at[at, here], g_ref.at[at, :], sems.at[4 + 2 * b]))
     for move in small + large:
         move.start()
+    leaving = []
+
+    def leave(src, dst):
+        leaving.append(pltpu.make_async_copy(src, dst, sems.at[7 + len(leaving)]))
+        leaving[-1].start()
+
+    pay_out, wg_out, part_out, tot_out = outs
     small[0].wait()
     decays = [spread_decays(running_of(ld_ref[:, b * Q : (b + 1) * Q]), lanes // GROUP) for b in range(2)]
+    ends = [decay_in[Q - 1 : Q, :] for decay_in, _ in decays]
+    tot_ref[0:8, :] = jnp.broadcast_to(ends[0], (8, lanes))
+    tot_ref[8:16, :] = jnp.broadcast_to(ends[1], (8, lanes))
+    leave(tot_ref, tot_out)
     small[1].wait()
     small[2].wait()
-    f_parts, g_parts, ends = [], [], []
+    f_parts, g_parts = [], []
     for b in range(2):
         at = slice(b * Q, (b + 1) * Q)
         decay_in, decay_out = decays[b]
         large[2 * b].wait()
         iw = (x_ref[at, :].astype(F32) * decay_out).astype(BF16)
+        wg_ref[1, at, :] = iw
+        leave(wg_ref.at[1, pl.ds(b * Q, Q), :], wg_out.at[1, pl.ds(b * Q, Q), :])
         f_parts.append(dot(w_ref[at, :].astype(F32).T.astype(BF16), iw))
         large[2 * b + 1].wait()
         gw = (g_ref[at, :].astype(F32) * decay_in).astype(BF16)
+        wg_ref[0, at, :] = gw
+        leave(wg_ref.at[0, pl.ds(b * Q, Q), :], wg_out.at[0, pl.ds(b * Q, Q), :])
         g_parts.append(dot(r_ref[at, :].astype(F32).T.astype(BF16), gw))
-        ends.append(decay_in[Q - 1 : Q, :])
     pay_ref[0:width, :] = ends[1] * f_parts[0] + f_parts[1]
     pay_ref[width : 2 * width, :] = ends[0] * g_parts[1] + g_parts[0]
     pay_ref[2 * width : 2 * width + 8, :] = jnp.broadcast_to(ends[0] * ends[1], (8, lanes))
+    leave(pay_ref, pay_out)
+    part_ref[0:width, :] = f_parts[0]
+    part_ref[width : 2 * width, :] = g_parts[1]
+    leave(part_ref, part_out)
+    for move in leaving:
+        move.wait()
 
 
 def params(limit=32):
@@ -116,31 +138,32 @@
 def states(which, inputs, grad_out, write_proj, read_proj, log_decay, head_size):
     rows, width = write_proj.shape
     lanes = GROUP * head_size
-    outs = [shape_of((2 * width + 8, lanes))]
+    shapes = [((2 * width + 8, lanes), F32), ((2, rows, lanes), BF16), ((2 * width, lanes), F32), ((16, lanes), F32)]
     return pl.pallas_call(
         state_kernel,
         grid_spec=pltpu.PrefetchScalarGridSpec(
             num_scalar_prefetch=1,
             grid=(1,),
             in_specs=[pl.BlockSpec(memory_space=pltpu.HBM)] * 5,
-            out_specs=[full(o) for o in outs],
+            out_specs=[ANYWHERE] * 4,
             scratch_shapes=[
                 pltpu.VMEM((rows, lanes), BF16),
                 pltpu.VMEM((rows, lanes), BF16),
                 pltpu.VMEM((rows, width), BF16),
                 pltpu.VMEM((rows, width), BF16),
                 pltpu.VMEM((GROUP, rows), F32),
-                pltpu.SemaphoreType.DMA((7,)),
+                *[pltpu.VMEM(*a) for a in shapes],
+                pltpu.SemaphoreType.DMA((14,)),
             ],
         ),
-        out_shape=outs,
+        out_shape=[shape_of(*shapes[0]), *[stored(*a) for a in shapes[1:]]],
         compiler_params=params(),
         cost_estimate=FREE,
         name="states",
-    )(which, *map(far_off, (inputs, grad_out, write_proj, read_proj, log_decay)))[0]
-
-
-def chip_kernel(sel, mine_ref, got_ref, px_ref, py_ref):
+    )(which, *map(far_off, (inputs, grad_out, write_proj, read_proj, log_decay)))
+
+
+def chip_kernel(sel, mine_ref, got_ref, first_ref, second_ref):
     width = (mine_ref.shape[0] - 8) // 2
     lead = sel[2] == 0
     f_rows, b_rows, d_rows = slice(0, width), slice(width, 2 * width), slice(2 * width, 2 * width + 8)
@@ -151,19 +174,15 @@
     b_mine, b_got = mine_ref[b_rows, :], got_ref[b_rows, :]
     forward = dec_second * jnp.where(lead, f_mine, f_got) + jnp.where(lead, f_got, f_mine)
     backward = jnp.where(lead, b_mine, b_got) + dec_first * jnp.where(lead, b_got, b_mine)
-    both = dec_mine * dec_got
-    px_ref[f_rows, :] = jnp.where(sel[3] == 0, forward, backward)
-    py_ref[f_rows, :] = jnp.where(sel[4] == 0, forward, backward)
-    px_ref[width : width + 8, :] = both
-    py_ref[width : width + 8, :] = both
+    low = sel[4] == 0
+    first_ref[f_rows, :] = jnp.where(low, forward, backward)
+    first_ref[width : width + 8, :] = dec_mine * dec_got
+    second_ref[...] = jnp.where(low, backward, forward)
 
 
 def full(ref_or_shape):
     shape = ref_or_shape.shape
     return pl.BlockSpec(shape, lambda i, s: (0,) * len(shape))
-
-
-ANYWHERE = pl.BlockSpec(memory_space=pl.ANY)
 
 
 def call(kernel, name, sel, args, outs, in_specs=None, scratch=(), out_specs=None, after=()):
@@ -188,33 +207,37 @@
     )(sel, *args, *after)
 
 
-def carry_kernel(way, sel, *refs):
-    *got_refs, mine_ref, got_ref, mine_dec, got_dec, own_ref, send_ref = refs
-    width = mine_ref.shape[0]
-    head, tail = slice(0, width), slice(width, width + 1)
-    same = sel[3] == sel[4]
-    rx = got_refs[0][head, :]
-    if len(got_refs) == 1:
-        entering = jnp.where(same, jnp.zeros_like(rx), rx)
-    else:
-        ry, rd = got_refs[1][head, :], got_refs[2][head, :]
-        dx, dy, dd = (ref[tail, :] for ref in got_refs)
-        entering = jnp.where(same, rx + dx * (ry + dy * rd), rd + dd * ry)
+def leave_states(way, sel, entering, mine_ref, got_ref, mine_dec, got_dec, own_ref, send_ref):
     first = sel[way] == sel[2]
     own_ref[...] = jnp.where(first, entering, got_dec[0:1, :] * entering + got_ref[...])
     send_ref[...] = jnp.where(first, mine_dec[0:1, :] * entering + mine_ref[...], entering)
 
 
-def carry(way, sel, arrived, mine, got, name, after=()):
-    width, lanes = arrived[0].shape[0] - 8, arrived[0].shape[1]
+def near_kernel(sel, rx_ref, px_ref, *refs):
+    width = rx_ref.shape[0] - 8
+    head, tail = slice(0, width), slice(width, width + 1)
+    same = sel[3] == sel[4]
+    rx, px = rx_ref[head, :], px_ref[head, :]
+    leave_states(0, sel, jnp.where(same, jnp.zeros_like(rx), rx), *refs[:-1])
+    refs[-1][...] = jnp.where(same, rx_ref[tail, :] * px + rx, px_ref[tail, :] * rx + px)
+
+
+def far_kernel(sel, rx_ref, sx_ref, ry_ref, *refs):
+    width = sx_ref.shape[0]
+    ry = ry_ref[...]
+    leave_states(1, sel, jnp.where(sel[3] == sel[4], sx_ref[...] + rx_ref[width : width + 1, :] * ry, ry), *refs)
+
+
+def carry(way, sel, arrived, mine, got, after=()):
+    width, lanes = mine.shape[0] // 2 - 4, mine.shape[1]
     part = pl.BlockSpec((width, lanes), lambda i, s: (s[way], 0))
     dec = pl.BlockSpec((8, lanes), lambda i, s: (2 * width // 8, 0))
     return call(
-        functools.partial(carry_kernel, way),
-        name,
+        (near_kernel, far_kernel)[way],
+        ("carry_near", "carry_far")[way],
         sel,
         [*arrived, mine, got, mine, got],
-        [shape_of((width, lanes))] * 2,
+        [shape_of((width, lanes))] * (3 - way),
         in_specs=[full(a) for a in arrived] + [part, part, dec, dec],
         after=after,
     )
@@ -238,8 +261,8 @@
     send_ref[...] = total[pl.ds(pl.multiple_of((1 - odd) * step, step), step), :]
 
 
-def late(way, sel, k, local_parts, carried, acc, cut, name):
-    wg, part, tot = local_parts
+def late(way, sel, state, carried, acc, cut, name):
+    _, wg, part, tot = state
     rows = wg.shape[1]
     width, lanes = carried.shape
     both = acc.shape[0] == 2
@@ -251,10 +274,10 @@
         [wg, carried, part, tot, acc],
         outs,
         in_specs=[
-            pl.BlockSpec((1, rows, lanes), lambda i, s: (s[way], 0, s[6 + k])),
+            pl.BlockSpec((1, rows, lanes), lambda i, s: (s[way], 0, 0)),
             full(carried),
-            pl.BlockSpec((width, lanes), lambda i, s: (s[way], s[6 + k])),
-            pl.BlockSpec((8, lanes), lambda i, s: (s[way], s[6 + k])),
+            pl.BlockSpec((width, lanes), lambda i, s: (s[way], 0)),
+            pl.BlockSpec((8, lanes), lambda i, s: (s[way], 0)),
             pl.BlockSpec((1, rows, width), lambda i, s: (s[way] if both else 0, 0, 0)),
         ],
         scratch=[pltpu.VMEM((rows, width), F32)] if cut else [],
@@ -288,26 +311,11 @@
 
 
 def scores_kernel(x_ref, g_ref, w_ref, r_ref, ld_ref, *rest):
-    acc_ref, wg_ref, part_ref, tot_ref, gs_ref = rest[-5:]
+    acc_ref, gs_ref = rest[-2:]
     group = pl.program_id(1)
     size = x_ref.shape[1] // GROUP
     half = Q // 2
     running = running_of(ld_ref[...])
-    decay_in, decay_out = spread_decays(running, size)
-    iw = (x_ref[...].astype(F32) * decay_out).astype(BF16)
-    gw = (g_ref[...].astype(F32) * decay_in).astype(BF16)
-    wg_ref[0] = gw
-    wg_ref[1] = iw
-    tot_ref[...] = jnp.broadcast_to(decay_in[Q - 1 : Q, :], tot_ref.shape)
-
-    @pl.when(pl.program_id(0) == 0)
-    def _():
-        part_ref[...] = dot(w_ref[...].astype(F32).T.astype(BF16), iw)
-
-    @pl.when(pl.program_id(0) == 1)
-    def _():
-        part_ref[...] = dot(r_ref[...].astype(F32).T.astype(BF16), gw)
-
     decays = decay_blocks(running)
     gs_top = jnp.zeros((half, Q), F32)
     gs_low = jnp.zeros((half, half), F32)
@@ -346,18 +354,8 @@
         scores_kernel,
         grid=(rows // Q, heads // GROUP),
         in_specs=[wide, wide, narrow, narrow, pl.BlockSpec((GROUP, Q), lambda b, j: (j, b))] + [ANYWHERE] * len(after),
-        out_specs=[
-            pl.BlockSpec((2, Q, width), lambda b, j: (0, b, 0)),
-            pl.BlockSpec((2, Q, lanes), lambda b, j: (0, b, j)),
-            pl.BlockSpec((width, lanes), lambda b, j: (b, j)),
-            pl.BlockSpec((8, lanes), lambda b, j: (b, j)),
-        ],
-        out_shape=[
-            shape_of((2, rows, width)),
-            stored((2, rows, heads * head_size), BF16),
-            stored((2 * width, heads * head_size)),
-            stored((16, heads * head_size)),
-        ],
+        out_specs=pl.BlockSpec((2, Q, width), lambda b, j: (0, b, 0)),
+        out_shape=shape_of((2, rows, width)),
         scratch_shapes=[pltpu.VMEM((Q, Q), F32)],
         compiler_params=params(),
         cost_estimate=FREE,
@@ -420,15 +418,15 @@
         gd_ref[:, at] = (times_ones(within, onward) + crossing) * scale
 
 
-def grads(sel, k, data, local_parts, carried, scale, head_size, held=(), after=()):
+def grads(sel, k, data, state, carried, scale, head_size, held=(), after=()):
     inputs, grad_out, write_proj, read_proj, log_decay = data
-    wg, part, tot = local_parts
+    pay, wg, part, tot = state
     rows, width = write_proj.shape
     heads = log_decay.shape[0]
     lanes = GROUP * head_size
     wide = pl.BlockSpec((rows, lanes), lambda i, s: (0, s[6 + k]))
     decays = pl.BlockSpec((GROUP, rows), lambda i, s: (s[6 + k], 0))
-    args = [inputs, grad_out, wg, write_proj, read_proj, log_decay, part, tot, *carried]
+    args = [inputs, grad_out, wg, write_proj, read_proj, log_decay, part, tot, *carried, pay]
     return pl.pallas_call(
         functools.partial(grads_kernel, scale),
         grid_spec=pltpu.PrefetchScalarGridSpec(
@@ -437,14 +435,12 @@
             in_specs=[
                 wide,
                 wide,
-                pl.BlockSpec((1, rows, lanes), lambda i, s: (0, 0, s[6 + k])),
+                pl.BlockSpec((1, rows, lanes), lambda i, s: (0, 0, 0)),
                 full(write_proj),
                 full(read_proj),
                 decays,
-                pl.BlockSpec((2 * width, lanes), lambda i, s: (0, s[6 + k])),
-                pl.BlockSpec((16, lanes), lambda i, s: (0, s[6 + k])),
             ]
-            + [full(a) for a in carried]
+            + [full(a) for a in (part, tot, *carried, pay)]
             + [ANYWHERE] * (len(held) + len(after)),
             out_specs=[wide, decays],
         ),
@@ -524,29 +520,31 @@
 
     if fast:
         other = states(order[1][None], *data, head_size)
-        got = swap(other, "seq", 1)
+        got = swap(other[0], "seq", 1)
         mine = states(order[0][None], *data, head_size)
-        px, py = call(chip_kernel, "chip", sel, (mine, got), [shape_of((width + 8, lanes))] * 2)
-        rx, ry, rd = swap(px, "seq", 2), swap(py, "seq", 4), swap(py, "seq", 6)
-        early, *parts = scores(*data, head_size, (px, py))
-        near_own, send = carry(0, sel, [rx], mine, got, "carry_near", (parts[2],))
+        outs = [shape_of((width + 8, lanes)), shape_of((width, lanes))]
+        px, qx = call(chip_kernel, "chip", sel, (mine[0], got), outs)
+        rx, sx = swap(px, "seq", 2), swap(qx, "seq", 2)
+        early = scores(*data, head_size, (px,))
+        near_own, send, pair = carry(0, sel, [rx, px], mine[0], got, (early,))
+        ry = swap(pair, "seq", 4)
         near_got = swap(send, "seq", 1)
-        (acc,) = late(0, sel, 0, parts, near_own, early, False, "late_near_mine")
-        near_parts = late(0, sel, 1, parts, near_got, acc[None], True, "late_near_other")
+        (acc,) = late(0, sel, mine, near_own, early, False, "late_near_mine")
+        near_parts = late(0, sel, other, near_got, acc[None], True, "late_near_other")
         near_half = near_parts[0] + swap(near_parts[1], "head", 1)
         near_cross = swap(near_half, "head", 2)
-        far_own, send = carry(1, sel, [rx, ry, rd], mine, got, "carry_far", (near_half,))
+        far_own, send = carry(1, sel, [rx, sx, ry], mine[0], got, (near_half,))
         far_got = swap(send, "seq", 1)
-        (acc,) = late(1, sel, 0, parts, far_own, early, False, "late_far_mine")
-        far_parts = late(1, sel, 1, parts, far_got, acc[None], True, "late_far_other")
+        (acc,) = late(1, sel, mine, far_own, early, False, "late_far_mine")
+        far_parts = late(1, sel, other, far_got, acc[None], True, "late_far_other")
         far_arrived = swap(far_parts[1], "head", 1)
         near_sum = near_half + near_cross
         near_rest = swap(near_sum, "head", 1)
-        held = grads(sel, 0, data, parts, (near_own, far_own, mine), scale, head_size, (), (far_parts[1],))
+        held = grads(sel, 0, data, mine, (near_own, far_own), scale, head_size, (), (far_parts[1],))
         far_half = far_parts[0] + tied(far_arrived, *held)
         far_cross = swap(far_half, "head", 2)
         grad_inputs, grad_decay = grads(
-            sel, 1, data, parts, (near_got, far_got, other), scale, head_size, held, (far_half,)
+            sel, 1, data, other, (near_got, far_got), scale, head_size, held, (far_half,)
         )
         far_sum = far_half + tied(far_cross, grad_decay)
         far_rest = swap(far_sum, "head", 1)
@@ -562,18 +560,18 @@
         )
         return grad_inputs, grad_write, grad_read, grad_decay
 
-    pays = [states(k[None], *data, head_size) for k in order]
-    early, *parts = scores(*data, head_size, ())
-    carried = [[scan_over(pay, width, bool(way)) for pay in pays] for way in (0, 1)]
+    local_states = [states(k[None], *data, head_size) for k in order]
+    early = scores(*data, head_size, ())
+    carried = [[scan_over(state[0], width, bool(way)) for state in local_states] for way in (0, 1)]
     totals = []
     for way in (0, 1):
         acc = early
-        for k in range(groups):
-            acc = late(way, sel, k, parts, carried[way][k], acc, False, "late")[0][None]
+        for k, state in enumerate(local_states):
+            acc = late(way, sel, state, carried[way][k], acc, False, "late")[0][None]
         totals.append(acc[0])
     held = ()
-    for k in range(groups):
-        held = grads(sel, k, data, parts, (carried[0][k], carried[1][k], pays[k]), scale, head_size, tuple(held))
+    for k, state in enumerate(local_states):
+        held = grads(sel, k, data, state, (carried[0][k], carried[1][k]), scale, head_size, tuple(held))
     grad_inputs, grad_decay = held
     grad_read, grad_write = lax.psum(tuple(totals), "head")
     return grad_inputs, grad_write, grad_read, grad_decay

time: 64.6 us -> 59.6 us (0.923)
  Pallas kernels: 31.9 us -> 29.3 us
  local copies, waits for them, and re-layouts: 2.32 us -> 0.58 us
    pallas_call x1, Pallas kernels: 7.05 us -> 3.51 us  [scores(): pl.pallas_call(scores_kernel, grid=(rows // Q, heads // GROUP), in_specs=...]
    unnamed x18 -> x22, local copies, waits for them, and re-layouts: 2.23 us -> 0.5 us
    pallas_call x2, Pallas kernels: 6.44 us -> 7.57 us  [states(): pl.pallas_call(state_kernel, grid_spec=pltpu.PrefetchScalarGridSpec(num_s...]
  transfers between devices with their start and end apart: 12 -> 12, of which waited for: 7 -> 6; matrix products, arithmetic and copies ran while one was open for 0% -> 0% of each run, Pallas kernels for 38% -> 36%
where the time goes in v3:
time: 59.6 us; the launch traced here: 59.4 us
  Pallas kernels  29.3 us (49%)
  starting transfers between devices  14.6 us (24%)
  waiting for transfers between devices  14 us (23%)
  between operations  0.89 us (1%)
    ppermute x12, starting transfers between devices, swap(): return lax.ppermute(values, axis, [(i, i ^ mask) for i in range(count)])  14.6 us
    ppermute x12, waiting for transfers between devices, swap(): return lax.ppermute(values, axis, [(i, i ^ mask) for i in range(count)])  14 us
    pallas_call x2, Pallas kernels, grads(): pl.pallas_call(functools.partial(grads_kernel, scale), grid_spec=pltpu.Pr...  11.4 us
    pallas_call x2, Pallas kernels, states(): pl.pallas_call(state_kernel, grid_spec=pltpu.PrefetchScalarGridSpec(num_s...  7.57 us
    pallas_call x8, Pallas kernels, call(): pl.pallas_call(body, grid_spec=pltpu.PrefetchScalarGridSpec(num_scalar_pr...  6.84 us
    pallas_call x1, Pallas kernels, scores(): pl.pallas_call(scores_kernel, grid=(rows // Q, heads // GROUP), in_specs=...  3.51 us
  transfers between devices with their start and end apart: 12, of which 6 were waited for; matrix products, arithmetic and copies ran while one was open for 0% of the time, Pallas kernels for 36%

profile of v3, /device:TPU:0, one launch (start us, length us, event | category | flops | bytes accessed | tf_op | source)
XLA Modules:
  0.0 59.4 jit_solution(17423679059624233272)
XLA Ops:
  0.6 3.8 %states.2 = (f32[264,512]{1,0:T(8,128)}, bf16[2,512,512]{2,1,0:T(8,128)(2,1)}, f32[256,512]{1,0:T(8,128)}, f32[16,512]{1,0:T(8,128)}) custom-call(s32[1]{0:T(128)} %bitcast.5.sel, bf16[512,1024]{1,0:T(8,128)(2,1)} %x_ref.5, bf16[512,1024]{1,0:T(8,128)(2,1)} %g_ref.5, bf16[512,128]{1,0:T(8,128)(2,1)} %w_ref.5, bf16[512,128]{1,0:T(8,128)(2,1)} %r_ref.5, ...), custom_call_target="tpu_custom_call" | custom-call | flops 1000 | bytes 1000 | tf_op jit(solution)/shard_map/states/pallas_call | solution.py:142
  4.4 0.5 collective-permute-start
  4.9 3.8 %states.3 = (f32[264,512]{1,0:T(8,128)S(1)}, bf16[2,512,512]{2,1,0:T(8,128)(2,1)}, f32[256,512]{1,0:T(8,128)}, f32[16,512]{1,0:T(8,128)}) custom-call(s32[1]{0:T(128)} %bitcast.2.sel, bf16[512,1024]{1,0:T(8,128)(2,1)} %x_ref.5, bf16[512,1024]{1,0:T(8,128)(2,1)} %g_ref.5, bf16[512,128]{1,0:T(8,128)(2,1)} %w_ref.5, bf16[512,128]{1,0:T(8,128)(2,1)} %r_ref.5, ...), custom_call_target="tpu_custom_call" | custom-call | flops 1000 | bytes 1000 | tf_op jit(solution)/shard_map/states/pallas_call | solution.py:142
  8.8 0.1 stack.29.s.sel
  8.9 0.7 %chip.1 = (f32[136,512]{1,0:T(8,128)S(1)}, f32[128,512]{1,0:T(8,128)S(1)}) custom-call(s32[8]{0:T(128)S(1)} %stack.29.s.sel, f32[264,512]{1,0:T(8,128)S(1)} %get-tuple-element.34.refs_0_.refs_2_.refs_4_.refs_3_.refs_5_.pay_ref, f32[264,512]{1,0:T(8,128)S(1)} %collective-permute-done.refs_1_.refs_3_.refs_5_.refs_4_.refs_6_), custom_call_target="tpu_custom_call" | custom-call | flops 1000 | bytes 1000 | tf_op jit(solution)/shard_map/chip/pallas_call | solution.py:194
  9.6 2.6 %collective-permute-start.1 = (f32[136,512]{1,0:T(8,128)S(1)}, f32[136,512]{1,0:T(8,128)S(1)}, u32[]{:S(2)}, u32[]{:S(2)}) collective-permute-start(f32[136,512]{1,0:T(8,128)S(1)} %get-tuple-element.36.rest_0_.refs_1_), channel_id=1, source_target_pairs={{0,8},{4,12},{8,0},{12,4},{16,24},{20,28},{24,16},{28,20},{1,9},{5... | collective-permute-start | bytes 835592 | tf_op jit(solution)/shard_map/ppermute | solution.py:477
  12.2 3.5 %scores.1.refs_6_.refs_4_ = f32[2,512,128]{2,1,0:T(8,128)S(1)} custom-call(bf16[512,1024]{1,0:T(8,128)(2,1)S(1)} %copy-done, bf16[512,1024]{1,0:T(8,128)(2,1)S(1)} %copy-done.1, bf16[512,128]{1,0:T(8,128)(2,1)S(1)} %copy-done.6, bf16[512,128]{1,0:T(8,128)(2,1)S(1)} %copy-done.7, f32[16,512]{1,0:T(8,128)S(1)} %copy-done.8, ...), custom_call_target="tpu_custom_call" | custom-call | flops 1000 | bytes 1000 | tf_op jit(solution)/shard_map/scores/pallas_call | solution.py:353
  15.7 3.7 %collective-permute-done.1.refs_0_ = f32[136,512]{1,0:T(8,128)S(1)} collective-permute-done((f32[136,512]{1,0:T(8,128)S(1)}, f32[136,512]{1,0:T(8,128)S(1)}, u32[]{:S(2)}, u32[]{:S(2)}) %collective-permute-start.1) | collective-permute-done | bytes 278560 | tf_op jit(solution)/shard_map/ppermute | solution.py:477
  19.5 0.7 %carry_near.1 = (f32[128,512]{1,0:T(8,128)S(1)}, f32[128,512]{1,0:T(8,128)S(1)}, f32[128,512]{1,0:T(8,128)S(1)}) custom-call(s32[8]{0:T(128)S(1)} %stack.29.s.sel, f32[136,512]{1,0:T(8,128)S(1)} %collective-permute-done.1.refs_0_, f32[136,512]{1,0:T(8,128)S(1)} %get-tuple-element.36.rest_0_.refs_1_, ...), custom_call_target="tpu_custom_call" | custom-call | flops 1000 | bytes 1000 | tf_op jit(solution)/shard_map/carry_near/pallas_call | solution.py:194
  20.2 1.8 %collective-permute-start.3 = (f32[128,512]{1,0:T(8,128)S(1)}, f32[128,512]{1,0:T(8,128)S(1)}, u32[]{:S(2)}, u32[]{:S(2)}) collective-permute-start(f32[128,512]{1,0:T(8,128)S(1)} %get-tuple-element.38), channel_id=1, source_target_pairs={{0,8},{4,12},{8,0},{12,4},{16,24},{20,28},{24,16},{28,20},{1,9},{5... | collective-permute-start | bytes 786440 | tf_op jit(solution)/shard_map/ppermute | solution.py:477
  22.0 1.5 %collective-permute-start.4 = (f32[128,512]{1,0:T(8,128)S(1)}, f32[128,512]{1,0:T(8,128)S(1)}, u32[]{:S(2)}, u32[]{:S(2)}) collective-permute-start(f32[128,512]{1,0:T(8,128)S(1)} %get-tuple-element.39), channel_id=1, source_target_pairs={{0,16},{4,20},{8,24},{12,28},{16,0},{20,4},{24,8},{28,12},{1,17},{... | collective-permute-start | bytes 786440 | tf_op jit(solution)/shard_map/ppermute | solution.py:477
  23.6 0.9 %late_near_mine.1 = f32[512,128]{1,0:T(8,128)S(1)} custom-call(s32[8]{0:T(128)S(1)} %stack.29.s.sel, bf16[2,512,512]{2,1,0:T(8,128)(2,1)S(1)} %copy-done.3, f32[128,512]{1,0:T(8,128)S(1)} %get-tuple-element.41.refs_1_.near_ref, f32[256,512]{1,0:T(8,128)S(1)} %copy-done.5, f32[16,512]{1,0:T(8,128)S(1)} %copy-done.10, f32[2,512,128]{2,1,0:T(8,128)S(1)} %scores.1.refs_6_.refs_4_), custom_call_target="tpu_custom_call" | custom-call | flops 1000 | bytes 1000 | tf_op jit(solution)/shard_map/late_near_mine/pallas_call | solution.py:194
  24.5 0.3 copy-done.2
  24.8 0.1 copy-done.4
  24.9 0.9 %late_near_other.1 = (f32[256,128]{1,0:T(8,128)S(1)}, f32[256,128]{1,0:T(8,128)S(1)}) custom-call(s32[8]{0:T(128)S(1)} %stack.29.s.sel, bf16[2,512,512]{2,1,0:T(8,128)(2,1)S(1)} %copy-done.2, f32[128,512]{1,0:T(8,128)S(1)} %collective-permute-done.2.refs_1_.near_ref, f32[256,512]{1,0:T(8,128)S(1)} %copy-done.4, f32[16,512]{1,0:T(8,128)S(1)} %copy-done.9, ...), custom_call_target="tpu_custom_call" | custom-call | flops 1000 | bytes 1000 | tf_op jit(solution)/shard_map/late_near_other/pallas_call | solution.py:194
  25.8 1.6 %collective-permute-start.5 = (f32[256,128]{1,0:T(8,128)S(1)}, f32[256,128]{1,0:T(8,128)S(1)}, u32[]{:S(2)}, u32[]{:S(2)}) collective-permute-start(f32[256,128]{1,0:T(8,128)S(1)} %get-tuple-element.45), channel_id=1, source_target_pairs={{0,1},{1,0},{2,3},{3,2},{4,5},{5,4},{6,7},{7,6},{8,9},{9,8},{10,11... | collective-permute-start | bytes 393224 | tf_op jit(solution)/shard_map/ppermute | solution.py:477
  27.5 3.7 %collective-permute-done.5 = f32[256,128]{1,0:T(8,128)S(1)} collective-permute-done((f32[256,128]{1,0:T(8,128)S(1)}, f32[256,128]{1,0:T(8,128)S(1)}, u32[]{:S(2)}, u32[]{:S(2)}) %collective-permute-start.5) | collective-permute-done | bytes 131104 | tf_op jit(solution)/shard_map/ppermute | solution.py:477
  31.2 0.6 %carry_far.1 = (f32[128,512]{1,0:T(8,128)S(1)}, f32[128,512]{1,0:T(8,128)S(1)}) custom-call(s32[8]{0:T(128)S(1)} %stack.29.s.sel, f32[136,512]{1,0:T(8,128)S(1)} %collective-permute-done.1.refs_0_, f32[128,512]{1,0:T(8,128)S(1)} %collective-permute-done.3.refs_1_, f32[128,512]{1,0:T(8,128)S(1)} %collective-permute-done.4.refs_2_, ...), custom_call_target="tpu_custom_call" | custom-call | flops 1000 | bytes 1000 | tf_op jit(solution)/shard_map/carry_far/pallas_call | solution.py:194
  31.9 0.9 %late_far_mine.1 = f32[512,128]{1,0:T(8,128)S(1)} custom-call(s32[8]{0:T(128)S(1)} %stack.29.s.sel, bf16[2,512,512]{2,1,0:T(8,128)(2,1)S(1)} %copy-done.3, f32[128,512]{1,0:T(8,128)S(1)} %get-tuple-element.47.refs_1_.far_ref, f32[256,512]{1,0:T(8,128)S(1)} %copy-done.5, f32[16,512]{1,0:T(8,128)S(1)} %copy-done.10, f32[2,512,128]{2,1,0:T(8,128)S(1)} %scores.1.refs_6_.refs_4_), custom_call_target="tpu_custom_call" | custom-call | flops 1000 | bytes 1000 | tf_op jit(solution)/shard_map/late_far_mine/pallas_call | solution.py:194
  32.8 0.7 %collective-permute-done.6.refs_1_.far_ref = f32[128,512]{1,0:T(8,128)S(1)} collective-permute-done((f32[128,512]{1,0:T(8,128)S(1)}, f32[128,512]{1,0:T(8,128)S(1)}, u32[]{:S(2)}, u32[]{:S(2)}) %collective-permute-start.6) | collective-permute-done | bytes 262176 | tf_op jit(solution)/shard_map/ppermute | solution.py:477
  33.4 0.9 %late_far_other.1 = (f32[256,128]{1,0:T(8,128)S(1)}, f32[256,128]{1,0:T(8,128)S(1)}) custom-call(s32[8]{0:T(128)S(1)} %stack.29.s.sel, bf16[2,512,512]{2,1,0:T(8,128)(2,1)S(1)} %copy-done.2, f32[128,512]{1,0:T(8,128)S(1)} %collective-permute-done.6.refs_1_.far_ref, f32[256,512]{1,0:T(8,128)S(1)} %copy-done.4, f32[16,512]{1,0:T(8,128)S(1)} %copy-done.9, ...), custom_call_target="tpu_custom_call" | custom-call | flops 1000 | bytes 1000 | tf_op jit(solution)/shard_map/late_far_other/pallas_call | solution.py:194
  34.3 1.6 %collective-permute-start.7 = (f32[256,128]{1,0:T(8,128)S(1)}, f32[256,128]{1,0:T(8,128)S(1)}, u32[]{:S(2)}, u32[]{:S(2)}) collective-permute-start(f32[256,128]{1,0:T(8,128)S(1)} %get-tuple-element.48.rest_0_), channel_id=1, source_target_pairs={{0,1},{1,0},{2,3},{3,2},{4,5},{5,4},{6,7},{7,6},{8,9},{9,8},{10,11... | collective-permute-start | bytes 393224 | tf_op jit(solution)/shard_map/ppermute | solution.py:477
  36.0 2.6 %collective-permute-start.8 = (f32[256,128]{1,0:T(8,128)S(1)}, f32[256,128]{1,0:T(8,128)S(1)}, u32[]{:S(2)}, u32[]{:S(2)}) collective-permute-start(f32[256,128]{1,0:T(8,128)S(1)} %add.27.refs_7_), channel_id=1, source_target_pairs={{0,2},{1,3},{2,0},{3,1},{4,6},{5,7},{6,4},{7,5},{8,10},{9,11},{10,... | collective-permute-start | bytes 393224 | tf_op jit(solution)/shard_map/ppermute | solution.py:477
  38.6 5.2 %grads.2 = (bf16[512,1024]{1,0:T(8,128)(2,1)}, f32[16,512]{1,0:T(8,128)}) custom-call(s32[8]{0:T(128)S(1)} %stack.29.s.sel, bf16[512,1024]{1,0:T(8,128)(2,1)S(1)} %copy-done, bf16[512,1024]{1,0:T(8,128)(2,1)S(1)} %copy-done.1, bf16[2,512,512]{2,1,0:T(8,128)(2,1)S(1)} %copy-done.3, bf16[512,128]{1,0:T(8,128)(2,1)S(1)} %copy-done.6, ...), custom_call_target="tpu_custom_call" | custom-call | flops 1000 | bytes 1000 | tf_op jit(solution)/shard_map/grads/pallas_call | solution.py:430
  43.8 0.4 collective-permute-start.10
  44.2 0.8 %collective-permute-done.8 = f32[256,128]{1,0:T(8,128)S(1)} collective-permute-done((f32[256,128]{1,0:T(8,128)S(1)}, f32[256,128]{1,0:T(8,128)S(1)}, u32[]{:S(2)}, u32[]{:S(2)}) %collective-permute-start.8) | collective-permute-done | bytes 131104 | tf_op jit(solution)/shard_map/ppermute | solution.py:477
  45.0 0.9 %collective-permute-start.9 = (f32[256,128]{1,0:T(8,128)S(1)}, f32[256,128]{1,0:T(8,128)S(1)}, u32[]{:S(2)}, u32[]{:S(2)}) collective-permute-start(f32[256,128]{1,0:T(8,128)S(1)} %add.29.refs_0_), channel_id=1, source_target_pairs={{0,1},{1,0},{2,3},{3,2},{4,5},{5,4},{6,7},{7,6},{8,9},{9,8},{10,11... | collective-permute-start | bytes 393224 | tf_op jit(solution)/shard_map/ppermute | solution.py:477
  45.9 6.2 %grads.3 = (bf16[512,1024]{1,0:T(8,128)(2,1)}, f32[16,512]{1,0:T(8,128)}) custom-call(s32[8]{0:T(128)S(1)} %stack.29.s.sel, bf16[512,1024]{1,0:T(8,128)(2,1)S(1)} %copy-done, bf16[512,1024]{1,0:T(8,128)(2,1)S(1)} %copy-done.1, bf16[2,512,512]{2,1,0:T(8,128)(2,1)S(1)} %copy-done.2, ...), custom_call_target="tpu_custom_call", output_to_operand_aliasing={{0}: (12, {}), {1}: (13, {})} | custom-call | flops 1000 | bytes 1000 | tf_op jit(solution)/shard_map/grads/pallas_call | solution.py:430
  52.1 0.5 collective-permute-done.10
  52.6 0.8 %collective-permute-start.11 = (f32[256,128]{1,0:T(8,128)S(1)}, f32[256,128]{1,0:T(8,128)S(1)}, u32[]{:S(2)}, u32[]{:S(2)}) collective-permute-start(f32[256,128]{1,0:T(8,128)S(1)} %add.30.refs_2_), channel_id=1, source_target_pairs={{0,1},{1,0},{2,3},{3,2},{4,5},{5,4},{6,7},{7,6},{8,9},{9,8},{10,11... | collective-permute-start | bytes 393224 | tf_op jit(solution)/shard_map/ppermute | solution.py:477
  53.4 4.6 %collective-permute-done.11.refs_3_ = f32[256,128]{1,0:T(8,128)S(1)} collective-permute-done((f32[256,128]{1,0:T(8,128)S(1)}, f32[256,128]{1,0:T(8,128)S(1)}, u32[]{:S(2)}, u32[]{:S(2)}) %collective-permute-start.11) | collective-permute-done | bytes 131104 | tf_op jit(solution)/shard_map/ppermute | solution.py:477
  58.0 1.4 %join.1 = (f32[512,128]{1,0:T(8,128)}, f32[512,128]{1,0:T(8,128)}) custom-call(s32[8]{0:T(128)S(1)} %stack.29.s.sel, f32[256,128]{1,0:T(8,128)S(1)} %add.29.refs_0_, f32[256,128]{1,0:T(8,128)S(1)} %collective-permute-done.9.refs_1_, f32[256,128]{1,0:T(8,128)S(1)} %add.30.refs_2_, f32[256,128]{1,0:T(8,128)S(1)} %collective-permute-done.11.refs_3_), custom_call_target="tpu_custom_call" | custom-call | flops 1000 | bytes 1000 | tf_op jit(solution)/shard_map/join/pallas_call | solution.py:194
  (32 shorter events, 0.3 us)
Async XLA Ops:
  4.4 4.5 %collective-permute-start = (f32[264,512]{1,0:T(8,128)}, f32[264,512]{1,0:T(8,128)S(1)}, u32[]{:S(2)}, u32[]{:S(2)}) collective-permute-start(f32[264,512]{1,0:T(8,128)} %get-tuple-element.35.pay_ref), channel_id=1, source_target_pairs={{0,4},{4,0},{8,12},{12,8},{16,20},{20,16},{24,28},{28,24},{1,5},{5... | collective-permute-start | bytes 1622024 | tf_op jit(solution)/shard_map/ppermute | solution.py:477
  4.9 7.2 %copy-start.1 = (bf16[512,1024]{1,0:T(8,128)(2,1)S(1)}, bf16[512,1024]{1,0:T(8,128)(2,1)}, u32[]{:S(2)}) copy-start(bf16[512,1024]{1,0:T(8,128)(2,1)} %g_ref.5) | copy-start | bytes 3145732
  4.9 7.2 %copy-start.7 = (bf16[512,128]{1,0:T(8,128)(2,1)S(1)}, bf16[512,128]{1,0:T(8,128)(2,1)}, u32[]{:S(2)}) copy-start(bf16[512,128]{1,0:T(8,128)(2,1)} %r_ref.5) | copy-start | bytes 393220
  4.9 7.2 %copy-start.8 = (f32[16,512]{1,0:T(8,128)S(1)}, f32[16,512]{1,0:T(8,128)}, u32[]{:S(2)}) copy-start(f32[16,512]{1,0:T(8,128)} %ld_ref.5) | copy-start | bytes 98308
  8.8 3.4 %copy-start = (bf16[512,1024]{1,0:T(8,128)(2,1)S(1)}, bf16[512,1024]{1,0:T(8,128)(2,1)}, u32[]{:S(2)}) copy-start(bf16[512,1024]{1,0:T(8,128)(2,1)} %x_ref.5) | copy-start | bytes 3145732
  8.9 3.3 %copy-start.6 = (bf16[512,128]{1,0:T(8,128)(2,1)S(1)}, bf16[512,128]{1,0:T(8,128)(2,1)}, u32[]{:S(2)}) copy-start(bf16[512,128]{1,0:T(8,128)(2,1)} %w_ref.5) | copy-start | bytes 393220
  9.6 9.9 %collective-permute-start.1 = (f32[136,512]{1,0:T(8,128)S(1)}, f32[136,512]{1,0:T(8,128)S(1)}, u32[]{:S(2)}, u32[]{:S(2)}) collective-permute-start(f32[136,512]{1,0:T(8,128)S(1)} %get-tuple-element.36.rest_0_.refs_1_), channel_id=1, source_target_pairs={{0,8},{4,12},{8,0},{12,4},{16,24},{20,28},{24,16},{28,20},{1,9},{5... | collective-permute-start | bytes 835592 | tf_op jit(solution)/shard_map/ppermute | solution.py:477
  15.7 7.8 %copy-start.3 = (bf16[2,512,512]{2,1,0:T(8,128)(2,1)S(1)}, bf16[2,512,512]{2,1,0:T(8,128)(2,1)}, u32[]{:S(2)}) copy-start(bf16[2,512,512]{2,1,0:T(8,128)(2,1)} %get-tuple-element.40.refs_0_.gw_ref) | copy-start | bytes 3145732
  15.7 7.8 %copy-start.5 = (f32[256,512]{1,0:T(8,128)S(1)}, f32[256,512]{1,0:T(8,128)}, u32[]{:S(2)}) copy-start(f32[256,512]{1,0:T(8,128)} %get-tuple-element.42.refs_2_.part_ref) | copy-start | bytes 1572868
  19.5 4.1 %copy-start.10 = (f32[16,512]{1,0:T(8,128)S(1)}, f32[16,512]{1,0:T(8,128)}, u32[]{:S(2)}) copy-start(f32[16,512]{1,0:T(8,128)} %get-tuple-element.43.refs_3_.tot_ref) | copy-start | bytes 98308
  20.1 4.3 %collective-permute-start.2 = (f32[128,512]{1,0:T(8,128)S(1)}, f32[128,512]{1,0:T(8,128)S(1)}, u32[]{:S(2)}, u32[]{:S(2)}) collective-permute-start(f32[128,512]{1,0:T(8,128)S(1)} %get-tuple-element.37), channel_id=1, source_target_pairs={{0,4},{4,0},{8,12},{12,8},{16,20},{20,16},{24,28},{28,24},{1,5},{5... | collective-permute-start | bytes 786440 | tf_op jit(solution)/shard_map/ppermute | solution.py:477
  20.2 11.0 %collective-permute-start.3 = (f32[128,512]{1,0:T(8,128)S(1)}, f32[128,512]{1,0:T(8,128)S(1)}, u32[]{:S(2)}, u32[]{:S(2)}) collective-permute-start(f32[128,512]{1,0:T(8,128)S(1)} %get-tuple-element.38), channel_id=1, source_target_pairs={{0,8},{4,12},{8,0},{12,4},{16,24},{20,28},{24,16},{28,20},{1,9},{5... | collective-permute-start | bytes 786440 | tf_op jit(solution)/shard_map/ppermute | solution.py:477
  22.0 9.2 %collective-permute-start.4 = (f32[128,512]{1,0:T(8,128)S(1)}, f32[128,512]{1,0:T(8,128)S(1)}, u32[]{:S(2)}, u32[]{:S(2)}) collective-permute-start(f32[128,512]{1,0:T(8,128)S(1)} %get-tuple-element.39), channel_id=1, source_target_pairs={{0,16},{4,20},{8,24},{12,28},{16,0},{20,4},{24,8},{28,12},{1,17},{... | collective-permute-start | bytes 786440 | tf_op jit(solution)/shard_map/ppermute | solution.py:477
  23.5 1.2 %copy-start.2 = (bf16[2,512,512]{2,1,0:T(8,128)(2,1)S(1)}, bf16[2,512,512]{2,1,0:T(8,128)(2,1)}, u32[]{:S(2)}) copy-start(bf16[2,512,512]{2,1,0:T(8,128)(2,1)} %get-tuple-element.31.refs_0_.gw_ref) | copy-start | bytes 3145732
  23.6 1.4 %copy-start.4 = (f32[256,512]{1,0:T(8,128)S(1)}, f32[256,512]{1,0:T(8,128)}, u32[]{:S(2)}) copy-start(f32[256,512]{1,0:T(8,128)} %get-tuple-element.32.refs_2_.part_ref) | copy-start | bytes 1572868
  23.6 1.3 %copy-start.9 = (f32[16,512]{1,0:T(8,128)S(1)}, f32[16,512]{1,0:T(8,128)}, u32[]{:S(2)}) copy-start(f32[16,512]{1,0:T(8,128)} %get-tuple-element.33.refs_3_.tot_ref) | copy-start | bytes 98308
  25.8 5.3 %collective-permute-start.5 = (f32[256,128]{1,0:T(8,128)S(1)}, f32[256,128]{1,0:T(8,128)S(1)}, u32[]{:S(2)}, u32[]{:S(2)}) collective-permute-start(f32[256,128]{1,0:T(8,128)S(1)} %get-tuple-element.45), channel_id=1, source_target_pairs={{0,1},{1,0},{2,3},{3,2},{4,5},{5,4},{6,7},{7,6},{8,9},{9,8},{10,11... | collective-permute-start | bytes 393224 | tf_op jit(solution)/shard_map/ppermute | solution.py:477
  31.8 1.6 %collective-permute-start.6 = (f32[128,512]{1,0:T(8,128)S(1)}, f32[128,512]{1,0:T(8,128)S(1)}, u32[]{:S(2)}, u32[]{:S(2)}) collective-permute-start(f32[128,512]{1,0:T(8,128)S(1)} %get-tuple-element.46), channel_id=1, source_target_pairs={{0,4},{4,0},{8,12},{12,8},{16,20},{20,16},{24,28},{28,24},{1,5},{5... | collective-permute-start | bytes 786440 | tf_op jit(solution)/shard_map/ppermute | solution.py:477
  34.3 9.4 %collective-permute-start.7 = (f32[256,128]{1,0:T(8,128)S(1)}, f32[256,128]{1,0:T(8,128)S(1)}, u32[]{:S(2)}, u32[]{:S(2)}) collective-permute-start(f32[256,128]{1,0:T(8,128)S(1)} %get-tuple-element.48.rest_0_), channel_id=1, source_target_pairs={{0,1},{1,0},{2,3},{3,2},{4,5},{5,4},{6,7},{7,6},{8,9},{9,8},{10,11... | collective-permute-start | bytes 393224 | tf_op jit(solution)/shard_map/ppermute | solution.py:477
  36.0 9.0 %collective-permute-start.8 = (f32[256,128]{1,0:T(8,128)S(1)}, f32[256,128]{1,0:T(8,128)S(1)}, u32[]{:S(2)}, u32[]{:S(2)}) collective-permute-start(f32[256,128]{1,0:T(8,128)S(1)} %add.27.refs_7_), channel_id=1, source_target_pairs={{0,2},{1,3},{2,0},{3,1},{4,6},{5,7},{6,4},{7,5},{8,10},{9,11},{10,... | collective-permute-start | bytes 393224 | tf_op jit(solution)/shard_map/ppermute | solution.py:477
  43.8 8.8 %collective-permute-start.10 = (f32[256,128]{1,0:T(8,128)S(1)}, f32[256,128]{1,0:T(8,128)S(1)}, u32[]{:S(2)}, u32[]{:S(2)}) collective-permute-start(f32[256,128]{1,0:T(8,128)S(1)} %add.28.rest_2_), channel_id=1, source_target_pairs={{0,2},{1,3},{2,0},{3,1},{4,6},{5,7},{6,4},{7,5},{8,10},{9,11},{10,... | collective-permute-start | bytes 393224 | tf_op jit(solution)/shard_map/ppermute | solution.py:477
  45.0 8.4 %collective-permute-start.9 = (f32[256,128]{1,0:T(8,128)S(1)}, f32[256,128]{1,0:T(8,128)S(1)}, u32[]{:S(2)}, u32[]{:S(2)}) collective-permute-start(f32[256,128]{1,0:T(8,128)S(1)} %add.29.refs_0_), channel_id=1, source_target_pairs={{0,1},{1,0},{2,3},{3,2},{4,5},{5,4},{6,7},{7,6},{8,9},{9,8},{10,11... | collective-permute-start | bytes 393224 | tf_op jit(solution)/shard_map/ppermute | solution.py:477
  52.6 5.4 %collective-permute-start.11 = (f32[256,128]{1,0:T(8,128)S(1)}, f32[256,128]{1,0:T(8,128)S(1)}, u32[]{:S(2)}, u32[]{:S(2)}) collective-permute-start(f32[256,128]{1,0:T(8,128)S(1)} %add.30.refs_2_), channel_id=1, source_target_pairs={{0,1},{1,0},{2,3},{3,2},{4,5},{5,4},{6,7},{7,6},{8,9},{9,8},{10,11... | collective-permute-start | bytes 393224 | tf_op jit(solution)/shard_map/ppermute | solution.py:477

commit v4 on v3

--- a/solution.py
+++ b/solution.py
@@ -64,20 +64,29 @@
 
 def state_kernel(sel, x_hbm, g_hbm, w_hbm, r_hbm, ld_hbm, *rest):
     outs, (x_ref, g_ref, w_ref, r_ref, ld_ref, pay_ref, wg_ref, part_ref, tot_ref, sems) = rest[:4], rest[4:]
+    state_body(sel, (x_hbm, g_hbm, w_hbm, r_hbm, ld_hbm), (x_ref, g_ref, w_ref, r_ref, ld_ref), outs, pay_ref, wg_ref, part_ref, tot_ref, sems)
+
+
+def loaded_kernel(sel, *refs):
+    state_body(sel, None, refs[:5], refs[5:9], *refs[9:])
+
+
+def state_body(sel, sources, refs, outs, pay_ref, wg_ref, part_ref, tot_ref, sems):
+    x_ref, g_ref, w_ref, r_ref, ld_ref = refs
     rows, lanes = x_ref.shape
     width = w_ref.shape[1]
     here = pl.ds(pl.multiple_of(sel[0] * lanes, lanes), lanes)
     group = pl.ds(pl.multiple_of(sel[0] * GROUP, GROUP), GROUP)
-    small = [
-        pltpu.make_async_copy(src, dst, sems.at[k])
-        for k, (src, dst) in enumerate(((ld_hbm.at[group, :], ld_ref), (w_hbm, w_ref), (r_hbm, r_ref)))
-    ]
-    large = []
-    for b in range(2):
-        at = pl.ds(b * Q, Q)
-        large.append(pltpu.make_async_copy(x_hbm.at[at, here], x_ref.at[at, :], sems.at[3 + 2 * b]))
-        large.append(pltpu.make_async_copy(g_hbm.at[at, here], g_ref.at[at, :], sems.at[4 + 2 * b]))
-    for move in small + large:
+    moves = []
+    if sources:
+        x_hbm, g_hbm, w_hbm, r_hbm, ld_hbm = sources
+        pairs = [(ld_hbm.at[group, :], ld_ref), (w_hbm, w_ref), (r_hbm, r_ref)]
+        for b in range(2):
+            at = pl.ds(b * Q, Q)
+            pairs.append((x_hbm.at[at, here], x_ref.at[at, :]))
+            pairs.append((g_hbm.at[at, here], g_ref.at[at, :]))
+        moves = [pltpu.make_async_copy(src, dst, sems.at[k]) for k, (src, dst) in enumerate(pairs)]
+    for move in moves:
         move.start()
     leaving = []
 
@@ -86,24 +95,27 @@
         leaving[-1].start()
 
     pay_out, wg_out, part_out, tot_out = outs
-    small[0].wait()
+    for move in moves[:1]:
+        move.wait()
     decays = [spread_decays(running_of(ld_ref[:, b * Q : (b + 1) * Q]), lanes // GROUP) for b in range(2)]
     ends = [decay_in[Q - 1 : Q, :] for decay_in, _ in decays]
     tot_ref[0:8, :] = jnp.broadcast_to(ends[0], (8, lanes))
     tot_ref[8:16, :] = jnp.broadcast_to(ends[1], (8, lanes))
     leave(tot_ref, tot_out)
-    small[1].wait()
-    small[2].wait()
+    for move in moves[1:3]:
+        move.wait()
     f_parts, g_parts = [], []
     for b in range(2):
         at = slice(b * Q, (b + 1) * Q)
         decay_in, decay_out = decays[b]
-        large[2 * b].wait()
+        for move in moves[3 + 2 * b : 4 + 2 * b]:
+            move.wait()
         iw = (x_ref[at, :].astype(F32) * decay_out).astype(BF16)
         wg_ref[1, at, :] = iw
         leave(wg_ref.at[1, pl.ds(b * Q, Q), :], wg_out.at[1, pl.ds(b * Q, Q), :])
         f_parts.append(dot(w_ref[at, :].astype(F32).T.astype(BF16), iw))
-        large[2 * b + 1].wait()
+        for move in moves[4 + 2 * b : 5 + 2 * b]:
+            move.wait()
         gw = (g_ref[at, :].astype(F32) * decay_in).astype(BF16)
         wg_ref[0, at, :] = gw
         leave(wg_ref.at[0, pl.ds(b * Q, Q), :], wg_out.at[0, pl.ds(b * Q, Q), :])
@@ -135,24 +147,24 @@
     return pltpu.with_memory_space_constraint(values, pltpu.HBM)
 
 
-def states(which, inputs, grad_out, write_proj, read_proj, log_decay, head_size):
+def states(which, inputs, grad_out, write_proj, read_proj, log_decay, head_size, loaded):
     rows, width = write_proj.shape
     lanes = GROUP * head_size
     shapes = [((2 * width + 8, lanes), F32), ((2, rows, lanes), BF16), ((2 * width, lanes), F32), ((16, lanes), F32)]
+    args = (inputs, grad_out, write_proj, read_proj, log_decay)
+    buffers = [((rows, lanes), BF16)] * 2 + [((rows, width), BF16)] * 2 + [((GROUP, rows), F32)]
+    wide = pl.BlockSpec((rows, lanes), lambda i, s: (0, s[0]))
     return pl.pallas_call(
-        state_kernel,
+        loaded_kernel if loaded else state_kernel,
         grid_spec=pltpu.PrefetchScalarGridSpec(
             num_scalar_prefetch=1,
             grid=(1,),
-            in_specs=[pl.BlockSpec(memory_space=pltpu.HBM)] * 5,
+            in_specs=[wide, wide, full(write_proj), full(read_proj), pl.BlockSpec((GROUP, rows), lambda i, s: (s[0], 0))]
+            if loaded
+            else [pl.BlockSpec(memory_space=pltpu.HBM)] * 5,
             out_specs=[ANYWHERE] * 4,
             scratch_shapes=[
-                pltpu.VMEM((rows, lanes), BF16),
-                pltpu.VMEM((rows, lanes), BF16),
-                pltpu.VMEM((rows, width), BF16),
-                pltpu.VMEM((rows, width), BF16),
-                pltpu.VMEM((GROUP, rows), F32),
-                *[pltpu.VMEM(*a) for a in shapes],
+                *[pltpu.VMEM(*a) for a in ([] if loaded else buffers) + shapes],
                 pltpu.SemaphoreType.DMA((14,)),
             ],
         ),
@@ -160,7 +172,7 @@
         compiler_params=params(),
         cost_estimate=FREE,
         name="states",
-    )(which, *map(far_off, (inputs, grad_out, write_proj, read_proj, log_decay)))
+    )(which, *(args if loaded else map(far_off, args)))
 
 
 def chip_kernel(sel, mine_ref, got_ref, first_ref, second_ref):
@@ -311,20 +323,37 @@
 
 
 def scores_kernel(x_ref, g_ref, w_ref, r_ref, ld_ref, *rest):
-    acc_ref, gs_ref = rest[-2:]
+    acc_ref, gint_ref, dot_ref, gs_ref = rest[-4:]
     group = pl.program_id(1)
     size = x_ref.shape[1] // GROUP
     half = Q // 2
-    running = running_of(ld_ref[...])
-    decays = decay_blocks(running)
+    decays = decay_blocks(running_of(ld_ref[...]))
+    products = dot_t(w_ref[...], r_ref[...])
+    left = iota((Q, 2 * size), 1) < size
     gs_top = jnp.zeros((half, Q), F32)
     gs_low = jnp.zeros((half, half), F32)
+    sums_top, sums_low = [], []
     for pair in range(GROUP // 2):
         at = slice(pair * 2 * size, (pair + 1) * 2 * size)
-        for k, (pairs_top, pairs_low) in enumerate(pair_products(x_ref[:, at], g_ref[:, at])):
+        g_pair = g_ref[:, at]
+        none = jnp.zeros_like(g_pair)
+        top = low = None
+        for k, (pairs_top, pairs_low) in enumerate(pair_products(x_ref[:, at], g_pair)):
             decay_top, decay_low = decays(2 * pair + k)
-            gs_top = gs_top + decay_top * pairs_top
-            gs_low = gs_low + decay_low * pairs_low
+            scaled_top, scaled_low = decay_top * pairs_top, decay_low * pairs_low
+            gs_top = gs_top + scaled_top
+            gs_low = gs_low + scaled_low
+            sums_top.append(jnp.sum(products[0:half] * scaled_top, axis=0, keepdims=True))
+            sums_low.append(jnp.sum(products[half:, half:] * scaled_low, axis=0, keepdims=True))
+            g_own = jnp.where(left, g_pair, none) if k == 0 else jnp.where(left, none, g_pair)
+            part_top = dot((products[0:half] * decay_top).astype(BF16), g_own)
+            part_low = dot((products[half:, half:] * decay_low).astype(BF16), g_own[half:])
+            top = part_top if top is None else top + part_top
+            low = part_low if low is None else low + part_low
+        gint_ref[0:half, at] = top
+        gint_ref[half:, at] = low
+    late_half = jnp.concatenate(sums_low, axis=0)
+    dot_ref[...] = jnp.concatenate(sums_top, axis=0) + jnp.concatenate([jnp.zeros_like(late_half), late_half], axis=1)
 
     @pl.when(group == 0)
     def _():
@@ -354,8 +383,12 @@
         scores_kernel,
         grid=(rows // Q, heads // GROUP),
         in_specs=[wide, wide, narrow, narrow, pl.BlockSpec((GROUP, Q), lambda b, j: (j, b))] + [ANYWHERE] * len(after),
-        out_specs=pl.BlockSpec((2, Q, width), lambda b, j: (0, b, 0)),
-        out_shape=shape_of((2, rows, width)),
+        out_specs=[
+            pl.BlockSpec((2, Q, width), lambda b, j: (0, b, 0)),
+            wide,
+            pl.BlockSpec((GROUP, Q), lambda b, j: (j, b)),
+        ],
+        out_shape=[shape_of((2, rows, width)), stored((rows, heads * head_size)), stored((heads, rows))],
         scratch_shapes=[pltpu.VMEM((Q, Q), F32)],
         compiler_params=params(),
         cost_estimate=FREE,
@@ -363,12 +396,13 @@
     )(inputs, grad_out, write_proj, read_proj, log_decay, *after)
 
 
-def grads_kernel(scale, sel, x_ref, g_ref, gw_ref, w_ref, r_ref, ld_ref, part_ref, tot_ref, near_ref, far_ref, pay_ref, *rest):
+def grads_kernel(
+    scale, sel, x_ref, gw_ref, w_ref, r_ref, ld_ref, gint_ref, dot_ref, part_ref, tot_ref, near_ref, far_ref, pay_ref, *rest
+):
     gi_ref, gd_ref = rest[-2:]
     lanes = x_ref.shape[1]
     width = w_ref.shape[1]
     size = lanes // GROUP
-    half = Q // 2
     near_forward = sel[0] == 0
     f_car = jnp.where(near_forward, near_ref[...], far_ref[...])
     b_car = jnp.where(near_forward, far_ref[...], near_ref[...])
@@ -380,53 +414,28 @@
     owner = iota((16, lanes), 0) == iota((16, lanes), 1) // size
     ones = owner.astype(F32).astype(BF16)
     onward = (iota((Q, Q), 0) >= iota((Q, Q), 1)).astype(F32).astype(BF16)
-    left = iota((Q, 2 * size), 1) < size
     for b in range(2):
         at = slice(b * Q, (b + 1) * Q)
-        running = running_of(ld_ref[:, at])
-        decays = decay_blocks(running)
-        decay_out = spread_decays(running, size)[1]
-        products = dot_t(w_ref[at, :], r_ref[at, :])
-        sums_top, sums_low, changes = [], [], None
-        for pair in range(GROUP // 2):
-            here = slice(pair * 2 * size, (pair + 1) * 2 * size)
-            x_pair, g_pair = x_ref[at, here], g_ref[at, here]
-            none = jnp.zeros_like(g_pair)
-            top = low = None
-            for k, (pairs_top, pairs_low) in enumerate(pair_products(x_pair, g_pair)):
-                decay_top, decay_low = decays(2 * pair + k)
-                weights_top = products[0:half] * decay_top
-                weights_low = products[half:, half:] * decay_low
-                sums_top.append(jnp.sum(weights_top * pairs_top, axis=0, keepdims=True))
-                sums_low.append(jnp.sum(weights_low * pairs_low, axis=0, keepdims=True))
-                g_own = jnp.where(left, g_pair, none) if k == 0 else jnp.where(left, none, g_pair)
-                part_top = dot(weights_top.astype(BF16), g_own)
-                part_low = dot(weights_low.astype(BF16), g_own[half:])
-                top = part_top if top is None else top + part_top
-                low = part_low if low is None else low + part_low
-            out_inter = dot(r_ref[at, :], state_in[b][:, here].astype(BF16))
-            grad_inter = dot(w_ref[at, :], grad_end[b][:, here].astype(BF16)) * decay_out[:, here]
-            grad_full = jnp.concatenate([top, low], axis=0) + grad_inter
-            gi_ref[at, here] = grad_full.astype(BF16)
-            high, low = split_two(gw_ref[0, at, here].astype(F32) * out_inter - x_pair.astype(F32) * grad_full)
-            change = dot_t(ones[:, here], high.astype(BF16)) + dot_t(ones[:, here], low.astype(BF16))
-            changes = change if changes is None else changes + change
-        early, late_half = jnp.concatenate(sums_top, axis=0), jnp.concatenate(sums_low, axis=0)
-        within = changes[0:GROUP] + early + jnp.concatenate([jnp.zeros_like(late_half), late_half], axis=1)
+        decay_out = spread_decays(running_of(ld_ref[:, at]), size)[1]
+        out_inter = dot(r_ref[at, :], state_in[b].astype(BF16))
+        grad_full = gint_ref[at, :] + dot(w_ref[at, :], grad_end[b].astype(BF16)) * decay_out
+        gi_ref[at, :] = grad_full.astype(BF16)
+        high, low = split_two(gw_ref[0, at, :].astype(F32) * out_inter - x_ref[at, :].astype(F32) * grad_full)
+        change = dot_t(ones, high.astype(BF16)) + dot_t(ones, low.astype(BF16))
         cross = jnp.sum(after[b] * grad_end[b], axis=0, keepdims=True)
         crossing = jnp.sum(jnp.where(owner[0:GROUP], cross, 0.0), axis=1, keepdims=True)
-        gd_ref[:, at] = (times_ones(within, onward) + crossing) * scale
-
-
-def grads(sel, k, data, state, carried, scale, head_size, held=(), after=()):
-    inputs, grad_out, write_proj, read_proj, log_decay = data
+        gd_ref[:, at] = (times_ones(change[0:GROUP] + dot_ref[:, at], onward) + crossing) * scale
+
+
+def grads(sel, k, data, gint, dots, state, carried, scale, head_size, held=(), after=()):
+    inputs, _, write_proj, read_proj, log_decay = data
     pay, wg, part, tot = state
     rows, width = write_proj.shape
     heads = log_decay.shape[0]
     lanes = GROUP * head_size
     wide = pl.BlockSpec((rows, lanes), lambda i, s: (0, s[6 + k]))
     decays = pl.BlockSpec((GROUP, rows), lambda i, s: (s[6 + k], 0))
-    args = [inputs, grad_out, wg, write_proj, read_proj, log_decay, part, tot, *carried, pay]
+    args = [inputs, wg, write_proj, read_proj, log_decay, gint, dots, part, tot, *carried, pay]
     return pl.pallas_call(
         functools.partial(grads_kernel, scale),
         grid_spec=pltpu.PrefetchScalarGridSpec(
@@ -434,10 +443,11 @@
             grid=(1,),
             in_specs=[
                 wide,
-                wide,
                 pl.BlockSpec((1, rows, lanes), lambda i, s: (0, 0, 0)),
                 full(write_proj),
                 full(read_proj),
+                decays,
+                wide,
                 decays,
             ]
             + [full(a) for a in (part, tot, *carried, pay)]
@@ -452,17 +462,17 @@
     )(sel, *args, *held, *after)
 
 
-def join_kernel(sel, near_own, near_other, far_own, far_other, read_ref, write_ref, sems):
-    step = near_own.shape[0]
+def join_kernel(places, sel, *refs):
+    count = len(places)
+    parts, (read_ref, write_ref, sems) = refs[:count], refs[-3:]
+    step = parts[0].shape[0]
     odd = sel[5] % 2
 
-    def copies(near_ref, far_ref):
+    def copies(*outs):
         moves = []
-        for k, (part, out) in enumerate(
-            ((near_own, near_ref), (near_other, near_ref), (far_own, far_ref), (far_other, far_ref))
-        ):
-            at = pl.multiple_of((odd if k % 2 == 0 else 1 - odd) * step, step)
-            moves.append(pltpu.make_async_copy(part, out.at[pl.ds(at, step), :], sems.at[k]))
+        for k, (part, (way, back)) in enumerate(zip(parts, places)):
+            at = pl.multiple_of((1 - odd if back else odd) * step, step)
+            moves.append(pltpu.make_async_copy(part, outs[way].at[pl.ds(at, step), :], sems.at[k]))
         for move in moves:
             move.start()
         for move in moves:
@@ -470,6 +480,25 @@
 
     pl.when(sel[0] == 0)(lambda: copies(read_ref, write_ref))
     pl.when(sel[0] != 0)(lambda: copies(write_ref, read_ref))
+
+
+def join(sel, parts, places, shape, held=()):
+    count = len(parts)
+    return pl.pallas_call(
+        functools.partial(join_kernel, places),
+        grid_spec=pltpu.PrefetchScalarGridSpec(
+            num_scalar_prefetch=1,
+            grid=(1,),
+            in_specs=[ANYWHERE] * (count + len(held)),
+            out_specs=[ANYWHERE] * 2,
+            scratch_shapes=[pltpu.SemaphoreType.DMA((count,))],
+        ),
+        out_shape=[stored(shape)] * 2,
+        input_output_aliases={1 + count: 0, 2 + count: 1} if held else {},
+        compiler_params=params(),
+        cost_estimate=FREE,
+        name="join",
+    )(sel, *parts, *held)
 
 
 def swap(values, axis, mask):
@@ -519,14 +548,14 @@
     data = (inputs, grad_out, write_proj, read_proj, log_decay)
 
     if fast:
-        other = states(order[1][None], *data, head_size)
+        other = states(order[1][None], *data, head_size, False)
         got = swap(other[0], "seq", 1)
-        mine = states(order[0][None], *data, head_size)
+        mine = states(order[0][None], *data, head_size, True)
         outs = [shape_of((width + 8, lanes)), shape_of((width, lanes))]
         px, qx = call(chip_kernel, "chip", sel, (mine[0], got), outs)
         rx, sx = swap(px, "seq", 2), swap(qx, "seq", 2)
-        early = scores(*data, head_size, (px,))
-        near_own, send, pair = carry(0, sel, [rx, px], mine[0], got, (early,))
+        early, gint, dots = scores(*data, head_size, (px,))
+        near_own, send, pair = carry(0, sel, [rx, px], mine[0], got, (dots,))
         ry = swap(pair, "seq", 4)
         near_got = swap(send, "seq", 1)
         (acc,) = late(0, sel, mine, near_own, early, False, "late_near_mine")
@@ -540,28 +569,20 @@
         far_arrived = swap(far_parts[1], "head", 1)
         near_sum = near_half + near_cross
         near_rest = swap(near_sum, "head", 1)
-        held = grads(sel, 0, data, mine, (near_own, far_own), scale, head_size, (), (far_parts[1],))
+        held = grads(sel, 0, data, gint, dots, mine, (near_own, far_own), scale, head_size, (), (far_parts[1],))
         far_half = far_parts[0] + tied(far_arrived, *held)
         far_cross = swap(far_half, "head", 2)
         grad_inputs, grad_decay = grads(
-            sel, 1, data, other, (near_got, far_got), scale, head_size, held, (far_half,)
+            sel, 1, data, gint, dots, other, (near_got, far_got), scale, head_size, held, (far_half,)
         )
         far_sum = far_half + tied(far_cross, grad_decay)
         far_rest = swap(far_sum, "head", 1)
-        grad_read, grad_write = call(
-            join_kernel,
-            "join",
-            sel,
-            (near_sum, near_rest, far_sum, far_rest),
-            [shape_of((rows, width))] * 2,
-            in_specs=[ANYWHERE] * 4,
-            out_specs=[ANYWHERE] * 2,
-            scratch=[pltpu.SemaphoreType.DMA((4,))],
-        )
+        held = join(sel, (near_sum, near_rest, far_sum), ((0, 0), (0, 1), (1, 0)), (rows, width))
+        grad_read, grad_write = join(sel, (tied(far_rest, *held),), ((1, 1),), (rows, width), held)
         return grad_inputs, grad_write, grad_read, grad_decay
 
-    local_states = [states(k[None], *data, head_size) for k in order]
-    early = scores(*data, head_size, ())
+    local_states = [states(k[None], *data, head_size, False) for k in order]
+    early, gint, dots = scores(*data, head_size, ())
     carried = [[scan_over(state[0], width, bool(way)) for state in local_states] for way in (0, 1)]
     totals = []
     for way in (0, 1):
@@ -571,7 +592,7 @@
         totals.append(acc[0])
     held = ()
     for k, state in enumerate(local_states):
-        held = grads(sel, k, data, state, (carried[0][k], carried[1][k]), scale, head_size, tuple(held))
+        held = grads(sel, k, data, gint, dots, state, (carried[0][k], carried[1][k]), scale, head_size, tuple(held))
     grad_inputs, grad_decay = held
     grad_read, grad_write = lax.psum(tuple(totals), "head")
     return grad_inputs, grad_write, grad_read, grad_decay

time: 59.6 us -> 57 us (0.956)
  waiting for transfers between devices: 14 us -> 11.4 us
  Pallas kernels: 29.3 us -> 27.7 us
  starting transfers between devices: 14.6 us -> 15.7 us
    pallas_call x2, Pallas kernels: 11.4 us -> 7.64 us  [grads(): pl.pallas_call(functools.partial(grads_kernel, scale), grid_spec=pltpu.Pr...]
    ppermute x12, waiting for transfers between devices: 14 us -> 11.4 us  [swap(): return lax.ppermute(values, axis, [(i, i ^ mask) for i in range(count)])]
    pallas_call x1, Pallas kernels: 3.51 us -> 5.82 us  [scores(): pl.pallas_call(scores_kernel, grid=(rows // Q, heads // GROUP), in_specs=...]
    pallas_call x8 -> x7, Pallas kernels: 6.84 us -> 5.48 us  [call(): pl.pallas_call(body, grid_spec=pltpu.PrefetchScalarGridSpec(num_scalar_pr...]
    pallas_call x2 -> x4, Pallas kernels: 7.57 us -> 8.77 us  [the longest x2 6.24 us: states(): pl.pallas_call(loaded_kernel if loaded else state_kernel, grid_spec=pltpu...]
    ppermute x12, starting transfers between devices: 14.6 us -> 15.7 us  [swap(): return lax.ppermute(values, axis, [(i, i ^ mask) for i in range(count)])]
  transfers between devices with their start and end apart: 12 -> 12, of which waited for: 6 -> 7; matrix products, arithmetic and copies ran while one was open for 0% -> 0% of each run, Pallas kernels for 36% -> 35%
where the time goes in v4:
time: 57 us; the launch traced here: 56.8 us
  Pallas kernels  27.7 us (49%)
  starting transfers between devices  15.7 us (28%)
  waiting for transfers between devices  11.4 us (20%)
  between operations  0.93 us (2%)
  local copies, waits for them, and re-layouts  0.9 us (2%)
    ppermute x12, starting transfers between devices, swap(): return lax.ppermute(values, axis, [(i, i ^ mask) for i in range(count)])  15.7 us
    ppermute x12, waiting for transfers between devices, swap(): return lax.ppermute(values, axis, [(i, i ^ mask) for i in range(count)])  11.4 us
    pallas_call x2, Pallas kernels, grads(): pl.pallas_call(functools.partial(grads_kernel, scale), grid_spec=pltpu.Pr...  7.64 us
    pallas_call x2, Pallas kernels, states(): pl.pallas_call(loaded_kernel if loaded else state_kernel, grid_spec=pltpu...  6.24 us
    pallas_call x1, Pallas kernels, scores(): pl.pallas_call(scores_kernel, grid=(rows // Q, heads // GROUP), in_specs=...  5.82 us
    pallas_call x7, Pallas kernels, call(): pl.pallas_call(body, grid_spec=pltpu.PrefetchScalarGridSpec(num_scalar_pr...  5.48 us
    pallas_call x2, Pallas kernels, join(): pl.pallas_call(functools.partial(join_kernel, places), grid_spec=pltpu.Pr...  2.52 us
  transfers between devices with their start and end apart: 12, of which 7 were waited for; matrix products, arithmetic and copies ran while one was open for 0% of the time, Pallas kernels for 35%

profile of v4, /device:TPU:0, one launch (start us, length us, event | category | flops | bytes accessed | tf_op | source)
XLA Modules:
  0.0 56.8 jit_solution(7401887502750663230)
XLA Ops:
  0.7 3.9 %states.2 = (f32[264,512]{1,0:T(8,128)}, bf16[2,512,512]{2,1,0:T(8,128)(2,1)}, f32[256,512]{1,0:T(8,128)}, f32[16,512]{1,0:T(8,128)}) custom-call(s32[1]{0:T(128)} %bitcast.5.sel, bf16[512,1024]{1,0:T(8,128)(2,1)} %x_ref.5, bf16[512,1024]{1,0:T(8,128)(2,1)} %g_ref.1, bf16[512,128]{1,0:T(8,128)(2,1)} %w_ref.5, bf16[512,128]{1,0:T(8,128)(2,1)} %r_ref.5, ...), custom_call_target="tpu_custom_call" | custom-call | flops 1000 | bytes 1000 | tf_op jit(solution)/shard_map/states/pallas_call | solution.py:157
  4.6 0.5 collective-permute-start
  5.2 2.3 %states.3 = (f32[264,512]{1,0:T(8,128)S(1)}, bf16[2,512,512]{2,1,0:T(8,128)(2,1)}, f32[256,512]{1,0:T(8,128)}, f32[16,512]{1,0:T(8,128)}) custom-call(s32[1]{0:T(128)} %bitcast.2.sel, bf16[512,1024]{1,0:T(8,128)(2,1)S(1)} %copy-done, bf16[512,1024]{1,0:T(8,128)(2,1)S(1)} %copy-done.2, bf16[512,128]{1,0:T(8,128)(2,1)S(1)} %copy-done.7, ...), custom_call_target="tpu_custom_call" | custom-call | flops 1000 | bytes 1000 | tf_op jit(solution)/shard_map/states/pallas_call | solution.py:157
  7.6 0.7 %chip.1 = (f32[136,512]{1,0:T(8,128)S(1)}, f32[128,512]{1,0:T(8,128)S(1)}) custom-call(s32[8]{0:T(128)S(1)} %stack.29.s.sel, f32[264,512]{1,0:T(8,128)S(1)} %get-tuple-element.38.refs_0_.refs_2_.refs_4_.refs_3_.refs_5_.pay_ref, f32[264,512]{1,0:T(8,128)S(1)} %collective-permute-done.refs_1_.refs_3_.refs_5_.refs_4_.refs_6_), custom_call_target="tpu_custom_call" | custom-call | flops 1000 | bytes 1000 | tf_op jit(solution)/shard_map/chip/pallas_call | solution.py:206
  8.3 2.6 %collective-permute-start.1 = (f32[136,512]{1,0:T(8,128)S(1)}, f32[136,512]{1,0:T(8,128)S(1)}, u32[]{:S(2)}, u32[]{:S(2)}) collective-permute-start(f32[136,512]{1,0:T(8,128)S(1)} %get-tuple-element.40.rest_0_.refs_1_), channel_id=1, source_target_pairs={{0,8},{4,12},{8,0},{12,4},{16,24},{20,28},{24,16},{28,20},{1,9},{5... | collective-permute-start | bytes 835592 | tf_op jit(solution)/shard_map/ppermute | solution.py:506
  10.9 5.8 %scores.1 = (f32[2,512,128]{2,1,0:T(8,128)S(1)}, f32[512,1024]{1,0:T(8,128)}, f32[16,512]{1,0:T(8,128)}) custom-call(bf16[512,1024]{1,0:T(8,128)(2,1)S(1)} %copy-done, bf16[512,1024]{1,0:T(8,128)(2,1)S(1)} %copy-done.2, bf16[512,128]{1,0:T(8,128)(2,1)S(1)} %copy-done.7, bf16[512,128]{1,0:T(8,128)(2,1)S(1)} %copy-done.8, f32[16,512]{1,0:T(8,128)S(1)} %copy-done.9, ...), custom_call_target="tpu_custom_call" | custom-call | flops 1000 | bytes 1000 | tf_op jit(solution)/shard_map/scores/pallas_call | solution.py:382
  16.7 1.5 %collective-permute-done.1.refs_0_ = f32[136,512]{1,0:T(8,128)S(1)} collective-permute-done((f32[136,512]{1,0:T(8,128)S(1)}, f32[136,512]{1,0:T(8,128)S(1)}, u32[]{:S(2)}, u32[]{:S(2)}) %collective-permute-start.1) | collective-permute-done | bytes 278560 | tf_op jit(solution)/shard_map/ppermute | solution.py:506
  18.2 0.8 %copy-done.12 = f32[16,512]{1,0:T(8,128)S(1)} copy-done((f32[16,512]{1,0:T(8,128)S(1)}, f32[16,512]{1,0:T(8,128)}, u32[]{:S(2)}) %copy-start.12) | copy-done | bytes 32792
  19.0 0.7 %carry_near.1 = (f32[128,512]{1,0:T(8,128)S(1)}, f32[128,512]{1,0:T(8,128)S(1)}, f32[128,512]{1,0:T(8,128)S(1)}) custom-call(s32[8]{0:T(128)S(1)} %stack.29.s.sel, f32[136,512]{1,0:T(8,128)S(1)} %collective-permute-done.1.refs_0_, f32[136,512]{1,0:T(8,128)S(1)} %get-tuple-element.40.rest_0_.refs_1_, ...), custom_call_target="tpu_custom_call" | custom-call | flops 1000 | bytes 1000 | tf_op jit(solution)/shard_map/carry_near/pallas_call | solution.py:206
  19.7 1.8 %collective-permute-start.3 = (f32[128,512]{1,0:T(8,128)S(1)}, f32[128,512]{1,0:T(8,128)S(1)}, u32[]{:S(2)}, u32[]{:S(2)}) collective-permute-start(f32[128,512]{1,0:T(8,128)S(1)} %get-tuple-element.46), channel_id=1, source_target_pairs={{0,8},{4,12},{8,0},{12,4},{16,24},{20,28},{24,16},{28,20},{1,9},{5... | collective-permute-start | bytes 786440 | tf_op jit(solution)/shard_map/ppermute | solution.py:506
  21.5 1.5 %collective-permute-start.4 = (f32[128,512]{1,0:T(8,128)S(1)}, f32[128,512]{1,0:T(8,128)S(1)}, u32[]{:S(2)}, u32[]{:S(2)}) collective-permute-start(f32[128,512]{1,0:T(8,128)S(1)} %get-tuple-element.47), channel_id=1, source_target_pairs={{0,16},{4,20},{8,24},{12,28},{16,0},{20,4},{24,8},{28,12},{1,17},{... | collective-permute-start | bytes 786440 | tf_op jit(solution)/shard_map/ppermute | solution.py:506
  23.1 0.9 %late_near_mine.1 = f32[512,128]{1,0:T(8,128)S(1)} custom-call(s32[8]{0:T(128)S(1)} %stack.29.s.sel, bf16[2,512,512]{2,1,0:T(8,128)(2,1)S(1)} %copy-done.1, f32[128,512]{1,0:T(8,128)S(1)} %get-tuple-element.49.refs_1_.near_ref, f32[256,512]{1,0:T(8,128)S(1)} %copy-done.6, f32[16,512]{1,0:T(8,128)S(1)} %copy-done.11, f32[2,512,128]{2,1,0:T(8,128)S(1)} %get-tuple-element.52.refs_4_), custom_call_target="tpu_custom_call" | custom-call | flops 1000 | bytes 1000 | tf_op jit(solution)/shard_map/late_near_mine/pallas_call | solution.py:206
  24.0 0.9 %late_near_other.1 = (f32[256,128]{1,0:T(8,128)S(1)}, f32[256,128]{1,0:T(8,128)S(1)}) custom-call(s32[8]{0:T(128)S(1)} %stack.29.s.sel, bf16[2,512,512]{2,1,0:T(8,128)(2,1)S(1)} %copy-done.3, f32[128,512]{1,0:T(8,128)S(1)} %collective-permute-done.2.refs_1_.near_ref, f32[256,512]{1,0:T(8,128)S(1)} %copy-done.5, f32[16,512]{1,0:T(8,128)S(1)} %copy-done.10, ...), custom_call_target="tpu_custom_call" | custom-call | flops 1000 | bytes 1000 | tf_op jit(solution)/shard_map/late_near_other/pallas_call | solution.py:206
  24.9 1.6 %collective-permute-start.5 = (f32[256,128]{1,0:T(8,128)S(1)}, f32[256,128]{1,0:T(8,128)S(1)}, u32[]{:S(2)}, u32[]{:S(2)}) collective-permute-start(f32[256,128]{1,0:T(8,128)S(1)} %get-tuple-element.54), channel_id=1, source_target_pairs={{0,1},{1,0},{2,3},{3,2},{4,5},{5,4},{6,7},{7,6},{8,9},{9,8},{10,11... | collective-permute-start | bytes 393224 | tf_op jit(solution)/shard_map/ppermute | solution.py:506
  26.5 3.7 %collective-permute-done.5 = f32[256,128]{1,0:T(8,128)S(1)} collective-permute-done((f32[256,128]{1,0:T(8,128)S(1)}, f32[256,128]{1,0:T(8,128)S(1)}, u32[]{:S(2)}, u32[]{:S(2)}) %collective-permute-start.5) | collective-permute-done | bytes 131104 | tf_op jit(solution)/shard_map/ppermute | solution.py:506
  30.3 0.6 %carry_far.1 = (f32[128,512]{1,0:T(8,128)S(1)}, f32[128,512]{1,0:T(8,128)S(1)}) custom-call(s32[8]{0:T(128)S(1)} %stack.29.s.sel, f32[136,512]{1,0:T(8,128)S(1)} %collective-permute-done.1.refs_0_, f32[128,512]{1,0:T(8,128)S(1)} %collective-permute-done.3.refs_1_, f32[128,512]{1,0:T(8,128)S(1)} %collective-permute-done.4.refs_2_, ...), custom_call_target="tpu_custom_call" | custom-call | flops 1000 | bytes 1000 | tf_op jit(solution)/shard_map/carry_far/pallas_call | solution.py:206
  31.0 0.9 %late_far_mine.1 = f32[512,128]{1,0:T(8,128)S(1)} custom-call(s32[8]{0:T(128)S(1)} %stack.29.s.sel, bf16[2,512,512]{2,1,0:T(8,128)(2,1)S(1)} %copy-done.1, f32[128,512]{1,0:T(8,128)S(1)} %get-tuple-element.56.refs_1_.far_ref, f32[256,512]{1,0:T(8,128)S(1)} %copy-done.6, f32[16,512]{1,0:T(8,128)S(1)} %copy-done.11, f32[2,512,128]{2,1,0:T(8,128)S(1)} %get-tuple-element.52.refs_4_), custom_call_target="tpu_custom_call" | custom-call | flops 1000 | bytes 1000 | tf_op jit(solution)/shard_map/late_far_mine/pallas_call | solution.py:206
  31.9 0.6 %collective-permute-done.6.refs_1_.far_ref = f32[128,512]{1,0:T(8,128)S(1)} collective-permute-done((f32[128,512]{1,0:T(8,128)S(1)}, f32[128,512]{1,0:T(8,128)S(1)}, u32[]{:S(2)}, u32[]{:S(2)}) %collective-permute-start.6) | collective-permute-done | bytes 262176 | tf_op jit(solution)/shard_map/ppermute | solution.py:506
  32.5 0.9 %late_far_other.1 = (f32[256,128]{1,0:T(8,128)S(1)}, f32[256,128]{1,0:T(8,128)S(1)}) custom-call(s32[8]{0:T(128)S(1)} %stack.29.s.sel, bf16[2,512,512]{2,1,0:T(8,128)(2,1)S(1)} %copy-done.3, f32[128,512]{1,0:T(8,128)S(1)} %collective-permute-done.6.refs_1_.far_ref, f32[256,512]{1,0:T(8,128)S(1)} %copy-done.5, f32[16,512]{1,0:T(8,128)S(1)} %copy-done.10, ...), custom_call_target="tpu_custom_call" | custom-call | flops 1000 | bytes 1000 | tf_op jit(solution)/shard_map/late_far_other/pallas_call | solution.py:206
  33.4 1.7 %collective-permute-start.7 = (f32[256,128]{1,0:T(8,128)S(1)}, f32[256,128]{1,0:T(8,128)S(1)}, u32[]{:S(2)}, u32[]{:S(2)}) collective-permute-start(f32[256,128]{1,0:T(8,128)S(1)} %get-tuple-element.57.rest_0_), channel_id=1, source_target_pairs={{0,1},{1,0},{2,3},{3,2},{4,5},{5,4},{6,7},{7,6},{8,9},{9,8},{10,11... | collective-permute-start | bytes 393224 | tf_op jit(solution)/shard_map/ppermute | solution.py:506
  35.1 2.6 %collective-permute-start.10 = (f32[256,128]{1,0:T(8,128)S(1)}, f32[256,128]{1,0:T(8,128)S(1)}, u32[]{:S(2)}, u32[]{:S(2)}) collective-permute-start(f32[256,128]{1,0:T(8,128)S(1)} %add.27.refs_7_), channel_id=1, source_target_pairs={{0,2},{1,3},{2,0},{3,1},{4,6},{5,7},{6,4},{7,5},{8,10},{9,11},{10,... | collective-permute-start | bytes 393224 | tf_op jit(solution)/shard_map/ppermute | solution.py:506
  37.7 3.3 %grads.2 = (bf16[512,1024]{1,0:T(8,128)(2,1)}, f32[16,512]{1,0:T(8,128)}) custom-call(s32[8]{0:T(128)S(1)} %stack.29.s.sel, bf16[512,1024]{1,0:T(8,128)(2,1)S(1)} %copy-done, bf16[2,512,512]{2,1,0:T(8,128)(2,1)S(1)} %copy-done.1, bf16[512,128]{1,0:T(8,128)(2,1)S(1)} %copy-done.7, bf16[512,128]{1,0:T(8,128)(2,1)S(1)} %copy-done.8, f32[16,512]{1,0:T(8,128)S(1)} %copy-done.9, ...), custom_call_target="tpu_custom_call" | custom-call | flops 1000 | bytes 1000 | tf_op jit(solution)/shard_map/grads/pallas_call | solution.py:439
  40.9 0.4 collective-permute-done.7
  41.4 1.1 %collective-permute-start.8 = (f32[256,128]{1,0:T(8,128)S(1)}, f32[256,128]{1,0:T(8,128)S(1)}, u32[]{:S(2)}, u32[]{:S(2)}) collective-permute-start(f32[256,128]{1,0:T(8,128)S(1)} %add.28.rest_2_), channel_id=1, source_target_pairs={{0,2},{1,3},{2,0},{3,1},{4,6},{5,7},{6,4},{7,5},{8,10},{9,11},{10,... | collective-permute-start | bytes 393224 | tf_op jit(solution)/shard_map/ppermute | solution.py:506
  42.5 1.6 %collective-permute-done.10 = f32[256,128]{1,0:T(8,128)S(1)} collective-permute-done((f32[256,128]{1,0:T(8,128)S(1)}, f32[256,128]{1,0:T(8,128)S(1)}, u32[]{:S(2)}, u32[]{:S(2)}) %collective-permute-start.10) | collective-permute-done | bytes 131104 | tf_op jit(solution)/shard_map/ppermute | solution.py:506
  44.1 2.0 %collective-permute-start.11 = (f32[256,128]{1,0:T(8,128)S(1)}, f32[256,128]{1,0:T(8,128)S(1)}, u32[]{:S(2)}, u32[]{:S(2)}) collective-permute-start(f32[256,128]{1,0:T(8,128)S(1)} %add.30.refs_0_), channel_id=1, source_target_pairs={{0,1},{1,0},{2,3},{3,2},{4,5},{5,4},{6,7},{7,6},{8,9},{9,8},{10,11... | collective-permute-start | bytes 393224 | tf_op jit(solution)/shard_map/ppermute | solution.py:506
  46.1 4.4 %grads.3 = (bf16[512,1024]{1,0:T(8,128)(2,1)}, f32[16,512]{1,0:T(8,128)}) custom-call(s32[8]{0:T(128)S(1)} %stack.29.s.sel, bf16[512,1024]{1,0:T(8,128)(2,1)S(1)} %copy-done, bf16[2,512,512]{2,1,0:T(8,128)(2,1)S(1)} %copy-done.3, bf16[512,128]{1,0:T(8,128)(2,1)S(1)} %copy-done.7, ...), custom_call_target="tpu_custom_call", output_to_operand_aliasing={{0}: (13, {}), {1}: (14, {})} | custom-call | flops 1000 | bytes 1000 | tf_op jit(solution)/shard_map/grads/pallas_call | solution.py:439
  50.5 0.1 collective-permute-start.9
  50.7 0.3 collective-permute-done.11.refs_1_
  50.9 1.3 %join.2 = (f32[512,128]{1,0:T(8,128)}, f32[512,128]{1,0:T(8,128)}) custom-call(s32[8]{0:T(128)S(1)} %stack.29.s.sel, f32[256,128]{1,0:T(8,128)S(1)} %add.30.refs_0_, f32[256,128]{1,0:T(8,128)S(1)} %collective-permute-done.11.refs_1_, f32[256,128]{1,0:T(8,128)S(1)} %add.29.refs_2_), custom_call_target="tpu_custom_call" | custom-call | flops 1000 | bytes 1000 | tf_op jit(solution)/shard_map/join/pallas_call | solution.py:487
  52.2 3.3 %collective-permute-done.9.refs_0_ = f32[256,128]{1,0:T(8,128)S(1)} collective-permute-done((f32[256,128]{1,0:T(8,128)S(1)}, f32[256,128]{1,0:T(8,128)S(1)}, u32[]{:S(2)}, u32[]{:S(2)}) %collective-permute-start.9) | collective-permute-done | bytes 131104 | tf_op jit(solution)/shard_map/ppermute | solution.py:506
  55.6 1.2 %join.3 = (f32[512,128]{1,0:T(8,128)}, f32[512,128]{1,0:T(8,128)}) custom-call(s32[8]{0:T(128)S(1)} %stack.29.s.sel, f32[256,128]{1,0:T(8,128)S(1)} %collective-permute-done.9.refs_0_, f32[512,128]{1,0:T(8,128)} %get-tuple-element.65.refs_1_, f32[512,128]{1,0:T(8,128)} %get-tuple-element.66.refs_2_), custom_call_target="tpu_custom_call", output_to_operand_aliasing={{0}: (2, {}), {1}: (3, {})} | custom-call | flops 1000 | bytes 1000 | tf_op jit(solution)/shard_map/join/pallas_call | solution.py:487
  (37 shorter events, 0.4 us)
Async XLA Ops:
  0.6 4.5 %copy-start = (bf16[512,1024]{1,0:T(8,128)(2,1)S(1)}, bf16[512,1024]{1,0:T(8,128)(2,1)}, u32[]{:S(2)}) copy-start(bf16[512,1024]{1,0:T(8,128)(2,1)} %x_ref.5) | copy-start | bytes 3145732
  0.6 4.5 %copy-start.2 = (bf16[512,1024]{1,0:T(8,128)(2,1)S(1)}, bf16[512,1024]{1,0:T(8,128)(2,1)}, u32[]{:S(2)}) copy-start(bf16[512,1024]{1,0:T(8,128)(2,1)} %g_ref.1) | copy-start | bytes 3145732
  0.7 4.5 %copy-start.7 = (bf16[512,128]{1,0:T(8,128)(2,1)S(1)}, bf16[512,128]{1,0:T(8,128)(2,1)}, u32[]{:S(2)}) copy-start(bf16[512,128]{1,0:T(8,128)(2,1)} %w_ref.5) | copy-start | bytes 393220
  0.7 4.5 %copy-start.8 = (bf16[512,128]{1,0:T(8,128)(2,1)S(1)}, bf16[512,128]{1,0:T(8,128)(2,1)}, u32[]{:S(2)}) copy-start(bf16[512,128]{1,0:T(8,128)(2,1)} %r_ref.5) | copy-start | bytes 393220
  0.7 4.5 %copy-start.9 = (f32[16,512]{1,0:T(8,128)S(1)}, f32[16,512]{1,0:T(8,128)}, u32[]{:S(2)}) copy-start(f32[16,512]{1,0:T(8,128)} %ld_ref.5) | copy-start | bytes 98308
  4.6 3.0 %collective-permute-start = (f32[264,512]{1,0:T(8,128)}, f32[264,512]{1,0:T(8,128)S(1)}, u32[]{:S(2)}, u32[]{:S(2)}) collective-permute-start(f32[264,512]{1,0:T(8,128)} %get-tuple-element.39.pay_ref), channel_id=1, source_target_pairs={{0,4},{4,0},{8,12},{12,8},{16,20},{20,16},{24,28},{28,24},{1,5},{5... | collective-permute-start | bytes 1622024 | tf_op jit(solution)/shard_map/ppermute | solution.py:506
  8.3 14.8 %copy-start.1 = (bf16[2,512,512]{2,1,0:T(8,128)(2,1)S(1)}, bf16[2,512,512]{2,1,0:T(8,128)(2,1)}, u32[]{:S(2)}) copy-start(bf16[2,512,512]{2,1,0:T(8,128)(2,1)} %get-tuple-element.48.refs_0_.gw_ref) | copy-start | bytes 3145732
  8.3 14.8 %copy-start.6 = (f32[256,512]{1,0:T(8,128)S(1)}, f32[256,512]{1,0:T(8,128)}, u32[]{:S(2)}) copy-start(f32[256,512]{1,0:T(8,128)} %get-tuple-element.50.refs_2_.part_ref) | copy-start | bytes 1572868
  8.3 14.7 %copy-start.11 = (f32[16,512]{1,0:T(8,128)S(1)}, f32[16,512]{1,0:T(8,128)}, u32[]{:S(2)}) copy-start(f32[16,512]{1,0:T(8,128)} %get-tuple-element.51.refs_3_.tot_ref) | copy-start | bytes 98308
  8.3 9.9 %collective-permute-start.1 = (f32[136,512]{1,0:T(8,128)S(1)}, f32[136,512]{1,0:T(8,128)S(1)}, u32[]{:S(2)}, u32[]{:S(2)}) collective-permute-start(f32[136,512]{1,0:T(8,128)S(1)} %get-tuple-element.40.rest_0_.refs_1_), channel_id=1, source_target_pairs={{0,8},{4,12},{8,0},{12,4},{16,24},{20,28},{24,16},{28,20},{1,9},{5... | collective-permute-start | bytes 835592 | tf_op jit(solution)/shard_map/ppermute | solution.py:506
  18.2 0.8 %copy-start.12 = (f32[16,512]{1,0:T(8,128)S(1)}, f32[16,512]{1,0:T(8,128)}, u32[]{:S(2)}) copy-start(f32[16,512]{1,0:T(8,128)} %get-tuple-element.42.refs_6_.dot_ref) | copy-start | bytes 98308
  19.0 5.0 %copy-start.3 = (bf16[2,512,512]{2,1,0:T(8,128)(2,1)S(1)}, bf16[2,512,512]{2,1,0:T(8,128)(2,1)}, u32[]{:S(2)}) copy-start(bf16[2,512,512]{2,1,0:T(8,128)(2,1)} %get-tuple-element.37.refs_0_.gw_ref) | copy-start | bytes 3145732
  19.0 5.0 %copy-start.5 = (f32[256,512]{1,0:T(8,128)S(1)}, f32[256,512]{1,0:T(8,128)}, u32[]{:S(2)}) copy-start(f32[256,512]{1,0:T(8,128)} %get-tuple-element.43.refs_2_.part_ref) | copy-start | bytes 1572868
  19.0 5.0 %copy-start.10 = (f32[16,512]{1,0:T(8,128)S(1)}, f32[16,512]{1,0:T(8,128)}, u32[]{:S(2)}) copy-start(f32[16,512]{1,0:T(8,128)} %get-tuple-element.44.refs_3_.tot_ref) | copy-start | bytes 98308
  19.7 4.3 %collective-permute-start.2 = (f32[128,512]{1,0:T(8,128)S(1)}, f32[128,512]{1,0:T(8,128)S(1)}, u32[]{:S(2)}, u32[]{:S(2)}) collective-permute-start(f32[128,512]{1,0:T(8,128)S(1)} %get-tuple-element.45), channel_id=1, source_target_pairs={{0,4},{4,0},{8,12},{12,8},{16,20},{20,16},{24,28},{28,24},{1,5},{5... | collective-permute-start | bytes 786440 | tf_op jit(solution)/shard_map/ppermute | solution.py:506
  19.7 10.5 %collective-permute-start.3 = (f32[128,512]{1,0:T(8,128)S(1)}, f32[128,512]{1,0:T(8,128)S(1)}, u32[]{:S(2)}, u32[]{:S(2)}) collective-permute-start(f32[128,512]{1,0:T(8,128)S(1)} %get-tuple-element.46), channel_id=1, source_target_pairs={{0,8},{4,12},{8,0},{12,4},{16,24},{20,28},{24,16},{28,20},{1,9},{5... | collective-permute-start | bytes 786440 | tf_op jit(solution)/shard_map/ppermute | solution.py:506
  21.5 8.7 %collective-permute-start.4 = (f32[128,512]{1,0:T(8,128)S(1)}, f32[128,512]{1,0:T(8,128)S(1)}, u32[]{:S(2)}, u32[]{:S(2)}) collective-permute-start(f32[128,512]{1,0:T(8,128)S(1)} %get-tuple-element.47), channel_id=1, source_target_pairs={{0,16},{4,20},{8,24},{12,28},{16,0},{20,4},{24,8},{28,12},{1,17},{... | collective-permute-start | bytes 786440 | tf_op jit(solution)/shard_map/ppermute | solution.py:506
  24.9 5.3 %collective-permute-start.5 = (f32[256,128]{1,0:T(8,128)S(1)}, f32[256,128]{1,0:T(8,128)S(1)}, u32[]{:S(2)}, u32[]{:S(2)}) collective-permute-start(f32[256,128]{1,0:T(8,128)S(1)} %get-tuple-element.54), channel_id=1, source_target_pairs={{0,1},{1,0},{2,3},{3,2},{4,5},{5,4},{6,7},{7,6},{8,9},{9,8},{10,11... | collective-permute-start | bytes 393224 | tf_op jit(solution)/shard_map/ppermute | solution.py:506
  30.9 1.6 %collective-permute-start.6 = (f32[128,512]{1,0:T(8,128)S(1)}, f32[128,512]{1,0:T(8,128)S(1)}, u32[]{:S(2)}, u32[]{:S(2)}) collective-permute-start(f32[128,512]{1,0:T(8,128)S(1)} %get-tuple-element.55), channel_id=1, source_target_pairs={{0,4},{4,0},{8,12},{12,8},{16,20},{20,16},{24,28},{28,24},{1,5},{5... | collective-permute-start | bytes 786440 | tf_op jit(solution)/shard_map/ppermute | solution.py:506
  31.0 6.7 %copy-start.4 = (f32[512,1024]{1,0:T(8,128)S(1)}, f32[512,1024]{1,0:T(8,128)}, u32[]{:S(2)}) copy-start(f32[512,1024]{1,0:T(8,128)} %get-tuple-element.41.gint_ref) | copy-start | bytes 6291460
  33.4 7.9 %collective-permute-start.7 = (f32[256,128]{1,0:T(8,128)S(1)}, f32[256,128]{1,0:T(8,128)S(1)}, u32[]{:S(2)}, u32[]{:S(2)}) collective-permute-start(f32[256,128]{1,0:T(8,128)S(1)} %get-tuple-element.57.rest_0_), channel_id=1, source_target_pairs={{0,1},{1,0},{2,3},{3,2},{4,5},{5,4},{6,7},{7,6},{8,9},{9,8},{10,11... | collective-permute-start | bytes 393224 | tf_op jit(solution)/shard_map/ppermute | solution.py:506
  35.1 9.0 %collective-permute-start.10 = (f32[256,128]{1,0:T(8,128)S(1)}, f32[256,128]{1,0:T(8,128)S(1)}, u32[]{:S(2)}, u32[]{:S(2)}) collective-permute-start(f32[256,128]{1,0:T(8,128)S(1)} %add.27.refs_7_), channel_id=1, source_target_pairs={{0,2},{1,3},{2,0},{3,1},{4,6},{5,7},{6,4},{7,5},{8,10},{9,11},{10,... | collective-permute-start | bytes 393224 | tf_op jit(solution)/shard_map/ppermute | solution.py:506
  41.4 9.1 %collective-permute-start.8 = (f32[256,128]{1,0:T(8,128)S(1)}, f32[256,128]{1,0:T(8,128)S(1)}, u32[]{:S(2)}, u32[]{:S(2)}) collective-permute-start(f32[256,128]{1,0:T(8,128)S(1)} %add.28.rest_2_), channel_id=1, source_target_pairs={{0,2},{1,3},{2,0},{3,1},{4,6},{5,7},{6,4},{7,5},{8,10},{9,11},{10,... | collective-permute-start | bytes 393224 | tf_op jit(solution)/shard_map/ppermute | solution.py:506
  44.1 6.8 %collective-permute-start.11 = (f32[256,128]{1,0:T(8,128)S(1)}, f32[256,128]{1,0:T(8,128)S(1)}, u32[]{:S(2)}, u32[]{:S(2)}) collective-permute-start(f32[256,128]{1,0:T(8,128)S(1)} %add.30.refs_0_), channel_id=1, source_target_pairs={{0,1},{1,0},{2,3},{3,2},{4,5},{5,4},{6,7},{7,6},{8,9},{9,8},{10,11... | collective-permute-start | bytes 393224 | tf_op jit(solution)/shard_map/ppermute | solution.py:506
  50.5 5.0 %collective-permute-start.9 = (f32[256,128]{1,0:T(8,128)S(1)}, f32[256,128]{1,0:T(8,128)S(1)}, u32[]{:S(2)}, u32[]{:S(2)}) collective-permute-start(f32[256,128]{1,0:T(8,128)S(1)} %add.29.refs_2_), channel_id=1, source_target_pairs={{0,1},{1,0},{2,3},{3,2},{4,5},{5,4},{6,7},{7,6},{8,9},{9,8},{10,11... | collective-permute-start | bytes 393224 | tf_op jit(solution)/shard_map/ppermute | solution.py:506

commit v5 on v4

--- a/solution.py
+++ b/solution.py
@@ -555,7 +555,7 @@
         px, qx = call(chip_kernel, "chip", sel, (mine[0], got), outs)
         rx, sx = swap(px, "seq", 2), swap(qx, "seq", 2)
         early, gint, dots = scores(*data, head_size, (px,))
-        near_own, send, pair = carry(0, sel, [rx, px], mine[0], got, (dots,))
+        near_own, send, pair = carry(0, sel, [rx, px], mine[0], got, (far_off(gint),))
         ry = swap(pair, "seq", 4)
         near_got = swap(send, "seq", 1)
         (acc,) = late(0, sel, mine, near_own, early, False, "late_near_mine")

time: 57 us -> 56.2 us (0.986)
  local copies, waits for them, and re-layouts: 0.9 us -> 0.15 us
    unnamed x26, local copies, waits for them, and re-layouts: 0.81 us -> 0.06 us
where the time goes in v5:
time: 56.2 us; the launch traced here: 56 us
  Pallas kernels  27.7 us (49%)
  starting transfers between devices  15.7 us (28%)
  waiting for transfers between devices  11.4 us (20%)
  between operations  0.94 us (2%)
    ppermute x12, starting transfers between devices, swap(): return lax.ppermute(values, axis, [(i, i ^ mask) for i in range(count)])  15.7 us
    ppermute x12, waiting for transfers between devices, swap(): return lax.ppermute(values, axis, [(i, i ^ mask) for i in range(count)])  11.4 us
    pallas_call x2, Pallas kernels, grads(): pl.pallas_call(functools.partial(grads_kernel, scale), grid_spec=pltpu.Pr...  7.64 us
    pallas_call x2, Pallas kernels, states(): pl.pallas_call(loaded_kernel if loaded else state_kernel, grid_spec=pltpu...  6.24 us
    pallas_call x1, Pallas kernels, scores(): pl.pallas_call(scores_kernel, grid=(rows // Q, heads // GROUP), in_specs=...  5.83 us
    pallas_call x7, Pallas kernels, call(): pl.pallas_call(body, grid_spec=pltpu.PrefetchScalarGridSpec(num_scalar_pr...  5.47 us
    pallas_call x2, Pallas kernels, join(): pl.pallas_call(functools.partial(join_kernel, places), grid_spec=pltpu.Pr...  2.52 us
  transfers between devices with their start and end apart: 12, of which 7 were waited for; matrix products, arithmetic and copies ran while one was open for 0% of the time, Pallas kernels for 35%

profile of v5, /device:TPU:0, one launch (start us, length us, event | category | flops | bytes accessed | tf_op | source)
XLA Modules:
  0.0 56.0 jit_solution(4295237794292528996)
XLA Ops:
  0.7 3.9 %states.2 = (f32[264,512]{1,0:T(8,128)}, bf16[2,512,512]{2,1,0:T(8,128)(2,1)}, f32[256,512]{1,0:T(8,128)}, f32[16,512]{1,0:T(8,128)}) custom-call(s32[1]{0:T(128)} %bitcast.5.sel, bf16[512,1024]{1,0:T(8,128)(2,1)} %x_ref.5, bf16[512,1024]{1,0:T(8,128)(2,1)} %g_ref.1, bf16[512,128]{1,0:T(8,128)(2,1)} %w_ref.5, bf16[512,128]{1,0:T(8,128)(2,1)} %r_ref.5, ...), custom_call_target="tpu_custom_call" | custom-call | flops 1000 | bytes 1000 | tf_op jit(solution)/shard_map/states/pallas_call | solution.py:157
  4.6 0.5 collective-permute-start
  5.2 2.3 %states.3 = (f32[264,512]{1,0:T(8,128)S(1)}, bf16[2,512,512]{2,1,0:T(8,128)(2,1)}, f32[256,512]{1,0:T(8,128)}, f32[16,512]{1,0:T(8,128)}) custom-call(s32[1]{0:T(128)} %bitcast.2.sel, bf16[512,1024]{1,0:T(8,128)(2,1)S(1)} %copy-done, bf16[512,1024]{1,0:T(8,128)(2,1)S(1)} %copy-done.3, bf16[512,128]{1,0:T(8,128)(2,1)S(1)} %copy-done.7, ...), custom_call_target="tpu_custom_call" | custom-call | flops 1000 | bytes 1000 | tf_op jit(solution)/shard_map/states/pallas_call | solution.py:157
  7.6 0.1 stack.29.s.sel
  7.6 0.7 %chip.1 = (f32[136,512]{1,0:T(8,128)S(1)}, f32[128,512]{1,0:T(8,128)S(1)}) custom-call(s32[8]{0:T(128)S(1)} %stack.29.s.sel, f32[264,512]{1,0:T(8,128)S(1)} %get-tuple-element.38.refs_0_.refs_2_.refs_4_.refs_3_.refs_5_.pay_ref, f32[264,512]{1,0:T(8,128)S(1)} %collective-permute-done.refs_1_.refs_3_.refs_5_.refs_4_.refs_6_), custom_call_target="tpu_custom_call" | custom-call | flops 1000 | bytes 1000 | tf_op jit(solution)/shard_map/chip/pallas_call | solution.py:206
  8.3 2.6 %collective-permute-start.1 = (f32[136,512]{1,0:T(8,128)S(1)}, f32[136,512]{1,0:T(8,128)S(1)}, u32[]{:S(2)}, u32[]{:S(2)}) collective-permute-start(f32[136,512]{1,0:T(8,128)S(1)} %get-tuple-element.40.rest_0_.refs_1_), channel_id=1, source_target_pairs={{0,8},{4,12},{8,0},{12,4},{16,24},{20,28},{24,16},{28,20},{1,9},{5... | collective-permute-start | bytes 835592 | tf_op jit(solution)/shard_map/ppermute | solution.py:506
  10.9 5.8 %scores.1 = (f32[2,512,128]{2,1,0:T(8,128)S(1)}, f32[512,1024]{1,0:T(8,128)}, f32[16,512]{1,0:T(8,128)}) custom-call(bf16[512,1024]{1,0:T(8,128)(2,1)S(1)} %copy-done, bf16[512,1024]{1,0:T(8,128)(2,1)S(1)} %copy-done.3, bf16[512,128]{1,0:T(8,128)(2,1)S(1)} %copy-done.7, bf16[512,128]{1,0:T(8,128)(2,1)S(1)} %copy-done.8, f32[16,512]{1,0:T(8,128)S(1)} %copy-done.9, ...), custom_call_target="tpu_custom_call" | custom-call | flops 1000 | bytes 1000 | tf_op jit(solution)/shard_map/scores/pallas_call | solution.py:382
  16.7 1.5 %collective-permute-done.1.refs_0_ = f32[136,512]{1,0:T(8,128)S(1)} collective-permute-done((f32[136,512]{1,0:T(8,128)S(1)}, f32[136,512]{1,0:T(8,128)S(1)}, u32[]{:S(2)}, u32[]{:S(2)}) %collective-permute-start.1) | collective-permute-done | bytes 278560 | tf_op jit(solution)/shard_map/ppermute | solution.py:506
  18.2 0.7 %carry_near.1 = (f32[128,512]{1,0:T(8,128)S(1)}, f32[128,512]{1,0:T(8,128)S(1)}, f32[128,512]{1,0:T(8,128)S(1)}) custom-call(s32[8]{0:T(128)S(1)} %stack.29.s.sel, f32[136,512]{1,0:T(8,128)S(1)} %collective-permute-done.1.refs_0_, f32[136,512]{1,0:T(8,128)S(1)} %get-tuple-element.40.rest_0_.refs_1_, ...), custom_call_target="tpu_custom_call" | custom-call | flops 1000 | bytes 1000 | tf_op jit(solution)/shard_map/carry_near/pallas_call | solution.py:206
  19.0 1.8 %collective-permute-start.3 = (f32[128,512]{1,0:T(8,128)S(1)}, f32[128,512]{1,0:T(8,128)S(1)}, u32[]{:S(2)}, u32[]{:S(2)}) collective-permute-start(f32[128,512]{1,0:T(8,128)S(1)} %get-tuple-element.46), channel_id=1, source_target_pairs={{0,8},{4,12},{8,0},{12,4},{16,24},{20,28},{24,16},{28,20},{1,9},{5... | collective-permute-start | bytes 786440 | tf_op jit(solution)/shard_map/ppermute | solution.py:506
  20.8 1.5 %collective-permute-start.4 = (f32[128,512]{1,0:T(8,128)S(1)}, f32[128,512]{1,0:T(8,128)S(1)}, u32[]{:S(2)}, u32[]{:S(2)}) collective-permute-start(f32[128,512]{1,0:T(8,128)S(1)} %get-tuple-element.47), channel_id=1, source_target_pairs={{0,16},{4,20},{8,24},{12,28},{16,0},{20,4},{24,8},{28,12},{1,17},{... | collective-permute-start | bytes 786440 | tf_op jit(solution)/shard_map/ppermute | solution.py:506
  22.3 0.9 %late_near_mine.1 = f32[512,128]{1,0:T(8,128)S(1)} custom-call(s32[8]{0:T(128)S(1)} %stack.29.s.sel, bf16[2,512,512]{2,1,0:T(8,128)(2,1)S(1)} %copy-done.2, f32[128,512]{1,0:T(8,128)S(1)} %get-tuple-element.49.refs_1_.near_ref, f32[256,512]{1,0:T(8,128)S(1)} %copy-done.6, f32[16,512]{1,0:T(8,128)S(1)} %copy-done.11, f32[2,512,128]{2,1,0:T(8,128)S(1)} %get-tuple-element.52.refs_4_), custom_call_target="tpu_custom_call" | custom-call | flops 1000 | bytes 1000 | tf_op jit(solution)/shard_map/late_near_mine/pallas_call | solution.py:206
  23.2 0.9 %late_near_other.1 = (f32[256,128]{1,0:T(8,128)S(1)}, f32[256,128]{1,0:T(8,128)S(1)}) custom-call(s32[8]{0:T(128)S(1)} %stack.29.s.sel, bf16[2,512,512]{2,1,0:T(8,128)(2,1)S(1)} %copy-done.4, f32[128,512]{1,0:T(8,128)S(1)} %collective-permute-done.2.refs_1_.near_ref, f32[256,512]{1,0:T(8,128)S(1)} %copy-done.5, f32[16,512]{1,0:T(8,128)S(1)} %copy-done.10, ...), custom_call_target="tpu_custom_call" | custom-call | flops 1000 | bytes 1000 | tf_op jit(solution)/shard_map/late_near_other/pallas_call | solution.py:206
  24.1 1.6 %collective-permute-start.5 = (f32[256,128]{1,0:T(8,128)S(1)}, f32[256,128]{1,0:T(8,128)S(1)}, u32[]{:S(2)}, u32[]{:S(2)}) collective-permute-start(f32[256,128]{1,0:T(8,128)S(1)} %get-tuple-element.54), channel_id=1, source_target_pairs={{0,1},{1,0},{2,3},{3,2},{4,5},{5,4},{6,7},{7,6},{8,9},{9,8},{10,11... | collective-permute-start | bytes 393224 | tf_op jit(solution)/shard_map/ppermute | solution.py:506
  25.8 3.7 %collective-permute-done.5 = f32[256,128]{1,0:T(8,128)S(1)} collective-permute-done((f32[256,128]{1,0:T(8,128)S(1)}, f32[256,128]{1,0:T(8,128)S(1)}, u32[]{:S(2)}, u32[]{:S(2)}) %collective-permute-start.5) | collective-permute-done | bytes 131104 | tf_op jit(solution)/shard_map/ppermute | solution.py:506
  29.5 0.6 %carry_far.1 = (f32[128,512]{1,0:T(8,128)S(1)}, f32[128,512]{1,0:T(8,128)S(1)}) custom-call(s32[8]{0:T(128)S(1)} %stack.29.s.sel, f32[136,512]{1,0:T(8,128)S(1)} %collective-permute-done.1.refs_0_, f32[128,512]{1,0:T(8,128)S(1)} %collective-permute-done.3.refs_1_, f32[128,512]{1,0:T(8,128)S(1)} %collective-permute-done.4.refs_2_, ...), custom_call_target="tpu_custom_call" | custom-call | flops 1000 | bytes 1000 | tf_op jit(solution)/shard_map/carry_far/pallas_call | solution.py:206
  30.3 0.9 %late_far_mine.1 = f32[512,128]{1,0:T(8,128)S(1)} custom-call(s32[8]{0:T(128)S(1)} %stack.29.s.sel, bf16[2,512,512]{2,1,0:T(8,128)(2,1)S(1)} %copy-done.2, f32[128,512]{1,0:T(8,128)S(1)} %get-tuple-element.56.refs_1_.far_ref, f32[256,512]{1,0:T(8,128)S(1)} %copy-done.6, f32[16,512]{1,0:T(8,128)S(1)} %copy-done.11, f32[2,512,128]{2,1,0:T(8,128)S(1)} %get-tuple-element.52.refs_4_), custom_call_target="tpu_custom_call" | custom-call | flops 1000 | bytes 1000 | tf_op jit(solution)/shard_map/late_far_mine/pallas_call | solution.py:206
  31.1 0.6 %collective-permute-done.6.refs_1_.far_ref = f32[128,512]{1,0:T(8,128)S(1)} collective-permute-done((f32[128,512]{1,0:T(8,128)S(1)}, f32[128,512]{1,0:T(8,128)S(1)}, u32[]{:S(2)}, u32[]{:S(2)}) %collective-permute-start.6) | collective-permute-done | bytes 262176 | tf_op jit(solution)/shard_map/ppermute | solution.py:506
  31.8 0.9 %late_far_other.1 = (f32[256,128]{1,0:T(8,128)S(1)}, f32[256,128]{1,0:T(8,128)S(1)}) custom-call(s32[8]{0:T(128)S(1)} %stack.29.s.sel, bf16[2,512,512]{2,1,0:T(8,128)(2,1)S(1)} %copy-done.4, f32[128,512]{1,0:T(8,128)S(1)} %collective-permute-done.6.refs_1_.far_ref, f32[256,512]{1,0:T(8,128)S(1)} %copy-done.5, f32[16,512]{1,0:T(8,128)S(1)} %copy-done.10, ...), custom_call_target="tpu_custom_call" | custom-call | flops 1000 | bytes 1000 | tf_op jit(solution)/shard_map/late_far_other/pallas_call | solution.py:206
  32.7 1.7 %collective-permute-start.7 = (f32[256,128]{1,0:T(8,128)S(1)}, f32[256,128]{1,0:T(8,128)S(1)}, u32[]{:S(2)}, u32[]{:S(2)}) collective-permute-start(f32[256,128]{1,0:T(8,128)S(1)} %get-tuple-element.57.rest_0_), channel_id=1, source_target_pairs={{0,1},{1,0},{2,3},{3,2},{4,5},{5,4},{6,7},{7,6},{8,9},{9,8},{10,11... | collective-permute-start | bytes 393224 | tf_op jit(solution)/shard_map/ppermute | solution.py:506
  34.3 2.6 %collective-permute-start.10 = (f32[256,128]{1,0:T(8,128)S(1)}, f32[256,128]{1,0:T(8,128)S(1)}, u32[]{:S(2)}, u32[]{:S(2)}) collective-permute-start(f32[256,128]{1,0:T(8,128)S(1)} %add.27.refs_7_), channel_id=1, source_target_pairs={{0,2},{1,3},{2,0},{3,1},{4,6},{5,7},{6,4},{7,5},{8,10},{9,11},{10,... | collective-permute-start | bytes 393224 | tf_op jit(solution)/shard_map/ppermute | solution.py:506
  36.9 3.3 %grads.2 = (bf16[512,1024]{1,0:T(8,128)(2,1)}, f32[16,512]{1,0:T(8,128)}) custom-call(s32[8]{0:T(128)S(1)} %stack.29.s.sel, bf16[512,1024]{1,0:T(8,128)(2,1)S(1)} %copy-done, bf16[2,512,512]{2,1,0:T(8,128)(2,1)S(1)} %copy-done.2, bf16[512,128]{1,0:T(8,128)(2,1)S(1)} %copy-done.7, bf16[512,128]{1,0:T(8,128)(2,1)S(1)} %copy-done.8, f32[16,512]{1,0:T(8,128)S(1)} %copy-done.9, ...), custom_call_target="tpu_custom_call" | custom-call | flops 1000 | bytes 1000 | tf_op jit(solution)/shard_map/grads/pallas_call | solution.py:439
  40.2 0.4 collective-permute-done.7
  40.6 1.1 %collective-permute-start.8 = (f32[256,128]{1,0:T(8,128)S(1)}, f32[256,128]{1,0:T(8,128)S(1)}, u32[]{:S(2)}, u32[]{:S(2)}) collective-permute-start(f32[256,128]{1,0:T(8,128)S(1)} %add.28.rest_2_), channel_id=1, source_target_pairs={{0,2},{1,3},{2,0},{3,1},{4,6},{5,7},{6,4},{7,5},{8,10},{9,11},{10,... | collective-permute-start | bytes 393224 | tf_op jit(solution)/shard_map/ppermute | solution.py:506
  41.7 1.6 %collective-permute-done.10 = f32[256,128]{1,0:T(8,128)S(1)} collective-permute-done((f32[256,128]{1,0:T(8,128)S(1)}, f32[256,128]{1,0:T(8,128)S(1)}, u32[]{:S(2)}, u32[]{:S(2)}) %collective-permute-start.10) | collective-permute-done | bytes 131104 | tf_op jit(solution)/shard_map/ppermute | solution.py:506
  43.3 2.0 %collective-permute-start.11 = (f32[256,128]{1,0:T(8,128)S(1)}, f32[256,128]{1,0:T(8,128)S(1)}, u32[]{:S(2)}, u32[]{:S(2)}) collective-permute-start(f32[256,128]{1,0:T(8,128)S(1)} %add.30.refs_0_), channel_id=1, source_target_pairs={{0,1},{1,0},{2,3},{3,2},{4,5},{5,4},{6,7},{7,6},{8,9},{9,8},{10,11... | collective-permute-start | bytes 393224 | tf_op jit(solution)/shard_map/ppermute | solution.py:506
  45.4 4.4 %grads.3 = (bf16[512,1024]{1,0:T(8,128)(2,1)}, f32[16,512]{1,0:T(8,128)}) custom-call(s32[8]{0:T(128)S(1)} %stack.29.s.sel, bf16[512,1024]{1,0:T(8,128)(2,1)S(1)} %copy-done, bf16[2,512,512]{2,1,0:T(8,128)(2,1)S(1)} %copy-done.4, bf16[512,128]{1,0:T(8,128)(2,1)S(1)} %copy-done.7, ...), custom_call_target="tpu_custom_call", output_to_operand_aliasing={{0}: (13, {}), {1}: (14, {})} | custom-call | flops 1000 | bytes 1000 | tf_op jit(solution)/shard_map/grads/pallas_call | solution.py:439
  49.8 0.1 collective-permute-start.9
  49.9 0.3 collective-permute-done.11.refs_1_
  50.2 1.3 %join.2 = (f32[512,128]{1,0:T(8,128)}, f32[512,128]{1,0:T(8,128)}) custom-call(s32[8]{0:T(128)S(1)} %stack.29.s.sel, f32[256,128]{1,0:T(8,128)S(1)} %add.30.refs_0_, f32[256,128]{1,0:T(8,128)S(1)} %collective-permute-done.11.refs_1_, f32[256,128]{1,0:T(8,128)S(1)} %add.29.refs_2_), custom_call_target="tpu_custom_call" | custom-call | flops 1000 | bytes 1000 | tf_op jit(solution)/shard_map/join/pallas_call | solution.py:487
  51.5 3.3 %collective-permute-done.9.refs_0_ = f32[256,128]{1,0:T(8,128)S(1)} collective-permute-done((f32[256,128]{1,0:T(8,128)S(1)}, f32[256,128]{1,0:T(8,128)S(1)}, u32[]{:S(2)}, u32[]{:S(2)}) %collective-permute-start.9) | collective-permute-done | bytes 131104 | tf_op jit(solution)/shard_map/ppermute | solution.py:506
  54.8 1.2 %join.3 = (f32[512,128]{1,0:T(8,128)}, f32[512,128]{1,0:T(8,128)}) custom-call(s32[8]{0:T(128)S(1)} %stack.29.s.sel, f32[256,128]{1,0:T(8,128)S(1)} %collective-permute-done.9.refs_0_, f32[512,128]{1,0:T(8,128)} %get-tuple-element.65.refs_1_, f32[512,128]{1,0:T(8,128)} %get-tuple-element.66.refs_2_), custom_call_target="tpu_custom_call", output_to_operand_aliasing={{0}: (2, {}), {1}: (3, {})} | custom-call | flops 1000 | bytes 1000 | tf_op jit(solution)/shard_map/join/pallas_call | solution.py:487
  (37 shorter events, 0.3 us)
Async XLA Ops:
  0.6 4.5 %copy-start = (bf16[512,1024]{1,0:T(8,128)(2,1)S(1)}, bf16[512,1024]{1,0:T(8,128)(2,1)}, u32[]{:S(2)}) copy-start(bf16[512,1024]{1,0:T(8,128)(2,1)} %x_ref.5) | copy-start | bytes 3145732
  0.6 4.5 %copy-start.3 = (bf16[512,1024]{1,0:T(8,128)(2,1)S(1)}, bf16[512,1024]{1,0:T(8,128)(2,1)}, u32[]{:S(2)}) copy-start(bf16[512,1024]{1,0:T(8,128)(2,1)} %g_ref.1) | copy-start | bytes 3145732
  0.7 4.5 %copy-start.7 = (bf16[512,128]{1,0:T(8,128)(2,1)S(1)}, bf16[512,128]{1,0:T(8,128)(2,1)}, u32[]{:S(2)}) copy-start(bf16[512,128]{1,0:T(8,128)(2,1)} %w_ref.5) | copy-start | bytes 393220
  0.7 4.5 %copy-start.8 = (bf16[512,128]{1,0:T(8,128)(2,1)S(1)}, bf16[512,128]{1,0:T(8,128)(2,1)}, u32[]{:S(2)}) copy-start(bf16[512,128]{1,0:T(8,128)(2,1)} %r_ref.5) | copy-start | bytes 393220
  0.7 4.5 %copy-start.9 = (f32[16,512]{1,0:T(8,128)S(1)}, f32[16,512]{1,0:T(8,128)}, u32[]{:S(2)}) copy-start(f32[16,512]{1,0:T(8,128)} %ld_ref.5) | copy-start | bytes 98308
  4.6 3.0 %collective-permute-start = (f32[264,512]{1,0:T(8,128)}, f32[264,512]{1,0:T(8,128)S(1)}, u32[]{:S(2)}, u32[]{:S(2)}) collective-permute-start(f32[264,512]{1,0:T(8,128)} %get-tuple-element.39.pay_ref), channel_id=1, source_target_pairs={{0,4},{4,0},{8,12},{12,8},{16,20},{20,16},{24,28},{28,24},{1,5},{5... | collective-permute-start | bytes 1622024 | tf_op jit(solution)/shard_map/ppermute | solution.py:506
  8.3 9.9 %collective-permute-start.1 = (f32[136,512]{1,0:T(8,128)S(1)}, f32[136,512]{1,0:T(8,128)S(1)}, u32[]{:S(2)}, u32[]{:S(2)}) collective-permute-start(f32[136,512]{1,0:T(8,128)S(1)} %get-tuple-element.40.rest_0_.refs_1_), channel_id=1, source_target_pairs={{0,8},{4,12},{8,0},{12,4},{16,24},{20,28},{24,16},{28,20},{1,9},{5... | collective-permute-start | bytes 835592 | tf_op jit(solution)/shard_map/ppermute | solution.py:506
  18.2 4.1 %copy-start.2 = (bf16[2,512,512]{2,1,0:T(8,128)(2,1)S(1)}, bf16[2,512,512]{2,1,0:T(8,128)(2,1)}, u32[]{:S(2)}) copy-start(bf16[2,512,512]{2,1,0:T(8,128)(2,1)} %get-tuple-element.48.refs_0_.gw_ref) | copy-start | bytes 3145732
  18.2 4.1 %copy-start.6 = (f32[256,512]{1,0:T(8,128)S(1)}, f32[256,512]{1,0:T(8,128)}, u32[]{:S(2)}) copy-start(f32[256,512]{1,0:T(8,128)} %get-tuple-element.50.refs_2_.part_ref) | copy-start | bytes 1572868
  18.2 4.1 %copy-start.11 = (f32[16,512]{1,0:T(8,128)S(1)}, f32[16,512]{1,0:T(8,128)}, u32[]{:S(2)}) copy-start(f32[16,512]{1,0:T(8,128)} %get-tuple-element.51.refs_3_.tot_ref) | copy-start | bytes 98308
  18.9 4.3 %copy-start.4 = (bf16[2,512,512]{2,1,0:T(8,128)(2,1)S(1)}, bf16[2,512,512]{2,1,0:T(8,128)(2,1)}, u32[]{:S(2)}) copy-start(bf16[2,512,512]{2,1,0:T(8,128)(2,1)} %get-tuple-element.37.refs_0_.gw_ref) | copy-start | bytes 3145732
  18.9 4.3 %copy-start.5 = (f32[256,512]{1,0:T(8,128)S(1)}, f32[256,512]{1,0:T(8,128)}, u32[]{:S(2)}) copy-start(f32[256,512]{1,0:T(8,128)} %get-tuple-element.43.refs_2_.part_ref) | copy-start | bytes 1572868
  18.9 4.3 %copy-start.10 = (f32[16,512]{1,0:T(8,128)S(1)}, f32[16,512]{1,0:T(8,128)}, u32[]{:S(2)}) copy-start(f32[16,512]{1,0:T(8,128)} %get-tuple-element.44.refs_3_.tot_ref) | copy-start | bytes 98308
  18.9 4.3 %collective-permute-start.2 = (f32[128,512]{1,0:T(8,128)S(1)}, f32[128,512]{1,0:T(8,128)S(1)}, u32[]{:S(2)}, u32[]{:S(2)}) collective-permute-start(f32[128,512]{1,0:T(8,128)S(1)} %get-tuple-element.45), channel_id=1, source_target_pairs={{0,4},{4,0},{8,12},{12,8},{16,20},{20,16},{24,28},{28,24},{1,5},{5... | collective-permute-start | bytes 786440 | tf_op jit(solution)/shard_map/ppermute | solution.py:506
  19.0 10.5 %collective-permute-start.3 = (f32[128,512]{1,0:T(8,128)S(1)}, f32[128,512]{1,0:T(8,128)S(1)}, u32[]{:S(2)}, u32[]{:S(2)}) collective-permute-start(f32[128,512]{1,0:T(8,128)S(1)} %get-tuple-element.46), channel_id=1, source_target_pairs={{0,8},{4,12},{8,0},{12,4},{16,24},{20,28},{24,16},{28,20},{1,9},{5... | collective-permute-start | bytes 786440 | tf_op jit(solution)/shard_map/ppermute | solution.py:506
  20.8 8.7 %collective-permute-start.4 = (f32[128,512]{1,0:T(8,128)S(1)}, f32[128,512]{1,0:T(8,128)S(1)}, u32[]{:S(2)}, u32[]{:S(2)}) collective-permute-start(f32[128,512]{1,0:T(8,128)S(1)} %get-tuple-element.47), channel_id=1, source_target_pairs={{0,16},{4,20},{8,24},{12,28},{16,0},{20,4},{24,8},{28,12},{1,17},{... | collective-permute-start | bytes 786440 | tf_op jit(solution)/shard_map/ppermute | solution.py:506
  24.1 5.4 %collective-permute-start.5 = (f32[256,128]{1,0:T(8,128)S(1)}, f32[256,128]{1,0:T(8,128)S(1)}, u32[]{:S(2)}, u32[]{:S(2)}) collective-permute-start(f32[256,128]{1,0:T(8,128)S(1)} %get-tuple-element.54), channel_id=1, source_target_pairs={{0,1},{1,0},{2,3},{3,2},{4,5},{5,4},{6,7},{7,6},{8,9},{9,8},{10,11... | collective-permute-start | bytes 393224 | tf_op jit(solution)/shard_map/ppermute | solution.py:506
  30.2 1.6 %collective-permute-start.6 = (f32[128,512]{1,0:T(8,128)S(1)}, f32[128,512]{1,0:T(8,128)S(1)}, u32[]{:S(2)}, u32[]{:S(2)}) collective-permute-start(f32[128,512]{1,0:T(8,128)S(1)} %get-tuple-element.55), channel_id=1, source_target_pairs={{0,4},{4,0},{8,12},{12,8},{16,20},{20,16},{24,28},{28,24},{1,5},{5... | collective-permute-start | bytes 786440 | tf_op jit(solution)/shard_map/ppermute | solution.py:506
  30.2 6.7 %copy-start.1 = (f32[512,1024]{1,0:T(8,128)S(1)}, f32[512,1024]{1,0:T(8,128)}, u32[]{:S(2)}) copy-start(f32[512,1024]{1,0:T(8,128)} %get-tuple-element.41.refs_6_.gint_ref) | copy-start | bytes 6291460
  30.2 6.7 %copy-start.12 = (f32[16,512]{1,0:T(8,128)S(1)}, f32[16,512]{1,0:T(8,128)}, u32[]{:S(2)}) copy-start(f32[16,512]{1,0:T(8,128)} %get-tuple-element.42.dot_ref) | copy-start | bytes 98308
  32.7 7.9 %collective-permute-start.7 = (f32[256,128]{1,0:T(8,128)S(1)}, f32[256,128]{1,0:T(8,128)S(1)}, u32[]{:S(2)}, u32[]{:S(2)}) collective-permute-start(f32[256,128]{1,0:T(8,128)S(1)} %get-tuple-element.57.rest_0_), channel_id=1, source_target_pairs={{0,1},{1,0},{2,3},{3,2},{4,5},{5,4},{6,7},{7,6},{8,9},{9,8},{10,11... | collective-permute-start | bytes 393224 | tf_op jit(solution)/shard_map/ppermute | solution.py:506
  34.3 9.0 %collective-permute-start.10 = (f32[256,128]{1,0:T(8,128)S(1)}, f32[256,128]{1,0:T(8,128)S(1)}, u32[]{:S(2)}, u32[]{:S(2)}) collective-permute-start(f32[256,128]{1,0:T(8,128)S(1)} %add.27.refs_7_), channel_id=1, source_target_pairs={{0,2},{1,3},{2,0},{3,1},{4,6},{5,7},{6,4},{7,5},{8,10},{9,11},{10,... | collective-permute-start | bytes 393224 | tf_op jit(solution)/shard_map/ppermute | solution.py:506
  40.6 9.1 %collective-permute-start.8 = (f32[256,128]{1,0:T(8,128)S(1)}, f32[256,128]{1,0:T(8,128)S(1)}, u32[]{:S(2)}, u32[]{:S(2)}) collective-permute-start(f32[256,128]{1,0:T(8,128)S(1)} %add.28.rest_2_), channel_id=1, source_target_pairs={{0,2},{1,3},{2,0},{3,1},{4,6},{5,7},{6,4},{7,5},{8,10},{9,11},{10,... | collective-permute-start | bytes 393224 | tf_op jit(solution)/shard_map/ppermute | solution.py:506
  43.3 6.8 %collective-permute-start.11 = (f32[256,128]{1,0:T(8,128)S(1)}, f32[256,128]{1,0:T(8,128)S(1)}, u32[]{:S(2)}, u32[]{:S(2)}) collective-permute-start(f32[256,128]{1,0:T(8,128)S(1)} %add.30.refs_0_), channel_id=1, source_target_pairs={{0,1},{1,0},{2,3},{3,2},{4,5},{5,4},{6,7},{7,6},{8,9},{9,8},{10,11... | collective-permute-start | bytes 393224 | tf_op jit(solution)/shard_map/ppermute | solution.py:506
  49.8 5.0 %collective-permute-start.9 = (f32[256,128]{1,0:T(8,128)S(1)}, f32[256,128]{1,0:T(8,128)S(1)}, u32[]{:S(2)}, u32[]{:S(2)}) collective-permute-start(f32[256,128]{1,0:T(8,128)S(1)} %add.29.refs_2_), channel_id=1, source_target_pairs={{0,1},{1,0},{2,3},{3,2},{4,5},{5,4},{6,7},{7,6},{8,9},{9,8},{10,11... | collective-permute-start | bytes 393224 | tf_op jit(solution)/shard_map/ppermute | solution.py:506

commit v6 on v5

--- a/solution.py
+++ b/solution.py
@@ -50,16 +50,21 @@
     return times_ones(decay_blk, upto)
 
 
-def spread_decays(running, head_size):
+def spread_both(ld_ref, head_size):
     lanes = GROUP * head_size
-    total = running[:, Q - 1 : Q]
-    parts = split_two(jnp.exp(running)) + split_two(jnp.exp(total - running))
-    stacked = jnp.concatenate(parts, axis=0).T.astype(BF16)
-    row = iota((4 * GROUP, lanes), 0)
-    owner = row % GROUP == iota((4 * GROUP, lanes), 1) // head_size
-    first = (owner & (row < 2 * GROUP)).astype(F32).astype(BF16)
-    second = (owner & (row >= 2 * GROUP)).astype(F32).astype(BF16)
-    return dot(stacked, first), dot(stacked, second)
+    upto = (iota((Q, Q), 0) <= iota((Q, Q), 1)).astype(BF16)
+    pieces = [split_three(ld_ref[:, b * Q : (b + 1) * Q]) for b in range(2)]
+    summed = dot(jnp.concatenate([*pieces[0], *pieces[1], *([jnp.zeros((GROUP, Q), F32)] * 2)], axis=0).astype(BF16), upto)
+    stacked = []
+    for b in range(2):
+        first, second, third = (summed[(3 * b + k) * GROUP : (3 * b + k + 1) * GROUP] for k in range(3))
+        running = first + second + third
+        stacked += split_two(jnp.exp(running)) + split_two(jnp.exp(running[:, Q - 1 : Q] - running))
+    stacked = jnp.concatenate(stacked, axis=0).T.astype(BF16)
+    row = iota((8 * GROUP, lanes), 0)
+    owner = row % GROUP == iota((8 * GROUP, lanes), 1) // head_size
+    masks = [(owner & (row // (2 * GROUP) == k)).astype(F32).astype(BF16) for k in range(4)]
+    return [(dot(stacked, masks[2 * b]), dot(stacked, masks[2 * b + 1])) for b in range(2)]
 
 
 def state_kernel(sel, x_hbm, g_hbm, w_hbm, r_hbm, ld_hbm, *rest):
@@ -81,10 +86,10 @@
     if sources:
         x_hbm, g_hbm, w_hbm, r_hbm, ld_hbm = sources
         pairs = [(ld_hbm.at[group, :], ld_ref), (w_hbm, w_ref), (r_hbm, r_ref)]
-        for b in range(2):
-            at = pl.ds(b * Q, Q)
-            pairs.append((x_hbm.at[at, here], x_ref.at[at, :]))
-            pairs.append((g_hbm.at[at, here], g_ref.at[at, :]))
+        for src, dst in ((x_hbm, x_ref), (g_hbm, g_ref)):
+            for b in range(2):
+                at = pl.ds(b * Q, Q)
+                pairs.append((src.at[at, here], dst.at[at, :]))
         moves = [pltpu.make_async_copy(src, dst, sems.at[k]) for k, (src, dst) in enumerate(pairs)]
     for move in moves:
         move.start()
@@ -97,36 +102,35 @@
     pay_out, wg_out, part_out, tot_out = outs
     for move in moves[:1]:
         move.wait()
-    decays = [spread_decays(running_of(ld_ref[:, b * Q : (b + 1) * Q]), lanes // GROUP) for b in range(2)]
+    decays = spread_both(ld_ref, lanes // GROUP)
     ends = [decay_in[Q - 1 : Q, :] for decay_in, _ in decays]
     tot_ref[0:8, :] = jnp.broadcast_to(ends[0], (8, lanes))
     tot_ref[8:16, :] = jnp.broadcast_to(ends[1], (8, lanes))
     leave(tot_ref, tot_out)
     for move in moves[1:3]:
         move.wait()
-    f_parts, g_parts = [], []
-    for b in range(2):
-        at = slice(b * Q, (b + 1) * Q)
-        decay_in, decay_out = decays[b]
-        for move in moves[3 + 2 * b : 4 + 2 * b]:
-            move.wait()
-        iw = (x_ref[at, :].astype(F32) * decay_out).astype(BF16)
-        wg_ref[1, at, :] = iw
-        leave(wg_ref.at[1, pl.ds(b * Q, Q), :], wg_out.at[1, pl.ds(b * Q, Q), :])
-        f_parts.append(dot(w_ref[at, :].astype(F32).T.astype(BF16), iw))
-        for move in moves[4 + 2 * b : 5 + 2 * b]:
-            move.wait()
-        gw = (g_ref[at, :].astype(F32) * decay_in).astype(BF16)
-        wg_ref[0, at, :] = gw
-        leave(wg_ref.at[0, pl.ds(b * Q, Q), :], wg_out.at[0, pl.ds(b * Q, Q), :])
-        g_parts.append(dot(r_ref[at, :].astype(F32).T.astype(BF16), gw))
-    pay_ref[0:width, :] = ends[1] * f_parts[0] + f_parts[1]
-    pay_ref[width : 2 * width, :] = ends[0] * g_parts[1] + g_parts[0]
-    pay_ref[2 * width : 2 * width + 8, :] = jnp.broadcast_to(ends[0] * ends[1], (8, lanes))
-    leave(pay_ref, pay_out)
-    part_ref[0:width, :] = f_parts[0]
-    part_ref[width : 2 * width, :] = g_parts[1]
-    leave(part_ref, part_out)
+    turned = [[ref[b * Q : (b + 1) * Q, :].astype(F32).T.astype(BF16) for b in range(2)] for ref in (w_ref, r_ref)]
+    for way, src in ((1, x_ref), (0, g_ref)):
+        parts = []
+        for b in range(2):
+            at = slice(b * Q, (b + 1) * Q)
+            for move in moves[5 - 2 * way + b : 6 - 2 * way + b]:
+                move.wait()
+            scaled = (src[at, :].astype(F32) * decays[b][way]).astype(BF16)
+            wg_ref[way, at, :] = scaled
+            leave(wg_ref.at[way, pl.ds(b * Q, Q), :], wg_out.at[way, pl.ds(b * Q, Q), :])
+            parts.append(dot(turned[1 - way][b], scaled))
+        rows_of = pl.ds((1 - way) * width, width)
+        if way:
+            pay_ref[rows_of, :] = ends[1] * parts[0] + parts[1]
+            leave(pay_ref.at[rows_of, :], pay_out.at[rows_of, :])
+        else:
+            pay_ref[rows_of, :] = ends[0] * parts[1] + parts[0]
+            pay_ref[2 * width : 2 * width + 8, :] = jnp.broadcast_to(ends[0] * ends[1], (8, lanes))
+            last = pl.ds(width, width + 8)
+            leave(pay_ref.at[last, :], pay_out.at[last, :])
+        part_ref[rows_of, :] = parts[1 - way]
+        leave(part_ref.at[rows_of, :], part_out.at[rows_of, :])
     for move in leaving:
         move.wait()
 
@@ -165,7 +169,7 @@
             out_specs=[ANYWHERE] * 4,
             scratch_shapes=[
                 *[pltpu.VMEM(*a) for a in ([] if loaded else buffers) + shapes],
-                pltpu.SemaphoreType.DMA((14,)),
+                pltpu.SemaphoreType.DMA((16,)),
             ],
         ),
         out_shape=[shape_of(*shapes[0]), *[stored(*a) for a in shapes[1:]]],
@@ -414,9 +418,10 @@
     owner = iota((16, lanes), 0) == iota((16, lanes), 1) // size
     ones = owner.astype(F32).astype(BF16)
     onward = (iota((Q, Q), 0) >= iota((Q, Q), 1)).astype(F32).astype(BF16)
+    decays = spread_both(ld_ref, size)
     for b in range(2):
         at = slice(b * Q, (b + 1) * Q)
-        decay_out = spread_decays(running_of(ld_ref[:, at]), size)[1]
+        decay_out = decays[b][1]
         out_inter = dot(r_ref[at, :], state_in[b].astype(BF16))
         grad_full = gint_ref[at, :] + dot(w_ref[at, :], grad_end[b].astype(BF16)) * decay_out
         gi_ref[at, :] = grad_full.astype(BF16)

time: 56.2 us -> 55.1 us (0.980)
  Pallas kernels: 27.7 us -> 26.2 us
    pallas_call x2, Pallas kernels: 7.64 us -> 6.75 us  [grads(): pl.pallas_call(functools.partial(grads_kernel, scale), grid_spec=pltpu.Pr...]
    pallas_call x2, Pallas kernels: 6.24 us -> 5.64 us  [states(): pl.pallas_call(loaded_kernel if loaded else state_kernel, grid_spec=pltpu...]
  transfers between devices with their start and end apart: 12 -> 12, of which waited for: 7 -> 7; matrix products, arithmetic and copies ran while one was open for 0% -> 0% of each run, Pallas kernels for 35% -> 34%
where the time goes in v6:
time: 55.1 us; the launch traced here: 54.9 us
  Pallas kernels  26.2 us (48%)
  starting transfers between devices  15.8 us (29%)
  waiting for transfers between devices  11.8 us (21%)
  between operations  0.94 us (2%)
    ppermute x12, starting transfers between devices, swap(): return lax.ppermute(values, axis, [(i, i ^ mask) for i in range(count)])  15.8 us
    ppermute x12, waiting for transfers between devices, swap(): return lax.ppermute(values, axis, [(i, i ^ mask) for i in range(count)])  11.8 us
    pallas_call x2, Pallas kernels, grads(): pl.pallas_call(functools.partial(grads_kernel, scale), grid_spec=pltpu.Pr...  6.75 us
    pallas_call x1, Pallas kernels, scores(): pl.pallas_call(scores_kernel, grid=(rows // Q, heads // GROUP), in_specs=...  5.82 us
    pallas_call x2, Pallas kernels, states(): pl.pallas_call(loaded_kernel if loaded else state_kernel, grid_spec=pltpu...  5.64 us
    pallas_call x7, Pallas kernels, call(): pl.pallas_call(body, grid_spec=pltpu.PrefetchScalarGridSpec(num_scalar_pr...  5.47 us
    pallas_call x2, Pallas kernels, join(): pl.pallas_call(functools.partial(join_kernel, places), grid_spec=pltpu.Pr...  2.52 us
  transfers between devices with their start and end apart: 12, of which 7 were waited for; matrix products, arithmetic and copies ran while one was open for 0% of the time, Pallas kernels for 34%

profile of v6, /device:TPU:0, one launch (start us, length us, event | category | flops | bytes accessed | tf_op | source)
XLA Modules:
  0.0 54.9 jit_solution(3994048352877694814)
XLA Ops:
  0.7 3.5 %states.2 = (f32[264,512]{1,0:T(8,128)}, bf16[2,512,512]{2,1,0:T(8,128)(2,1)}, f32[256,512]{1,0:T(8,128)}, f32[16,512]{1,0:T(8,128)}) custom-call(s32[1]{0:T(128)} %bitcast.5.sel, bf16[512,1024]{1,0:T(8,128)(2,1)} %x_ref.5, bf16[512,1024]{1,0:T(8,128)(2,1)} %g_ref.1, bf16[512,128]{1,0:T(8,128)(2,1)} %w_ref.5, bf16[512,128]{1,0:T(8,128)(2,1)} %r_ref.5, ...), custom_call_target="tpu_custom_call" | custom-call | flops 1000 | bytes 1000 | tf_op jit(solution)/shard_map/states/pallas_call | solution.py:161
  4.2 0.5 collective-permute-start
  4.8 2.1 %states.3 = (f32[264,512]{1,0:T(8,128)S(1)}, bf16[2,512,512]{2,1,0:T(8,128)(2,1)}, f32[256,512]{1,0:T(8,128)}, f32[16,512]{1,0:T(8,128)}) custom-call(s32[1]{0:T(128)} %bitcast.2.sel, bf16[512,1024]{1,0:T(8,128)(2,1)S(1)} %copy-done, bf16[512,1024]{1,0:T(8,128)(2,1)S(1)} %copy-done.3, bf16[512,128]{1,0:T(8,128)(2,1)S(1)} %copy-done.7, ...), custom_call_target="tpu_custom_call" | custom-call | flops 1000 | bytes 1000 | tf_op jit(solution)/shard_map/states/pallas_call | solution.py:161
  6.9 0.1 stack.29.s.sel
  7.0 0.7 %chip.1 = (f32[136,512]{1,0:T(8,128)S(1)}, f32[128,512]{1,0:T(8,128)S(1)}) custom-call(s32[8]{0:T(128)S(1)} %stack.29.s.sel, f32[264,512]{1,0:T(8,128)S(1)} %get-tuple-element.38.refs_0_.refs_2_.refs_4_.refs_3_.refs_5_.pay_ref, f32[264,512]{1,0:T(8,128)S(1)} %collective-permute-done.refs_1_.refs_3_.refs_5_.refs_4_.refs_6_), custom_call_target="tpu_custom_call" | custom-call | flops 1000 | bytes 1000 | tf_op jit(solution)/shard_map/chip/pallas_call | solution.py:210
  7.7 2.6 %collective-permute-start.1 = (f32[136,512]{1,0:T(8,128)S(1)}, f32[136,512]{1,0:T(8,128)S(1)}, u32[]{:S(2)}, u32[]{:S(2)}) collective-permute-start(f32[136,512]{1,0:T(8,128)S(1)} %get-tuple-element.40.rest_0_.refs_1_), channel_id=1, source_target_pairs={{0,8},{4,12},{8,0},{12,4},{16,24},{20,28},{24,16},{28,20},{1,9},{5... | collective-permute-start | bytes 835592 | tf_op jit(solution)/shard_map/ppermute | solution.py:511
  10.3 5.8 %scores.1 = (f32[2,512,128]{2,1,0:T(8,128)S(1)}, f32[512,1024]{1,0:T(8,128)}, f32[16,512]{1,0:T(8,128)}) custom-call(bf16[512,1024]{1,0:T(8,128)(2,1)S(1)} %copy-done, bf16[512,1024]{1,0:T(8,128)(2,1)S(1)} %copy-done.3, bf16[512,128]{1,0:T(8,128)(2,1)S(1)} %copy-done.7, bf16[512,128]{1,0:T(8,128)(2,1)S(1)} %copy-done.8, f32[16,512]{1,0:T(8,128)S(1)} %copy-done.9, ...), custom_call_target="tpu_custom_call" | custom-call | flops 1000 | bytes 1000 | tf_op jit(solution)/shard_map/scores/pallas_call | solution.py:386
  16.1 1.5 %collective-permute-done.1.refs_0_ = f32[136,512]{1,0:T(8,128)S(1)} collective-permute-done((f32[136,512]{1,0:T(8,128)S(1)}, f32[136,512]{1,0:T(8,128)S(1)}, u32[]{:S(2)}, u32[]{:S(2)}) %collective-permute-start.1) | collective-permute-done | bytes 278560 | tf_op jit(solution)/shard_map/ppermute | solution.py:511
  17.6 0.7 %carry_near.1 = (f32[128,512]{1,0:T(8,128)S(1)}, f32[128,512]{1,0:T(8,128)S(1)}, f32[128,512]{1,0:T(8,128)S(1)}) custom-call(s32[8]{0:T(128)S(1)} %stack.29.s.sel, f32[136,512]{1,0:T(8,128)S(1)} %collective-permute-done.1.refs_0_, f32[136,512]{1,0:T(8,128)S(1)} %get-tuple-element.40.rest_0_.refs_1_, ...), custom_call_target="tpu_custom_call" | custom-call | flops 1000 | bytes 1000 | tf_op jit(solution)/shard_map/carry_near/pallas_call | solution.py:210
  18.4 1.8 %collective-permute-start.3 = (f32[128,512]{1,0:T(8,128)S(1)}, f32[128,512]{1,0:T(8,128)S(1)}, u32[]{:S(2)}, u32[]{:S(2)}) collective-permute-start(f32[128,512]{1,0:T(8,128)S(1)} %get-tuple-element.46), channel_id=1, source_target_pairs={{0,8},{4,12},{8,0},{12,4},{16,24},{20,28},{24,16},{28,20},{1,9},{5... | collective-permute-start | bytes 786440 | tf_op jit(solution)/shard_map/ppermute | solution.py:511
  20.2 1.5 %collective-permute-start.4 = (f32[128,512]{1,0:T(8,128)S(1)}, f32[128,512]{1,0:T(8,128)S(1)}, u32[]{:S(2)}, u32[]{:S(2)}) collective-permute-start(f32[128,512]{1,0:T(8,128)S(1)} %get-tuple-element.47), channel_id=1, source_target_pairs={{0,16},{4,20},{8,24},{12,28},{16,0},{20,4},{24,8},{28,12},{1,17},{... | collective-permute-start | bytes 786440 | tf_op jit(solution)/shard_map/ppermute | solution.py:511
  21.7 0.9 %late_near_mine.1 = f32[512,128]{1,0:T(8,128)S(1)} custom-call(s32[8]{0:T(128)S(1)} %stack.29.s.sel, bf16[2,512,512]{2,1,0:T(8,128)(2,1)S(1)} %copy-done.2, f32[128,512]{1,0:T(8,128)S(1)} %get-tuple-element.49.refs_1_.near_ref, f32[256,512]{1,0:T(8,128)S(1)} %copy-done.6, f32[16,512]{1,0:T(8,128)S(1)} %copy-done.11, f32[2,512,128]{2,1,0:T(8,128)S(1)} %get-tuple-element.52.refs_4_), custom_call_target="tpu_custom_call" | custom-call | flops 1000 | bytes 1000 | tf_op jit(solution)/shard_map/late_near_mine/pallas_call | solution.py:210
  22.6 0.9 %late_near_other.1 = (f32[256,128]{1,0:T(8,128)S(1)}, f32[256,128]{1,0:T(8,128)S(1)}) custom-call(s32[8]{0:T(128)S(1)} %stack.29.s.sel, bf16[2,512,512]{2,1,0:T(8,128)(2,1)S(1)} %copy-done.4, f32[128,512]{1,0:T(8,128)S(1)} %collective-permute-done.2.refs_1_.near_ref, f32[256,512]{1,0:T(8,128)S(1)} %copy-done.5, f32[16,512]{1,0:T(8,128)S(1)} %copy-done.10, ...), custom_call_target="tpu_custom_call" | custom-call | flops 1000 | bytes 1000 | tf_op jit(solution)/shard_map/late_near_other/pallas_call | solution.py:210
  23.5 1.6 %collective-permute-start.5 = (f32[256,128]{1,0:T(8,128)S(1)}, f32[256,128]{1,0:T(8,128)S(1)}, u32[]{:S(2)}, u32[]{:S(2)}) collective-permute-start(f32[256,128]{1,0:T(8,128)S(1)} %get-tuple-element.54), channel_id=1, source_target_pairs={{0,1},{1,0},{2,3},{3,2},{4,5},{5,4},{6,7},{7,6},{8,9},{9,8},{10,11... | collective-permute-start | bytes 393224 | tf_op jit(solution)/shard_map/ppermute | solution.py:511
  25.2 3.7 %collective-permute-done.5 = f32[256,128]{1,0:T(8,128)S(1)} collective-permute-done((f32[256,128]{1,0:T(8,128)S(1)}, f32[256,128]{1,0:T(8,128)S(1)}, u32[]{:S(2)}, u32[]{:S(2)}) %collective-permute-start.5) | collective-permute-done | bytes 131104 | tf_op jit(solution)/shard_map/ppermute | solution.py:511
  28.9 0.6 %carry_far.1 = (f32[128,512]{1,0:T(8,128)S(1)}, f32[128,512]{1,0:T(8,128)S(1)}) custom-call(s32[8]{0:T(128)S(1)} %stack.29.s.sel, f32[136,512]{1,0:T(8,128)S(1)} %collective-permute-done.1.refs_0_, f32[128,512]{1,0:T(8,128)S(1)} %collective-permute-done.3.refs_1_, f32[128,512]{1,0:T(8,128)S(1)} %collective-permute-done.4.refs_2_, ...), custom_call_target="tpu_custom_call" | custom-call | flops 1000 | bytes 1000 | tf_op jit(solution)/shard_map/carry_far/pallas_call | solution.py:210
  29.6 0.9 %late_far_mine.1 = f32[512,128]{1,0:T(8,128)S(1)} custom-call(s32[8]{0:T(128)S(1)} %stack.29.s.sel, bf16[2,512,512]{2,1,0:T(8,128)(2,1)S(1)} %copy-done.2, f32[128,512]{1,0:T(8,128)S(1)} %get-tuple-element.56.refs_1_.far_ref, f32[256,512]{1,0:T(8,128)S(1)} %copy-done.6, f32[16,512]{1,0:T(8,128)S(1)} %copy-done.11, f32[2,512,128]{2,1,0:T(8,128)S(1)} %get-tuple-element.52.refs_4_), custom_call_target="tpu_custom_call" | custom-call | flops 1000 | bytes 1000 | tf_op jit(solution)/shard_map/late_far_mine/pallas_call | solution.py:210
  30.5 0.6 %collective-permute-done.6.refs_1_.far_ref = f32[128,512]{1,0:T(8,128)S(1)} collective-permute-done((f32[128,512]{1,0:T(8,128)S(1)}, f32[128,512]{1,0:T(8,128)S(1)}, u32[]{:S(2)}, u32[]{:S(2)}) %collective-permute-start.6) | collective-permute-done | bytes 262176 | tf_op jit(solution)/shard_map/ppermute | solution.py:511
  31.1 0.9 %late_far_other.1 = (f32[256,128]{1,0:T(8,128)S(1)}, f32[256,128]{1,0:T(8,128)S(1)}) custom-call(s32[8]{0:T(128)S(1)} %stack.29.s.sel, bf16[2,512,512]{2,1,0:T(8,128)(2,1)S(1)} %copy-done.4, f32[128,512]{1,0:T(8,128)S(1)} %collective-permute-done.6.refs_1_.far_ref, f32[256,512]{1,0:T(8,128)S(1)} %copy-done.5, f32[16,512]{1,0:T(8,128)S(1)} %copy-done.10, ...), custom_call_target="tpu_custom_call" | custom-call | flops 1000 | bytes 1000 | tf_op jit(solution)/shard_map/late_far_other/pallas_call | solution.py:210
  32.0 1.7 %collective-permute-start.7 = (f32[256,128]{1,0:T(8,128)S(1)}, f32[256,128]{1,0:T(8,128)S(1)}, u32[]{:S(2)}, u32[]{:S(2)}) collective-permute-start(f32[256,128]{1,0:T(8,128)S(1)} %get-tuple-element.57.rest_0_), channel_id=1, source_target_pairs={{0,1},{1,0},{2,3},{3,2},{4,5},{5,4},{6,7},{7,6},{8,9},{9,8},{10,11... | collective-permute-start | bytes 393224 | tf_op jit(solution)/shard_map/ppermute | solution.py:511
  33.7 2.6 %collective-permute-start.10 = (f32[256,128]{1,0:T(8,128)S(1)}, f32[256,128]{1,0:T(8,128)S(1)}, u32[]{:S(2)}, u32[]{:S(2)}) collective-permute-start(f32[256,128]{1,0:T(8,128)S(1)} %add.27.refs_7_), channel_id=1, source_target_pairs={{0,2},{1,3},{2,0},{3,1},{4,6},{5,7},{6,4},{7,5},{8,10},{9,11},{10,... | collective-permute-start | bytes 393224 | tf_op jit(solution)/shard_map/ppermute | solution.py:511
  36.3 2.8 %grads.2 = (bf16[512,1024]{1,0:T(8,128)(2,1)}, f32[16,512]{1,0:T(8,128)}) custom-call(s32[8]{0:T(128)S(1)} %stack.29.s.sel, bf16[512,1024]{1,0:T(8,128)(2,1)S(1)} %copy-done, bf16[2,512,512]{2,1,0:T(8,128)(2,1)S(1)} %copy-done.2, bf16[512,128]{1,0:T(8,128)(2,1)S(1)} %copy-done.7, bf16[512,128]{1,0:T(8,128)(2,1)S(1)} %copy-done.8, f32[16,512]{1,0:T(8,128)S(1)} %copy-done.9, ...), custom_call_target="tpu_custom_call" | custom-call | flops 1000 | bytes 1000 | tf_op jit(solution)/shard_map/grads/pallas_call | solution.py:444
  39.1 0.8 %collective-permute-done.7 = f32[256,128]{1,0:T(8,128)S(1)} collective-permute-done((f32[256,128]{1,0:T(8,128)S(1)}, f32[256,128]{1,0:T(8,128)S(1)}, u32[]{:S(2)}, u32[]{:S(2)}) %collective-permute-start.7) | collective-permute-done | bytes 131104 | tf_op jit(solution)/shard_map/ppermute | solution.py:511
  40.0 1.1 %collective-permute-start.8 = (f32[256,128]{1,0:T(8,128)S(1)}, f32[256,128]{1,0:T(8,128)S(1)}, u32[]{:S(2)}, u32[]{:S(2)}) collective-permute-start(f32[256,128]{1,0:T(8,128)S(1)} %add.28.rest_2_), channel_id=1, source_target_pairs={{0,2},{1,3},{2,0},{3,1},{4,6},{5,7},{6,4},{7,5},{8,10},{9,11},{10,... | collective-permute-start | bytes 393224 | tf_op jit(solution)/shard_map/ppermute | solution.py:511
  41.1 1.6 %collective-permute-done.10 = f32[256,128]{1,0:T(8,128)S(1)} collective-permute-done((f32[256,128]{1,0:T(8,128)S(1)}, f32[256,128]{1,0:T(8,128)S(1)}, u32[]{:S(2)}, u32[]{:S(2)}) %collective-permute-start.10) | collective-permute-done | bytes 131104 | tf_op jit(solution)/shard_map/ppermute | solution.py:511
  42.8 2.0 %collective-permute-start.11 = (f32[256,128]{1,0:T(8,128)S(1)}, f32[256,128]{1,0:T(8,128)S(1)}, u32[]{:S(2)}, u32[]{:S(2)}) collective-permute-start(f32[256,128]{1,0:T(8,128)S(1)} %add.30.refs_0_), channel_id=1, source_target_pairs={{0,1},{1,0},{2,3},{3,2},{4,5},{5,4},{6,7},{7,6},{8,9},{9,8},{10,11... | collective-permute-start | bytes 393224 | tf_op jit(solution)/shard_map/ppermute | solution.py:511
  44.8 3.9 %grads.3 = (bf16[512,1024]{1,0:T(8,128)(2,1)}, f32[16,512]{1,0:T(8,128)}) custom-call(s32[8]{0:T(128)S(1)} %stack.29.s.sel, bf16[512,1024]{1,0:T(8,128)(2,1)S(1)} %copy-done, bf16[2,512,512]{2,1,0:T(8,128)(2,1)S(1)} %copy-done.4, bf16[512,128]{1,0:T(8,128)(2,1)S(1)} %copy-done.7, ...), custom_call_target="tpu_custom_call", output_to_operand_aliasing={{0}: (13, {}), {1}: (14, {})} | custom-call | flops 1000 | bytes 1000 | tf_op jit(solution)/shard_map/grads/pallas_call | solution.py:444
  48.7 0.2 collective-permute-start.9
  48.9 0.7 %collective-permute-done.11.refs_1_ = f32[256,128]{1,0:T(8,128)S(1)} collective-permute-done((f32[256,128]{1,0:T(8,128)S(1)}, f32[256,128]{1,0:T(8,128)S(1)}, u32[]{:S(2)}, u32[]{:S(2)}) %collective-permute-start.11) | collective-permute-done | bytes 131104 | tf_op jit(solution)/shard_map/ppermute | solution.py:511
  49.5 1.3 %join.2 = (f32[512,128]{1,0:T(8,128)}, f32[512,128]{1,0:T(8,128)}) custom-call(s32[8]{0:T(128)S(1)} %stack.29.s.sel, f32[256,128]{1,0:T(8,128)S(1)} %add.30.refs_0_, f32[256,128]{1,0:T(8,128)S(1)} %collective-permute-done.11.refs_1_, f32[256,128]{1,0:T(8,128)S(1)} %add.29.refs_2_), custom_call_target="tpu_custom_call" | custom-call | flops 1000 | bytes 1000 | tf_op jit(solution)/shard_map/join/pallas_call | solution.py:492
  50.9 2.9 %collective-permute-done.9.refs_0_ = f32[256,128]{1,0:T(8,128)S(1)} collective-permute-done((f32[256,128]{1,0:T(8,128)S(1)}, f32[256,128]{1,0:T(8,128)S(1)}, u32[]{:S(2)}, u32[]{:S(2)}) %collective-permute-start.9) | collective-permute-done | bytes 131104 | tf_op jit(solution)/shard_map/ppermute | solution.py:511
  53.7 1.2 %join.3 = (f32[512,128]{1,0:T(8,128)}, f32[512,128]{1,0:T(8,128)}) custom-call(s32[8]{0:T(128)S(1)} %stack.29.s.sel, f32[256,128]{1,0:T(8,128)S(1)} %collective-permute-done.9.refs_0_, f32[512,128]{1,0:T(8,128)} %get-tuple-element.65.refs_1_, f32[512,128]{1,0:T(8,128)} %get-tuple-element.66.refs_2_), custom_call_target="tpu_custom_call", output_to_operand_aliasing={{0}: (2, {}), {1}: (3, {})} | custom-call | flops 1000 | bytes 1000 | tf_op jit(solution)/shard_map/join/pallas_call | solution.py:492
  (37 shorter events, 0.3 us)
Async XLA Ops:
  0.6 4.1 %copy-start = (bf16[512,1024]{1,0:T(8,128)(2,1)S(1)}, bf16[512,1024]{1,0:T(8,128)(2,1)}, u32[]{:S(2)}) copy-start(bf16[512,1024]{1,0:T(8,128)(2,1)} %x_ref.5) | copy-start | bytes 3145732
  0.6 4.1 %copy-start.3 = (bf16[512,1024]{1,0:T(8,128)(2,1)S(1)}, bf16[512,1024]{1,0:T(8,128)(2,1)}, u32[]{:S(2)}) copy-start(bf16[512,1024]{1,0:T(8,128)(2,1)} %g_ref.1) | copy-start | bytes 3145732
  0.7 4.1 %copy-start.7 = (bf16[512,128]{1,0:T(8,128)(2,1)S(1)}, bf16[512,128]{1,0:T(8,128)(2,1)}, u32[]{:S(2)}) copy-start(bf16[512,128]{1,0:T(8,128)(2,1)} %w_ref.5) | copy-start | bytes 393220
  0.7 4.1 %copy-start.8 = (bf16[512,128]{1,0:T(8,128)(2,1)S(1)}, bf16[512,128]{1,0:T(8,128)(2,1)}, u32[]{:S(2)}) copy-start(bf16[512,128]{1,0:T(8,128)(2,1)} %r_ref.5) | copy-start | bytes 393220
  0.7 4.1 %copy-start.9 = (f32[16,512]{1,0:T(8,128)S(1)}, f32[16,512]{1,0:T(8,128)}, u32[]{:S(2)}) copy-start(f32[16,512]{1,0:T(8,128)} %ld_ref.5) | copy-start | bytes 98308
  4.2 2.8 %collective-permute-start = (f32[264,512]{1,0:T(8,128)}, f32[264,512]{1,0:T(8,128)S(1)}, u32[]{:S(2)}, u32[]{:S(2)}) collective-permute-start(f32[264,512]{1,0:T(8,128)} %get-tuple-element.39.pay_ref), channel_id=1, source_target_pairs={{0,4},{4,0},{8,12},{12,8},{16,20},{20,16},{24,28},{28,24},{1,5},{5... | collective-permute-start | bytes 1622024 | tf_op jit(solution)/shard_map/ppermute | solution.py:511
  7.7 9.9 %collective-permute-start.1 = (f32[136,512]{1,0:T(8,128)S(1)}, f32[136,512]{1,0:T(8,128)S(1)}, u32[]{:S(2)}, u32[]{:S(2)}) collective-permute-start(f32[136,512]{1,0:T(8,128)S(1)} %get-tuple-element.40.rest_0_.refs_1_), channel_id=1, source_target_pairs={{0,8},{4,12},{8,0},{12,4},{16,24},{20,28},{24,16},{28,20},{1,9},{5... | collective-permute-start | bytes 835592 | tf_op jit(solution)/shard_map/ppermute | solution.py:511
  17.6 4.1 %copy-start.2 = (bf16[2,512,512]{2,1,0:T(8,128)(2,1)S(1)}, bf16[2,512,512]{2,1,0:T(8,128)(2,1)}, u32[]{:S(2)}) copy-start(bf16[2,512,512]{2,1,0:T(8,128)(2,1)} %get-tuple-element.48.refs_0_.gw_ref) | copy-start | bytes 3145732
  17.6 4.1 %copy-start.6 = (f32[256,512]{1,0:T(8,128)S(1)}, f32[256,512]{1,0:T(8,128)}, u32[]{:S(2)}) copy-start(f32[256,512]{1,0:T(8,128)} %get-tuple-element.50.refs_2_.part_ref) | copy-start | bytes 1572868
  17.6 4.1 %copy-start.11 = (f32[16,512]{1,0:T(8,128)S(1)}, f32[16,512]{1,0:T(8,128)}, u32[]{:S(2)}) copy-start(f32[16,512]{1,0:T(8,128)} %get-tuple-element.51.refs_3_.tot_ref) | copy-start | bytes 98308
  18.2 4.3 %copy-start.4 = (bf16[2,512,512]{2,1,0:T(8,128)(2,1)S(1)}, bf16[2,512,512]{2,1,0:T(8,128)(2,1)}, u32[]{:S(2)}) copy-start(bf16[2,512,512]{2,1,0:T(8,128)(2,1)} %get-tuple-element.37.refs_0_.gw_ref) | copy-start | bytes 3145732
  18.3 4.3 %copy-start.5 = (f32[256,512]{1,0:T(8,128)S(1)}, f32[256,512]{1,0:T(8,128)}, u32[]{:S(2)}) copy-start(f32[256,512]{1,0:T(8,128)} %get-tuple-element.43.refs_2_.part_ref) | copy-start | bytes 1572868
  18.3 4.3 %copy-start.10 = (f32[16,512]{1,0:T(8,128)S(1)}, f32[16,512]{1,0:T(8,128)}, u32[]{:S(2)}) copy-start(f32[16,512]{1,0:T(8,128)} %get-tuple-element.44.refs_3_.tot_ref) | copy-start | bytes 98308
  18.3 4.3 %collective-permute-start.2 = (f32[128,512]{1,0:T(8,128)S(1)}, f32[128,512]{1,0:T(8,128)S(1)}, u32[]{:S(2)}, u32[]{:S(2)}) collective-permute-start(f32[128,512]{1,0:T(8,128)S(1)} %get-tuple-element.45), channel_id=1, source_target_pairs={{0,4},{4,0},{8,12},{12,8},{16,20},{20,16},{24,28},{28,24},{1,5},{5... | collective-permute-start | bytes 786440 | tf_op jit(solution)/shard_map/ppermute | solution.py:511
  18.4 10.5 %collective-permute-start.3 = (f32[128,512]{1,0:T(8,128)S(1)}, f32[128,512]{1,0:T(8,128)S(1)}, u32[]{:S(2)}, u32[]{:S(2)}) collective-permute-start(f32[128,512]{1,0:T(8,128)S(1)} %get-tuple-element.46), channel_id=1, source_target_pairs={{0,8},{4,12},{8,0},{12,4},{16,24},{20,28},{24,16},{28,20},{1,9},{5... | collective-permute-start | bytes 786440 | tf_op jit(solution)/shard_map/ppermute | solution.py:511
  20.2 8.7 %collective-permute-start.4 = (f32[128,512]{1,0:T(8,128)S(1)}, f32[128,512]{1,0:T(8,128)S(1)}, u32[]{:S(2)}, u32[]{:S(2)}) collective-permute-start(f32[128,512]{1,0:T(8,128)S(1)} %get-tuple-element.47), channel_id=1, source_target_pairs={{0,16},{4,20},{8,24},{12,28},{16,0},{20,4},{24,8},{28,12},{1,17},{... | collective-permute-start | bytes 786440 | tf_op jit(solution)/shard_map/ppermute | solution.py:511
  23.5 5.4 %collective-permute-start.5 = (f32[256,128]{1,0:T(8,128)S(1)}, f32[256,128]{1,0:T(8,128)S(1)}, u32[]{:S(2)}, u32[]{:S(2)}) collective-permute-start(f32[256,128]{1,0:T(8,128)S(1)} %get-tuple-element.54), channel_id=1, source_target_pairs={{0,1},{1,0},{2,3},{3,2},{4,5},{5,4},{6,7},{7,6},{8,9},{9,8},{10,11... | collective-permute-start | bytes 393224 | tf_op jit(solution)/shard_map/ppermute | solution.py:511
  29.5 1.6 %collective-permute-start.6 = (f32[128,512]{1,0:T(8,128)S(1)}, f32[128,512]{1,0:T(8,128)S(1)}, u32[]{:S(2)}, u32[]{:S(2)}) collective-permute-start(f32[128,512]{1,0:T(8,128)S(1)} %get-tuple-element.55), channel_id=1, source_target_pairs={{0,4},{4,0},{8,12},{12,8},{16,20},{20,16},{24,28},{28,24},{1,5},{5... | collective-permute-start | bytes 786440 | tf_op jit(solution)/shard_map/ppermute | solution.py:511
  29.6 6.7 %copy-start.1 = (f32[512,1024]{1,0:T(8,128)S(1)}, f32[512,1024]{1,0:T(8,128)}, u32[]{:S(2)}) copy-start(f32[512,1024]{1,0:T(8,128)} %get-tuple-element.41.refs_6_.gint_ref) | copy-start | bytes 6291460
  29.6 6.7 %copy-start.12 = (f32[16,512]{1,0:T(8,128)S(1)}, f32[16,512]{1,0:T(8,128)}, u32[]{:S(2)}) copy-start(f32[16,512]{1,0:T(8,128)} %get-tuple-element.42.dot_ref) | copy-start | bytes 98308
  32.0 7.9 %collective-permute-start.7 = (f32[256,128]{1,0:T(8,128)S(1)}, f32[256,128]{1,0:T(8,128)S(1)}, u32[]{:S(2)}, u32[]{:S(2)}) collective-permute-start(f32[256,128]{1,0:T(8,128)S(1)} %get-tuple-element.57.rest_0_), channel_id=1, source_target_pairs={{0,1},{1,0},{2,3},{3,2},{4,5},{5,4},{6,7},{7,6},{8,9},{9,8},{10,11... | collective-permute-start | bytes 393224 | tf_op jit(solution)/shard_map/ppermute | solution.py:511
  33.7 9.1 %collective-permute-start.10 = (f32[256,128]{1,0:T(8,128)S(1)}, f32[256,128]{1,0:T(8,128)S(1)}, u32[]{:S(2)}, u32[]{:S(2)}) collective-permute-start(f32[256,128]{1,0:T(8,128)S(1)} %add.27.refs_7_), channel_id=1, source_target_pairs={{0,2},{1,3},{2,0},{3,1},{4,6},{5,7},{6,4},{7,5},{8,10},{9,11},{10,... | collective-permute-start | bytes 393224 | tf_op jit(solution)/shard_map/ppermute | solution.py:511
  40.0 8.7 %collective-permute-start.8 = (f32[256,128]{1,0:T(8,128)S(1)}, f32[256,128]{1,0:T(8,128)S(1)}, u32[]{:S(2)}, u32[]{:S(2)}) collective-permute-start(f32[256,128]{1,0:T(8,128)S(1)} %add.28.rest_2_), channel_id=1, source_target_pairs={{0,2},{1,3},{2,0},{3,1},{4,6},{5,7},{6,4},{7,5},{8,10},{9,11},{10,... | collective-permute-start | bytes 393224 | tf_op jit(solution)/shard_map/ppermute | solution.py:511
  42.8 6.8 %collective-permute-start.11 = (f32[256,128]{1,0:T(8,128)S(1)}, f32[256,128]{1,0:T(8,128)S(1)}, u32[]{:S(2)}, u32[]{:S(2)}) collective-permute-start(f32[256,128]{1,0:T(8,128)S(1)} %add.30.refs_0_), channel_id=1, source_target_pairs={{0,1},{1,0},{2,3},{3,2},{4,5},{5,4},{6,7},{7,6},{8,9},{9,8},{10,11... | collective-permute-start | bytes 393224 | tf_op jit(solution)/shard_map/ppermute | solution.py:511
  48.7 5.0 %collective-permute-start.9 = (f32[256,128]{1,0:T(8,128)S(1)}, f32[256,128]{1,0:T(8,128)S(1)}, u32[]{:S(2)}, u32[]{:S(2)}) collective-permute-start(f32[256,128]{1,0:T(8,128)S(1)} %add.29.refs_2_), channel_id=1, source_target_pairs={{0,1},{1,0},{2,3},{3,2},{4,5},{5,4},{6,7},{7,6},{8,9},{9,8},{10,11... | collective-permute-start | bytes 393224 | tf_op jit(solution)/shard_map/ppermute | solution.py:511

commit v7 on v6

--- a/solution.py
+++ b/solution.py
@@ -261,12 +261,16 @@
 
 def late_kernel(way, sel, wg_ref, car_ref, part_ref, tot_ref, acc_ref, out_ref):
     car = car_ref[...]
-    onward = tot_ref[0:1, :] * car + part_ref[...]
-    forward = sel[way] == 0
+    width = car_ref.shape[0]
+    chosen = sel[way]
+    part = part_ref[pl.ds(pl.multiple_of(chosen * width, width), width), :]
+    onward = tot_ref[pl.ds(pl.multiple_of(chosen * 8, 8), 8), :][0:1] * car + part
+    forward = chosen == 0
+    of = chosen if acc_ref.shape[0] == 2 else 0
     for b in range(2):
         at = slice(b * Q, (b + 1) * Q)
         held = jnp.where(forward, onward if b else car, car if b else onward).astype(BF16)
-        out_ref[at, :] = acc_ref[0, at, :] + dot_t(wg_ref[0, at, :], held)
+        out_ref[at, :] = acc_ref[of, at, :] + dot_t(wg_ref[chosen, at, :], held)
 
 
 def cut_kernel(way, sel, wg_ref, car_ref, part_ref, tot_ref, acc_ref, keep_ref, send_ref, total):
@@ -280,24 +284,55 @@
 def late(way, sel, state, carried, acc, cut, name):
     _, wg, part, tot = state
     rows = wg.shape[1]
-    width, lanes = carried.shape
-    both = acc.shape[0] == 2
+    width = carried.shape[0]
     outs = [shape_of((rows // 2, width))] * 2 if cut else [shape_of((rows, width))]
-    return call(
+    here = pl.BlockSpec(memory_space=pltpu.VMEM)
+    return pl.pallas_call(
         functools.partial(cut_kernel if cut else late_kernel, way),
-        name,
-        sel,
-        [wg, carried, part, tot, acc],
-        outs,
-        in_specs=[
-            pl.BlockSpec((1, rows, lanes), lambda i, s: (s[way], 0, 0)),
-            full(carried),
-            pl.BlockSpec((width, lanes), lambda i, s: (s[way], 0)),
-            pl.BlockSpec((8, lanes), lambda i, s: (s[way], 0)),
-            pl.BlockSpec((1, rows, width), lambda i, s: (s[way] if both else 0, 0, 0)),
-        ],
-        scratch=[pltpu.VMEM((rows, width), F32)] if cut else [],
-    )
+        in_specs=[pl.BlockSpec(memory_space=pltpu.SMEM)] + [here] * 5,
+        out_specs=[here] * len(outs),
+        out_shape=outs,
+        scratch_shapes=[pltpu.VMEM((rows, width), F32)] if cut else [],
+        compiler_params=params(),
+        cost_estimate=FREE,
+        name=name,
+    )(sel, wg, carried, part, tot, acc)
+
+
+def both_kernel(way, sel, *refs):
+    first, second, (acc_ref, keep_ref, send_ref, total) = refs[:4], refs[4:8], refs[8:]
+    chosen = sel[way]
+    forward = chosen == 0
+    helds = []
+    for wg_ref, car_ref, part_ref, tot_ref in (first, second):
+        width = car_ref.shape[0]
+        car = car_ref[...]
+        part = part_ref[pl.ds(pl.multiple_of(chosen * width, width), width), :]
+        onward = tot_ref[pl.ds(pl.multiple_of(chosen * 8, 8), 8), :][0:1] * car + part
+        helds.append([jnp.where(forward, a, c).astype(BF16) for a, c in ((car, onward), (onward, car))])
+    for b in range(2):
+        at = slice(b * Q, (b + 1) * Q)
+        sums = dot_t(first[0][chosen, at, :], helds[0][b]) + dot_t(second[0][chosen, at, :], helds[1][b])
+        total[at, :] = acc_ref[chosen, at, :] + sums
+    step = keep_ref.shape[0]
+    odd = sel[5] % 2
+    keep_ref[...] = total[pl.ds(pl.multiple_of(odd * step, step), step), :]
+    send_ref[...] = total[pl.ds(pl.multiple_of((1 - odd) * step, step), step), :]
+
+
+def late_both(way, sel, mine, own, other, got, acc, name):
+    rows, width = acc.shape[1:]
+    here = pl.BlockSpec(memory_space=pltpu.VMEM)
+    return pl.pallas_call(
+        functools.partial(both_kernel, way),
+        in_specs=[pl.BlockSpec(memory_space=pltpu.SMEM)] + [here] * 9,
+        out_specs=[here] * 2,
+        out_shape=[shape_of((rows // 2, width))] * 2,
+        scratch_shapes=[pltpu.VMEM((rows, width), F32)],
+        compiler_params=params(),
+        cost_estimate=FREE,
+        name=name,
+    )(sel, mine[1], own, *mine[2:], other[1], got, *other[2:], acc)
 
 
 def decay_blocks(running):
@@ -563,8 +598,7 @@
         near_own, send, pair = carry(0, sel, [rx, px], mine[0], got, (far_off(gint),))
         ry = swap(pair, "seq", 4)
         near_got = swap(send, "seq", 1)
-        (acc,) = late(0, sel, mine, near_own, early, False, "late_near_mine")
-        near_parts = late(0, sel, other, near_got, acc[None], True, "late_near_other")
+        near_parts = late_both(0, sel, mine, near_own, other, near_got, early, "late_near")
         near_half = near_parts[0] + swap(near_parts[1], "head", 1)
         near_cross = swap(near_half, "head", 2)
         far_own, send = carry(1, sel, [rx, sx, ry], mine[0], got, (near_half,))

time: 55.1 us -> 54.8 us (level)
  Pallas kernels: 26.2 us -> 25.5 us
    pallas_call x7 -> x3, Pallas kernels: 5.47 us -> 1.95 us  [call(): pl.pallas_call(body, grid_spec=pltpu.PrefetchScalarGridSpec(num_scalar_pr...]
    pallas_call x0 -> x3, Pallas kernels: none -> 2.81 us  [the longest x2 1.75 us: late(): pl.pallas_call(functools.partial(cut_kernel if cut else late_kernel, way)...]
  transfers between devices with their start and end apart: 12 -> 12, of which waited for: 7 -> 8; matrix products, arithmetic and copies ran while one was open for 0% -> 0% of each run, Pallas kernels for 34% -> 33%
where the time goes in v7:
time: 54.8 us; the launch traced here: 54.6 us
  Pallas kernels  25.5 us (47%)
  starting transfers between devices  15.7 us (29%)
  waiting for transfers between devices  12.2 us (22%)
  between operations  0.92 us (2%)
    ppermute x12, starting transfers between devices, swap(): return lax.ppermute(values, axis, [(i, i ^ mask) for i in range(count)])  15.7 us
    ppermute x12, waiting for transfers between devices, swap(): return lax.ppermute(values, axis, [(i, i ^ mask) for i in range(count)])  12.2 us
    pallas_call x2, Pallas kernels, grads(): pl.pallas_call(functools.partial(grads_kernel, scale), grid_spec=pltpu.Pr...  6.74 us
    pallas_call x1, Pallas kernels, scores(): pl.pallas_call(scores_kernel, grid=(rows // Q, heads // GROUP), in_specs=...  5.82 us
    pallas_call x2, Pallas kernels, states(): pl.pallas_call(loaded_kernel if loaded else state_kernel, grid_spec=pltpu...  5.64 us
    pallas_call x2, Pallas kernels, join(): pl.pallas_call(functools.partial(join_kernel, places), grid_spec=pltpu.Pr...  2.52 us
    pallas_call x3, Pallas kernels, call(): pl.pallas_call(body, grid_spec=pltpu.PrefetchScalarGridSpec(num_scalar_pr...  1.95 us
    pallas_call x2, Pallas kernels, late(): pl.pallas_call(functools.partial(cut_kernel if cut else late_kernel, way)...  1.75 us
  transfers between devices with their start and end apart: 12, of which 8 were waited for; matrix products, arithmetic and copies ran while one was open for 0% of the time, Pallas kernels for 33%

profile of v7, /device:TPU:0, one launch (start us, length us, event | category | flops | bytes accessed | tf_op | source)
XLA Modules:
  0.0 54.6 jit_solution(6406861158375257316)
XLA Ops:
  0.7 3.5 %states.2 = (f32[264,512]{1,0:T(8,128)}, bf16[2,512,512]{2,1,0:T(8,128)(2,1)}, f32[256,512]{1,0:T(8,128)}, f32[16,512]{1,0:T(8,128)}) custom-call(s32[1]{0:T(128)} %bitcast.5.sel, bf16[512,1024]{1,0:T(8,128)(2,1)} %x_ref.5, bf16[512,1024]{1,0:T(8,128)(2,1)} %g_ref.1, bf16[512,128]{1,0:T(8,128)(2,1)} %w_ref.5, bf16[512,128]{1,0:T(8,128)(2,1)} %r_ref.5, ...), custom_call_target="tpu_custom_call" | custom-call | flops 1000 | bytes 1000 | tf_op jit(solution)/shard_map/states/pallas_call | solution.py:161
  4.2 0.5 collective-permute-start
  4.8 2.1 %states.3 = (f32[264,512]{1,0:T(8,128)S(1)}, bf16[2,512,512]{2,1,0:T(8,128)(2,1)}, f32[256,512]{1,0:T(8,128)}, f32[16,512]{1,0:T(8,128)}) custom-call(s32[1]{0:T(128)} %bitcast.2.sel, bf16[512,1024]{1,0:T(8,128)(2,1)S(1)} %copy-done, bf16[512,1024]{1,0:T(8,128)(2,1)S(1)} %copy-done.4, bf16[512,128]{1,0:T(8,128)(2,1)S(1)} %copy-done.7, ...), custom_call_target="tpu_custom_call" | custom-call | flops 1000 | bytes 1000 | tf_op jit(solution)/shard_map/states/pallas_call | solution.py:161
  6.9 0.1 stack.29.s.sel
  7.0 0.7 %chip.1 = (f32[136,512]{1,0:T(8,128)S(1)}, f32[128,512]{1,0:T(8,128)S(1)}) custom-call(s32[8]{0:T(128)S(1)} %stack.29.s.sel, f32[264,512]{1,0:T(8,128)S(1)} %get-tuple-element.38.refs_0_.refs_2_.refs_4_.refs_3_.refs_5_.pay_ref, f32[264,512]{1,0:T(8,128)S(1)} %collective-permute-done.refs_1_.refs_3_.refs_5_.refs_4_.refs_6_), custom_call_target="tpu_custom_call" | custom-call | flops 1000 | bytes 1000 | tf_op jit(solution)/shard_map/chip/pallas_call | solution.py:210
  7.7 2.6 %collective-permute-start.1 = (f32[136,512]{1,0:T(8,128)S(1)}, f32[136,512]{1,0:T(8,128)S(1)}, u32[]{:S(2)}, u32[]{:S(2)}) collective-permute-start(f32[136,512]{1,0:T(8,128)S(1)} %get-tuple-element.40.rest_0_.refs_1_), channel_id=1, source_target_pairs={{0,8},{4,12},{8,0},{12,4},{16,24},{20,28},{24,16},{28,20},{1,9},{5... | collective-permute-start | bytes 835592 | tf_op jit(solution)/shard_map/ppermute | solution.py:546
  10.3 5.8 %scores.1 = (f32[2,512,128]{2,1,0:T(8,128)S(1)}, f32[512,1024]{1,0:T(8,128)}, f32[16,512]{1,0:T(8,128)}) custom-call(bf16[512,1024]{1,0:T(8,128)(2,1)S(1)} %copy-done, bf16[512,1024]{1,0:T(8,128)(2,1)S(1)} %copy-done.4, bf16[512,128]{1,0:T(8,128)(2,1)S(1)} %copy-done.7, bf16[512,128]{1,0:T(8,128)(2,1)S(1)} %copy-done.8, f32[16,512]{1,0:T(8,128)S(1)} %copy-done.9, ...), custom_call_target="tpu_custom_call" | custom-call | flops 1000 | bytes 1000 | tf_op jit(solution)/shard_map/scores/pallas_call | solution.py:421
  16.1 1.5 %collective-permute-done.1.refs_0_ = f32[136,512]{1,0:T(8,128)S(1)} collective-permute-done((f32[136,512]{1,0:T(8,128)S(1)}, f32[136,512]{1,0:T(8,128)S(1)}, u32[]{:S(2)}, u32[]{:S(2)}) %collective-permute-start.1) | collective-permute-done | bytes 278560 | tf_op jit(solution)/shard_map/ppermute | solution.py:546
  17.6 0.7 %carry_near.1 = (f32[128,512]{1,0:T(8,128)S(1)}, f32[128,512]{1,0:T(8,128)S(1)}, f32[128,512]{1,0:T(8,128)S(1)}) custom-call(s32[8]{0:T(128)S(1)} %stack.29.s.sel, f32[136,512]{1,0:T(8,128)S(1)} %collective-permute-done.1.refs_0_, f32[136,512]{1,0:T(8,128)S(1)} %get-tuple-element.40.rest_0_.refs_1_, ...), custom_call_target="tpu_custom_call" | custom-call | flops 1000 | bytes 1000 | tf_op jit(solution)/shard_map/carry_near/pallas_call | solution.py:210
  18.4 1.8 %collective-permute-start.3 = (f32[128,512]{1,0:T(8,128)S(1)}, f32[128,512]{1,0:T(8,128)S(1)}, u32[]{:S(2)}, u32[]{:S(2)}) collective-permute-start(f32[128,512]{1,0:T(8,128)S(1)} %get-tuple-element.46), channel_id=1, source_target_pairs={{0,8},{4,12},{8,0},{12,4},{16,24},{20,28},{24,16},{28,20},{1,9},{5... | collective-permute-start | bytes 786440 | tf_op jit(solution)/shard_map/ppermute | solution.py:546
  20.2 1.5 %collective-permute-start.4 = (f32[128,512]{1,0:T(8,128)S(1)}, f32[128,512]{1,0:T(8,128)S(1)}, u32[]{:S(2)}, u32[]{:S(2)}) collective-permute-start(f32[128,512]{1,0:T(8,128)S(1)} %get-tuple-element.47), channel_id=1, source_target_pairs={{0,16},{4,20},{8,24},{12,28},{16,0},{20,4},{24,8},{28,12},{1,17},{... | collective-permute-start | bytes 786440 | tf_op jit(solution)/shard_map/ppermute | solution.py:546
  21.7 1.1 %late_near.1 = (f32[256,128]{1,0:T(8,128)S(1)}, f32[256,128]{1,0:T(8,128)S(1)}) custom-call(s32[8]{0:T(128)S(1)} %stack.29.s.sel, bf16[2,512,512]{2,1,0:T(8,128)(2,1)S(1)} %copy-done.2, f32[128,512]{1,0:T(8,128)S(1)} %get-tuple-element.49.refs_1_.near_ref, f32[256,512]{1,0:T(8,128)S(1)} %copy-done.5, f32[16,512]{1,0:T(8,128)S(1)} %copy-done.11, ...), custom_call_target="tpu_custom_call" | custom-call | flops 1000 | bytes 1000 | tf_op jit(solution)/shard_map/late_near/pallas_call | solution.py:326
  22.8 1.6 %collective-permute-start.5 = (f32[256,128]{1,0:T(8,128)S(1)}, f32[256,128]{1,0:T(8,128)S(1)}, u32[]{:S(2)}, u32[]{:S(2)}) collective-permute-start(f32[256,128]{1,0:T(8,128)S(1)} %get-tuple-element.54), channel_id=1, source_target_pairs={{0,1},{1,0},{2,3},{3,2},{4,5},{5,4},{6,7},{7,6},{8,9},{9,8},{10,11... | collective-permute-start | bytes 393224 | tf_op jit(solution)/shard_map/ppermute | solution.py:546
  24.4 3.7 %collective-permute-done.5 = f32[256,128]{1,0:T(8,128)S(1)} collective-permute-done((f32[256,128]{1,0:T(8,128)S(1)}, f32[256,128]{1,0:T(8,128)S(1)}, u32[]{:S(2)}, u32[]{:S(2)}) %collective-permute-start.5) | collective-permute-done | bytes 131104 | tf_op jit(solution)/shard_map/ppermute | solution.py:546
  28.2 0.4 collective-permute-done.4.refs_2_
  28.5 0.6 %carry_far.1 = (f32[128,512]{1,0:T(8,128)S(1)}, f32[128,512]{1,0:T(8,128)S(1)}) custom-call(s32[8]{0:T(128)S(1)} %stack.29.s.sel, f32[136,512]{1,0:T(8,128)S(1)} %collective-permute-done.1.refs_0_, f32[128,512]{1,0:T(8,128)S(1)} %collective-permute-done.3.refs_1_, f32[128,512]{1,0:T(8,128)S(1)} %collective-permute-done.4.refs_2_, ...), custom_call_target="tpu_custom_call" | custom-call | flops 1000 | bytes 1000 | tf_op jit(solution)/shard_map/carry_far/pallas_call | solution.py:210
  29.3 0.9 %late_far_mine.1 = f32[512,128]{1,0:T(8,128)S(1)} custom-call(s32[8]{0:T(128)S(1)} %stack.29.s.sel, bf16[2,512,512]{2,1,0:T(8,128)(2,1)S(1)} %copy-done.2, f32[128,512]{1,0:T(8,128)S(1)} %get-tuple-element.56.car_ref.far_ref, f32[256,512]{1,0:T(8,128)S(1)} %copy-done.5, f32[16,512]{1,0:T(8,128)S(1)} %copy-done.11, ...), custom_call_target="tpu_custom_call" | custom-call | flops 1000 | bytes 1000 | tf_op jit(solution)/shard_map/late_far_mine/pallas_call | solution.py:290
  30.1 0.6 %collective-permute-done.6.car_ref.far_ref = f32[128,512]{1,0:T(8,128)S(1)} collective-permute-done((f32[128,512]{1,0:T(8,128)S(1)}, f32[128,512]{1,0:T(8,128)S(1)}, u32[]{:S(2)}, u32[]{:S(2)}) %collective-permute-start.6) | collective-permute-done | bytes 262176 | tf_op jit(solution)/shard_map/ppermute | solution.py:546
  30.8 0.9 %late_far_other.1 = (f32[256,128]{1,0:T(8,128)S(1)}, f32[256,128]{1,0:T(8,128)S(1)}) custom-call(s32[8]{0:T(128)S(1)} %stack.29.s.sel, bf16[2,512,512]{2,1,0:T(8,128)(2,1)S(1)} %copy-done.3, f32[128,512]{1,0:T(8,128)S(1)} %collective-permute-done.6.car_ref.far_ref, f32[256,512]{1,0:T(8,128)S(1)} %copy-done.6, f32[16,512]{1,0:T(8,128)S(1)} %copy-done.10, ...), custom_call_target="tpu_custom_call" | custom-call | flops 1000 | bytes 1000 | tf_op jit(solution)/shard_map/late_far_other/pallas_call | solution.py:290
  31.7 1.6 %collective-permute-start.7 = (f32[256,128]{1,0:T(8,128)S(1)}, f32[256,128]{1,0:T(8,128)S(1)}, u32[]{:S(2)}, u32[]{:S(2)}) collective-permute-start(f32[256,128]{1,0:T(8,128)S(1)} %get-tuple-element.57.rest_0_), channel_id=1, source_target_pairs={{0,1},{1,0},{2,3},{3,2},{4,5},{5,4},{6,7},{7,6},{8,9},{9,8},{10,11... | collective-permute-start | bytes 393224 | tf_op jit(solution)/shard_map/ppermute | solution.py:546
  33.3 2.6 %collective-permute-start.10 = (f32[256,128]{1,0:T(8,128)S(1)}, f32[256,128]{1,0:T(8,128)S(1)}, u32[]{:S(2)}, u32[]{:S(2)}) collective-permute-start(f32[256,128]{1,0:T(8,128)S(1)} %add.27.refs_7_), channel_id=1, source_target_pairs={{0,2},{1,3},{2,0},{3,1},{4,6},{5,7},{6,4},{7,5},{8,10},{9,11},{10,... | collective-permute-start | bytes 393224 | tf_op jit(solution)/shard_map/ppermute | solution.py:546
  35.9 2.8 %grads.2 = (bf16[512,1024]{1,0:T(8,128)(2,1)}, f32[16,512]{1,0:T(8,128)}) custom-call(s32[8]{0:T(128)S(1)} %stack.29.s.sel, bf16[512,1024]{1,0:T(8,128)(2,1)S(1)} %copy-done, bf16[2,512,512]{2,1,0:T(8,128)(2,1)S(1)} %copy-done.2, bf16[512,128]{1,0:T(8,128)(2,1)S(1)} %copy-done.7, bf16[512,128]{1,0:T(8,128)(2,1)S(1)} %copy-done.8, f32[16,512]{1,0:T(8,128)S(1)} %copy-done.9, ...), custom_call_target="tpu_custom_call" | custom-call | flops 1000 | bytes 1000 | tf_op jit(solution)/shard_map/grads/pallas_call | solution.py:479
  38.7 0.9 %collective-permute-done.7 = f32[256,128]{1,0:T(8,128)S(1)} collective-permute-done((f32[256,128]{1,0:T(8,128)S(1)}, f32[256,128]{1,0:T(8,128)S(1)}, u32[]{:S(2)}, u32[]{:S(2)}) %collective-permute-start.7) | collective-permute-done | bytes 131104 | tf_op jit(solution)/shard_map/ppermute | solution.py:546
  39.6 1.1 %collective-permute-start.8 = (f32[256,128]{1,0:T(8,128)S(1)}, f32[256,128]{1,0:T(8,128)S(1)}, u32[]{:S(2)}, u32[]{:S(2)}) collective-permute-start(f32[256,128]{1,0:T(8,128)S(1)} %add.28.rest_2_), channel_id=1, source_target_pairs={{0,2},{1,3},{2,0},{3,1},{4,6},{5,7},{6,4},{7,5},{8,10},{9,11},{10,... | collective-permute-start | bytes 393224 | tf_op jit(solution)/shard_map/ppermute | solution.py:546
  40.8 1.6 %collective-permute-done.10 = f32[256,128]{1,0:T(8,128)S(1)} collective-permute-done((f32[256,128]{1,0:T(8,128)S(1)}, f32[256,128]{1,0:T(8,128)S(1)}, u32[]{:S(2)}, u32[]{:S(2)}) %collective-permute-start.10) | collective-permute-done | bytes 131104 | tf_op jit(solution)/shard_map/ppermute | solution.py:546
  42.4 2.0 %collective-permute-start.11 = (f32[256,128]{1,0:T(8,128)S(1)}, f32[256,128]{1,0:T(8,128)S(1)}, u32[]{:S(2)}, u32[]{:S(2)}) collective-permute-start(f32[256,128]{1,0:T(8,128)S(1)} %add.30.refs_0_), channel_id=1, source_target_pairs={{0,1},{1,0},{2,3},{3,2},{4,5},{5,4},{6,7},{7,6},{8,9},{9,8},{10,11... | collective-permute-start | bytes 393224 | tf_op jit(solution)/shard_map/ppermute | solution.py:546
  44.4 3.9 %grads.3 = (bf16[512,1024]{1,0:T(8,128)(2,1)}, f32[16,512]{1,0:T(8,128)}) custom-call(s32[8]{0:T(128)S(1)} %stack.29.s.sel, bf16[512,1024]{1,0:T(8,128)(2,1)S(1)} %copy-done, bf16[2,512,512]{2,1,0:T(8,128)(2,1)S(1)} %copy-done.3, bf16[512,128]{1,0:T(8,128)(2,1)S(1)} %copy-done.7, ...), custom_call_target="tpu_custom_call", output_to_operand_aliasing={{0}: (13, {}), {1}: (14, {})} | custom-call | flops 1000 | bytes 1000 | tf_op jit(solution)/shard_map/grads/pallas_call | solution.py:479
  48.3 0.2 collective-permute-start.9
  48.5 0.7 %collective-permute-done.11.refs_1_ = f32[256,128]{1,0:T(8,128)S(1)} collective-permute-done((f32[256,128]{1,0:T(8,128)S(1)}, f32[256,128]{1,0:T(8,128)S(1)}, u32[]{:S(2)}, u32[]{:S(2)}) %collective-permute-start.11) | collective-permute-done | bytes 131104 | tf_op jit(solution)/shard_map/ppermute | solution.py:546
  49.2 1.3 %join.2 = (f32[512,128]{1,0:T(8,128)}, f32[512,128]{1,0:T(8,128)}) custom-call(s32[8]{0:T(128)S(1)} %stack.29.s.sel, f32[256,128]{1,0:T(8,128)S(1)} %add.30.refs_0_, f32[256,128]{1,0:T(8,128)S(1)} %collective-permute-done.11.refs_1_, f32[256,128]{1,0:T(8,128)S(1)} %add.29.refs_2_), custom_call_target="tpu_custom_call" | custom-call | flops 1000 | bytes 1000 | tf_op jit(solution)/shard_map/join/pallas_call | solution.py:527
  50.5 2.9 %collective-permute-done.9.refs_0_ = f32[256,128]{1,0:T(8,128)S(1)} collective-permute-done((f32[256,128]{1,0:T(8,128)S(1)}, f32[256,128]{1,0:T(8,128)S(1)}, u32[]{:S(2)}, u32[]{:S(2)}) %collective-permute-start.9) | collective-permute-done | bytes 131104 | tf_op jit(solution)/shard_map/ppermute | solution.py:546
  53.4 1.2 %join.3 = (f32[512,128]{1,0:T(8,128)}, f32[512,128]{1,0:T(8,128)}) custom-call(s32[8]{0:T(128)S(1)} %stack.29.s.sel, f32[256,128]{1,0:T(8,128)S(1)} %collective-permute-done.9.refs_0_, f32[512,128]{1,0:T(8,128)} %get-tuple-element.65.refs_1_, f32[512,128]{1,0:T(8,128)} %get-tuple-element.66.refs_2_), custom_call_target="tpu_custom_call", output_to_operand_aliasing={{0}: (2, {}), {1}: (3, {})} | custom-call | flops 1000 | bytes 1000 | tf_op jit(solution)/shard_map/join/pallas_call | solution.py:527
  (36 shorter events, 0.3 us)
Async XLA Ops:
  0.6 4.1 %copy-start = (bf16[512,1024]{1,0:T(8,128)(2,1)S(1)}, bf16[512,1024]{1,0:T(8,128)(2,1)}, u32[]{:S(2)}) copy-start(bf16[512,1024]{1,0:T(8,128)(2,1)} %x_ref.5) | copy-start | bytes 3145732
  0.6 4.1 %copy-start.4 = (bf16[512,1024]{1,0:T(8,128)(2,1)S(1)}, bf16[512,1024]{1,0:T(8,128)(2,1)}, u32[]{:S(2)}) copy-start(bf16[512,1024]{1,0:T(8,128)(2,1)} %g_ref.1) | copy-start | bytes 3145732
  0.7 4.1 %copy-start.7 = (bf16[512,128]{1,0:T(8,128)(2,1)S(1)}, bf16[512,128]{1,0:T(8,128)(2,1)}, u32[]{:S(2)}) copy-start(bf16[512,128]{1,0:T(8,128)(2,1)} %w_ref.5) | copy-start | bytes 393220
  0.7 4.1 %copy-start.8 = (bf16[512,128]{1,0:T(8,128)(2,1)S(1)}, bf16[512,128]{1,0:T(8,128)(2,1)}, u32[]{:S(2)}) copy-start(bf16[512,128]{1,0:T(8,128)(2,1)} %r_ref.5) | copy-start | bytes 393220
  0.7 4.1 %copy-start.9 = (f32[16,512]{1,0:T(8,128)S(1)}, f32[16,512]{1,0:T(8,128)}, u32[]{:S(2)}) copy-start(f32[16,512]{1,0:T(8,128)} %ld_ref.5) | copy-start | bytes 98308
  4.2 2.8 %collective-permute-start = (f32[264,512]{1,0:T(8,128)}, f32[264,512]{1,0:T(8,128)S(1)}, u32[]{:S(2)}, u32[]{:S(2)}) collective-permute-start(f32[264,512]{1,0:T(8,128)} %get-tuple-element.39.pay_ref), channel_id=1, source_target_pairs={{0,4},{4,0},{8,12},{12,8},{16,20},{20,16},{24,28},{28,24},{1,5},{5... | collective-permute-start | bytes 1622024 | tf_op jit(solution)/shard_map/ppermute | solution.py:546
  7.7 9.9 %collective-permute-start.1 = (f32[136,512]{1,0:T(8,128)S(1)}, f32[136,512]{1,0:T(8,128)S(1)}, u32[]{:S(2)}, u32[]{:S(2)}) collective-permute-start(f32[136,512]{1,0:T(8,128)S(1)} %get-tuple-element.40.rest_0_.refs_1_), channel_id=1, source_target_pairs={{0,8},{4,12},{8,0},{12,4},{16,24},{20,28},{24,16},{28,20},{1,9},{5... | collective-permute-start | bytes 835592 | tf_op jit(solution)/shard_map/ppermute | solution.py:546
  17.6 4.1 %copy-start.2 = (bf16[2,512,512]{2,1,0:T(8,128)(2,1)S(1)}, bf16[2,512,512]{2,1,0:T(8,128)(2,1)}, u32[]{:S(2)}) copy-start(bf16[2,512,512]{2,1,0:T(8,128)(2,1)} %get-tuple-element.48.refs_0_.wg_ref.gw_ref) | copy-start | bytes 3145732
  17.6 4.1 %copy-start.3 = (bf16[2,512,512]{2,1,0:T(8,128)(2,1)S(1)}, bf16[2,512,512]{2,1,0:T(8,128)(2,1)}, u32[]{:S(2)}) copy-start(bf16[2,512,512]{2,1,0:T(8,128)(2,1)} %get-tuple-element.37.refs_4_.wg_ref.gw_ref) | copy-start | bytes 3145732
  17.6 4.1 %copy-start.5 = (f32[256,512]{1,0:T(8,128)S(1)}, f32[256,512]{1,0:T(8,128)}, u32[]{:S(2)}) copy-start(f32[256,512]{1,0:T(8,128)} %get-tuple-element.50.refs_2_.part_ref) | copy-start | bytes 1572868
  17.6 4.1 %copy-start.6 = (f32[256,512]{1,0:T(8,128)S(1)}, f32[256,512]{1,0:T(8,128)}, u32[]{:S(2)}) copy-start(f32[256,512]{1,0:T(8,128)} %get-tuple-element.43.refs_6_.part_ref) | copy-start | bytes 1572868
  17.6 4.1 %copy-start.10 = (f32[16,512]{1,0:T(8,128)S(1)}, f32[16,512]{1,0:T(8,128)}, u32[]{:S(2)}) copy-start(f32[16,512]{1,0:T(8,128)} %get-tuple-element.44.refs_7_.tot_ref) | copy-start | bytes 98308
  17.6 4.1 %copy-start.11 = (f32[16,512]{1,0:T(8,128)S(1)}, f32[16,512]{1,0:T(8,128)}, u32[]{:S(2)}) copy-start(f32[16,512]{1,0:T(8,128)} %get-tuple-element.51.refs_3_.tot_ref) | copy-start | bytes 98308
  18.3 3.4 %collective-permute-start.2 = (f32[128,512]{1,0:T(8,128)S(1)}, f32[128,512]{1,0:T(8,128)S(1)}, u32[]{:S(2)}, u32[]{:S(2)}) collective-permute-start(f32[128,512]{1,0:T(8,128)S(1)} %get-tuple-element.45), channel_id=1, source_target_pairs={{0,4},{4,0},{8,12},{12,8},{16,20},{20,16},{24,28},{28,24},{1,5},{5... | collective-permute-start | bytes 786440 | tf_op jit(solution)/shard_map/ppermute | solution.py:546
  18.4 9.8 %collective-permute-start.3 = (f32[128,512]{1,0:T(8,128)S(1)}, f32[128,512]{1,0:T(8,128)S(1)}, u32[]{:S(2)}, u32[]{:S(2)}) collective-permute-start(f32[128,512]{1,0:T(8,128)S(1)} %get-tuple-element.46), channel_id=1, source_target_pairs={{0,8},{4,12},{8,0},{12,4},{16,24},{20,28},{24,16},{28,20},{1,9},{5... | collective-permute-start | bytes 786440 | tf_op jit(solution)/shard_map/ppermute | solution.py:546
  20.2 8.4 %collective-permute-start.4 = (f32[128,512]{1,0:T(8,128)S(1)}, f32[128,512]{1,0:T(8,128)S(1)}, u32[]{:S(2)}, u32[]{:S(2)}) collective-permute-start(f32[128,512]{1,0:T(8,128)S(1)} %get-tuple-element.47), channel_id=1, source_target_pairs={{0,16},{4,20},{8,24},{12,28},{16,0},{20,4},{24,8},{28,12},{1,17},{... | collective-permute-start | bytes 786440 | tf_op jit(solution)/shard_map/ppermute | solution.py:546
  22.8 5.4 %collective-permute-start.5 = (f32[256,128]{1,0:T(8,128)S(1)}, f32[256,128]{1,0:T(8,128)S(1)}, u32[]{:S(2)}, u32[]{:S(2)}) collective-permute-start(f32[256,128]{1,0:T(8,128)S(1)} %get-tuple-element.54), channel_id=1, source_target_pairs={{0,1},{1,0},{2,3},{3,2},{4,5},{5,4},{6,7},{7,6},{8,9},{9,8},{10,11... | collective-permute-start | bytes 393224 | tf_op jit(solution)/shard_map/ppermute | solution.py:546
  29.2 1.6 %collective-permute-start.6 = (f32[128,512]{1,0:T(8,128)S(1)}, f32[128,512]{1,0:T(8,128)S(1)}, u32[]{:S(2)}, u32[]{:S(2)}) collective-permute-start(f32[128,512]{1,0:T(8,128)S(1)} %get-tuple-element.55), channel_id=1, source_target_pairs={{0,4},{4,0},{8,12},{12,8},{16,20},{20,16},{24,28},{28,24},{1,5},{5... | collective-permute-start | bytes 786440 | tf_op jit(solution)/shard_map/ppermute | solution.py:546
  29.3 6.7 %copy-start.1 = (f32[512,1024]{1,0:T(8,128)S(1)}, f32[512,1024]{1,0:T(8,128)}, u32[]{:S(2)}) copy-start(f32[512,1024]{1,0:T(8,128)} %get-tuple-element.41.refs_6_.gint_ref) | copy-start | bytes 6291460
  29.3 6.7 %copy-start.12 = (f32[16,512]{1,0:T(8,128)S(1)}, f32[16,512]{1,0:T(8,128)}, u32[]{:S(2)}) copy-start(f32[16,512]{1,0:T(8,128)} %get-tuple-element.42.dot_ref) | copy-start | bytes 98308
  31.7 7.9 %collective-permute-start.7 = (f32[256,128]{1,0:T(8,128)S(1)}, f32[256,128]{1,0:T(8,128)S(1)}, u32[]{:S(2)}, u32[]{:S(2)}) collective-permute-start(f32[256,128]{1,0:T(8,128)S(1)} %get-tuple-element.57.rest_0_), channel_id=1, source_target_pairs={{0,1},{1,0},{2,3},{3,2},{4,5},{5,4},{6,7},{7,6},{8,9},{9,8},{10,11... | collective-permute-start | bytes 393224 | tf_op jit(solution)/shard_map/ppermute | solution.py:546
  33.3 9.1 %collective-permute-start.10 = (f32[256,128]{1,0:T(8,128)S(1)}, f32[256,128]{1,0:T(8,128)S(1)}, u32[]{:S(2)}, u32[]{:S(2)}) collective-permute-start(f32[256,128]{1,0:T(8,128)S(1)} %add.27.refs_7_), channel_id=1, source_target_pairs={{0,2},{1,3},{2,0},{3,1},{4,6},{5,7},{6,4},{7,5},{8,10},{9,11},{10,... | collective-permute-start | bytes 393224 | tf_op jit(solution)/shard_map/ppermute | solution.py:546
  39.6 8.7 %collective-permute-start.8 = (f32[256,128]{1,0:T(8,128)S(1)}, f32[256,128]{1,0:T(8,128)S(1)}, u32[]{:S(2)}, u32[]{:S(2)}) collective-permute-start(f32[256,128]{1,0:T(8,128)S(1)} %add.28.rest_2_), channel_id=1, source_target_pairs={{0,2},{1,3},{2,0},{3,1},{4,6},{5,7},{6,4},{7,5},{8,10},{9,11},{10,... | collective-permute-start | bytes 393224 | tf_op jit(solution)/shard_map/ppermute | solution.py:546
  42.4 6.8 %collective-permute-start.11 = (f32[256,128]{1,0:T(8,128)S(1)}, f32[256,128]{1,0:T(8,128)S(1)}, u32[]{:S(2)}, u32[]{:S(2)}) collective-permute-start(f32[256,128]{1,0:T(8,128)S(1)} %add.30.refs_0_), channel_id=1, source_target_pairs={{0,1},{1,0},{2,3},{3,2},{4,5},{5,4},{6,7},{7,6},{8,9},{9,8},{10,11... | collective-permute-start | bytes 393224 | tf_op jit(solution)/shard_map/ppermute | solution.py:546
  48.3 5.0 %collective-permute-start.9 = (f32[256,128]{1,0:T(8,128)S(1)}, f32[256,128]{1,0:T(8,128)S(1)}, u32[]{:S(2)}, u32[]{:S(2)}) collective-permute-start(f32[256,128]{1,0:T(8,128)S(1)} %add.29.refs_2_), channel_id=1, source_target_pairs={{0,1},{1,0},{2,3},{3,2},{4,5},{5,4},{6,7},{7,6},{8,9},{9,8},{10,11... | collective-permute-start | bytes 393224 | tf_op jit(solution)/shard_map/ppermute | solution.py:546
